TPU v7x, 512 devices: a whole 4x8x8 slice. The times are simulated.
512 devices in a mesh: depth: 4 (over x), row: 16 (over y, core), col: 8 (over z).
Axes of the slice: x: 4, y: 8, z: 8, core: 2. Of those that a mesh axis runs over, the one named last changes fastest.
Arguments:
- latents: bfloat16 [4, 16, 8, 3, 8, 8, 8, 256], P('depth', 'row', 'col'), may hold values from -6 to 6
- neighbours: int32 [4, 16, 8, 3, 6], P('depth', 'row', 'col'), may hold values from -1 to 1535, as said below
- owners: int32 [4, 16, 8, 3, 8], P('depth', 'row', 'col'), may hold values from -1 to 255, as said below
- conv_weight: bfloat16 [27, 256, 256], P(None, None, 'row'), may hold values from -0.078125 to 0.078125
- step_embed: float32 [256], replicated, may hold values from -6 to 6
- up_weight: bfloat16 [8, 256, 128], replicated, may hold values from -0.375 to 0.375
Outputs:
- upsampled: bfloat16 [4, 16, 8, 16, 8, 8, 8, 128], P('depth', 'row', 'col')
Inputs may be any that keep to these rules, and one draw needn't show every extreme that they name: `neighbours`: entry d names the brick beside a brick's face in direction d (order -z, +z, -y, +y, -x, +x) as ((depth * 16 + row) * 8 + col) * 3 + slot; that brick lies on the same device or on the device beside it across that face. -1 where no brick is there and in every entry of an empty slot. The occupied slots of a device come first. `owners`: for an occupied slot, entry k is j * 16 + u: child k goes to slot u of the device at row j with the same depth and col; -1 in empty slots. Each device holds 1 to 3 occupied slots, and in every line of devices along row some device holds 3. Every device receives exactly 16 children, each slot once, and no device sends more than 2 children to one device.
All inputs are finite; a program needn't handle non-finite values.
Results may differ from a plain program's by a relative error of at most 0.0051.
Values may be sent and summed in bfloat16 or wider, within the bound.
No kernel may reach another device: no remote copies, remote signals or barrier semaphores. Data moves between devices by JAX's collectives and lax.ppermute only.
A program may use at most 64 MiB of HBM per device.

v0:
```python
import jax
import jax.numpy as jnp
from jax import lax
from jax.sharding import PartitionSpec as P

OCAP = 16


def with_halo(cells, sides, width):
    for axis, dim in sides:
        count = lax.axis_size(axis)
        ends = count - 1
        head = lax.slice_in_dim(cells, 0, width, axis=dim)
        tail = lax.slice_in_dim(cells, cells.shape[dim] - width, cells.shape[dim], axis=dim)
        cells = jnp.concatenate(
            [
                lax.ppermute(tail, axis, [(i, (i + 1) % count) for i in range(ends)]),
                cells,
                lax.ppermute(head, axis, [((i + 1) % count, i) for i in range(ends)]),
            ],
            axis=dim,
        )
    return cells


def normed_silu(values):
    mean_square = jnp.mean(values * values, axis=-1, keepdims=True)
    return jax.nn.silu(values * lax.rsqrt(mean_square + 1e-06))


def borrowed(local_face, remote_face, near_index, own_index, offset, slots_dev):
    owner_dev = near_index // slots_dev
    in_slot = near_index % slots_dev
    chosen = jnp.where(
        near_index < 0,
        -1,
        jnp.where(
            owner_dev == own_index,
            in_slot,
            jnp.where(owner_dev == own_index + offset, slots_dev + in_slot, -1),
        ),
    )
    picker = (chosen[:, None] == jnp.arange(2 * slots_dev, dtype=jnp.int32)[None, :]).astype(
        jnp.bfloat16
    )
    stacked = jnp.concatenate([local_face, remote_face], axis=0).reshape(2 * slots_dev, -1)
    picked = jnp.dot(picker, stacked, preferred_element_type=jnp.float32)
    return picked.astype(jnp.bfloat16).reshape(local_face.shape)


def padded_field(source, near_ids, own_index, row_count, col_count):
    slots_dev = source.shape[0]
    edge_len = source.shape[1]
    depth_faces = with_halo(jnp.stack([source[:, 0], source[:, -1]]), (("depth", 0),), 1)
    row_faces = with_halo(jnp.stack([source[:, :, 0], source[:, :, -1]]), (("row", 0),), 1)
    col_faces = with_halo(jnp.stack([source[:, :, :, 0], source[:, :, :, -1]]), (("col", 0),), 1)
    plane_size = row_count * col_count
    below_z = borrowed(
        depth_faces[2], depth_faces[0], near_ids[:, 0], own_index, -plane_size, slots_dev
    )
    above_z = borrowed(
        depth_faces[1], depth_faces[3], near_ids[:, 1], own_index, plane_size, slots_dev
    )
    below_y = borrowed(row_faces[2], row_faces[0], near_ids[:, 2], own_index, -col_count, slots_dev)
    above_y = borrowed(row_faces[1], row_faces[3], near_ids[:, 3], own_index, col_count, slots_dev)
    below_x = borrowed(col_faces[2], col_faces[0], near_ids[:, 4], own_index, -1, slots_dev)
    above_x = borrowed(col_faces[1], col_faces[3], near_ids[:, 5], own_index, 1, slots_dev)
    padded = jnp.zeros(
        (slots_dev, edge_len + 2, edge_len + 2, edge_len + 2, source.shape[-1]), jnp.bfloat16
    )
    padded = padded.at[:, 1:-1, 1:-1, 1:-1].set(source)
    padded = padded.at[:, 0, 1:-1, 1:-1].set(below_z)
    padded = padded.at[:, edge_len + 1, 1:-1, 1:-1].set(above_z)
    padded = padded.at[:, 1:-1, 0, 1:-1].set(below_y)
    padded = padded.at[:, 1:-1, edge_len + 1, 1:-1].set(above_y)
    padded = padded.at[:, 1:-1, 1:-1, 0].set(below_x)
    padded = padded.at[:, 1:-1, 1:-1, edge_len + 1].set(above_x)
    return padded


def convolve(source, weight, near_ids, own_index, row_count, col_count):
    channels = source.shape[-1]
    padded = padded_field(source, near_ids, own_index, row_count, col_count)
    weight_piece = lax.all_gather(weight, "row", axis=2, tiled=True)
    kernel = weight_piece.reshape(3, 3, 3, channels, weight_piece.shape[2])
    return lax.conv_general_dilated(
        padded,
        kernel,
        (1, 1, 1),
        "VALID",
        dimension_numbers=("NDHWC", "DHWIO", "NDHWC"),
        preferred_element_type=jnp.float32,
    )


def body(latents, neighbours, owners, conv_weight, step_embed, up_weight):
    row_count = lax.axis_size("row")
    col_count = lax.axis_size("col")
    own_row = lax.axis_index("row")
    own_index = (lax.axis_index("depth") * row_count + own_row) * col_count + lax.axis_index("col")
    latent = latents.reshape(latents.shape[3:]).astype(jnp.float32)
    slots_dev, edge_len, channels = (latent.shape[0], latent.shape[1], latent.shape[-1])
    half_len = edge_len // 2
    out_channels = up_weight.shape[-1]
    near_ids = neighbours.reshape(slots_dev, 6)
    owner_ids = owners.reshape(slots_dev * 8)
    first_input = normed_silu(latent).astype(jnp.bfloat16)
    conv_sum = (
        convolve(first_input, conv_weight, near_ids, own_index, row_count, col_count) + step_embed
    )
    refined = (latent + conv_sum).astype(jnp.bfloat16)
    expand = up_weight.transpose(1, 0, 2).reshape(channels, 8 * out_channels)
    projected = jnp.dot(
        refined.reshape(slots_dev * edge_len**3, channels),
        expand,
        preferred_element_type=jnp.float32,
    )
    projected = projected.reshape(
        slots_dev, 2, half_len, 2, half_len, 2, half_len, 2, 2, 2, out_channels
    )
    projected = projected.transpose(0, 1, 3, 5, 2, 7, 4, 8, 6, 9, 10)
    payload = projected.reshape(slots_dev * 8, edge_len**3, out_channels).astype(jnp.bfloat16)
    item_shape = payload.shape[1:]
    send_cap = (8 * slots_dev + row_count - 1) // row_count
    is_valid = owner_ids >= 0
    target_row = jnp.where(is_valid, owner_ids // OCAP, 0)
    target_slot = jnp.where(is_valid, owner_ids % OCAP, -1)
    serial = jnp.arange(slots_dev * 8, dtype=jnp.int32)
    earlier = (
        (target_row[None, :] == target_row[:, None])
        & (serial[None, :] < serial[:, None])
        & is_valid[None, :]
    )
    ranked = jnp.sum(earlier.astype(jnp.int32), axis=1)
    position = jnp.where(is_valid, target_row * send_cap + ranked, row_count * send_cap)
    outgoing = (
        jnp.zeros((row_count * send_cap,) + item_shape, jnp.bfloat16)
        .at[position]
        .set(payload, mode="drop")
    )
    labels = (
        jnp.full((row_count * send_cap,), -1, jnp.int32).at[position].set(target_slot, mode="drop")
    )
    arrived, arrived_labels = (
        lax.all_to_all(
            outgoing.reshape((row_count, send_cap) + item_shape),
            "row",
            split_axis=0,
            concat_axis=0,
            tiled=True,
        ),
        lax.all_to_all(
            labels.reshape(row_count, send_cap), "row", split_axis=0, concat_axis=0, tiled=True
        ),
    )
    arrived = arrived.reshape((row_count * send_cap,) + item_shape)
    arrived_labels = arrived_labels.reshape(row_count * send_cap)
    placed = jnp.where(arrived_labels >= 0, arrived_labels, OCAP)
    upsampled = (
        jnp.zeros((OCAP, edge_len**3, out_channels), jnp.bfloat16)
        .at[placed]
        .set(arrived, mode="drop")
    )
    return upsampled.reshape(1, 1, 1, OCAP, edge_len, edge_len, edge_len, out_channels)


def solution(mesh):
    return jax.shard_map(
        body,
        mesh=mesh,
        in_specs=(
            P("depth", "row", "col", None, None, None, None, None),
            P("depth", "row", "col", None, None),
            P("depth", "row", "col", None, None),
            P(None, None, "row"),
            P(),
            P(),
        ),
        out_specs=P("depth", "row", "col", None, None, None, None, None),
        check_vma=False,
    )
```

profile of v0, /device:TPU:1, one launch (start us, length us, event | category | flops | bytes accessed | tf_op | source)
XLA Modules:
  0.0 205.4 jit_solution(4541175386371983872)
XLA Ops:
  6.5 0.7 all-gather.2.cloned.1.call-update
  7.3 1.9 fusion.5
  9.3 1.6 fusion.4
  10.9 0.9 fusion.56
  11.8 4.6 %collective-permute-start = (bf16[1,3,8,8,256]{4,1,3,2,0:T(4,128)(2,1)}, bf16[1,3,8,8,256]{4,1,3,2,0:T(4,128)(2,1)}, u32[]{:S(2)}, u32[]{:S(2)}) collective-permute-start(bf16[1,3,8,8,256]{4,1,3,2,0:T(4,128)(2,1)} %get-tuple-element.104), channel_id=1, source_target_pairs={{0,128},{128,256},{256,384},{1,129},{129,257},{257,385},{2,130},{1... | collective-permute-start | bytes 294920 | tf_op jit(solution)/shard_map/ppermute | solution.py:17
  16.4 1.3 collective-permute-start.1
  17.9 4.2 %collective-permute-start.2 = (bf16[1,3,8,8,256]{4,1,3,2,0:T(4,128)(2,1)S(1)}, bf16[1,3,8,8,256]{4,1,3,2,0:T(4,128)(2,1)}, u32[]{:S(2)}, u32[]{:S(2)}) collective-permute-start(bf16[1,3,8,8,256]{4,1,3,2,0:T(4,128)(2,1)S(1)} %get-tuple-element.100), channel_id=1, source_target_pairs={{0,8},{8,16},{16,24},{24,32},{32,40},{40,48},{48,56},{56,64},{64,7... | collective-permute-start | bytes 294920 | tf_op jit(solution)/shard_map/ppermute | solution.py:17
  22.1 4.0 %collective-permute-start.3 = (bf16[1,3,8,8,256]{4,1,3,2,0:T(4,128)(2,1)S(1)}, bf16[1,3,8,8,256]{4,1,3,2,0:T(4,128)(2,1)}, u32[]{:S(2)}, u32[]{:S(2)}) collective-permute-start(bf16[1,3,8,8,256]{4,1,3,2,0:T(4,128)(2,1)S(1)} %get-tuple-element.101), channel_id=1, source_target_pairs={{8,0},{16,8},{24,16},{32,24},{40,32},{48,40},{56,48},{64,56},{72,6... | collective-permute-start | bytes 294920 | tf_op jit(solution)/shard_map/ppermute | solution.py:19
  26.4 2.5 %collective-permute-start.4 = (bf16[1,3,8,8,256]{4,1,3,2,0:T(4,128)(2,1)S(1)}, bf16[1,3,8,8,256]{4,1,3,2,0:T(4,128)(2,1)}, u32[]{:S(2)}, u32[]{:S(2)}) collective-permute-start(bf16[1,3,8,8,256]{4,1,3,2,0:T(4,128)(2,1)S(1)} %get-tuple-element.96), channel_id=1, source_target_pairs={{0,1},{1,2},{2,3},{3,4},{4,5},{5,6},{6,7},{8,9},{9,10},{10,11},{11... | collective-permute-start | bytes 294920 | tf_op jit(solution)/shard_map/ppermute | solution.py:17
  29.8 0.8 scatter_custom_fusion
  31.3 9.2 %all-to-all-start = ((s32[16,1,2]{2,1,0:T(1,128)}), s32[16,1,2]{2,1,0:T(1,128)S(1)}, u32[]{:S(2)}, u32[]{:S(2)}) async-start(s32[16,1,2]{2,1,0:T(1,128)} %bitcast.88), calls=%async_computation | async-start | bytes 16384 | tf_op jit(solution)/shard_map/all_to_all | solution.py:152
  40.5 2.0 scatter.45
  43.0 1.5 collective-permute-start.5
  44.5 1.2 convolution_convert_fusion.5
  45.7 0.7 constant_dynamic-update-slice_fusion.5
  46.4 1.2 convolution_convert_fusion.4
  48.3 1.2 convolution_convert_fusion.3
  49.5 0.7 constant_dynamic-update-slice_fusion.3
  50.2 1.2 convolution_convert_fusion.2
  51.4 0.7 constant_dynamic-update-slice_fusion.2
  52.1 1.2 convolution_convert_fusion.1
  54.3 0.7 constant_dynamic-update-slice_fusion
  55.0 4.4 %all-gather.2.cloned.1.call-done = bf16[27,256,256]{1,2,0:T(8,128)(2,1)} async-done(((bf16[27,256,16]{1,2,0:T(8,128)(2,1)}), bf16[27,256,256]{1,2,0:T(8,128)(2,1)}) %all-gather.2.cloned.1.call-update) | async-done | bytes 3538960 | tf_op jit(solution)/shard_map/all_gather | solution.py:84
  59.5 17.9 %fusion.6 = bf16[3,8,8,8,256]{4,0,3,2,1:T(4,128)(2,1)S(1)} fusion(bf16[3,10,10,10,256]{4,0,3,2,1:T(4,128)(2,1)} %constant_dynamic-update-slice_fusion, bf16[3,3,3,256,256]{3,4,2,1,0:T(8,128)(2,1)} %bitcast.89, f32[256]{0:T(256)S(1)} %copy-done.7, bf16[1,1,1,3,8,8,8,256]{7,6,5,4,3,2,1,0:T(8,128)(2,1)S(1)} %copy-done.1), kind=kOutput, calls=%fused_computation.19 | convolution fusion | flops 5437390848 | bytes 6648832 | tf_op jit(solution)/shard_map/conv_general_dilated | solution.py:86
  77.4 1.2 convert_bitcast_fusion
  78.6 3.4 %copy.50 = bf16[3,2,2,2,4,2,4,2,4,2,128]{10,9,8,7,6,5,4,3,2,1,0:T(2,128)(2,1)S(1)} copy(bf16[3,2,2,2,4,2,4,2,4,2,128]{10,8,9,7,5,3,6,2,4,1,0:T(4,128)(2,1)S(1)} %convert_bitcast_fusion) | data formatting | bytes 6291456 | tf_op jit(solution)/shard_map/convert_element_type | solution.py:122
  82.0 2.9 %broadcast_in_dim.62 = bf16[32,512,128]{2,1,0:T(8,128)(2,1)} broadcast(bf16[]{:T(256)} %constant.330.clone.1), dimensions={} | broadcast | bytes 4194306 | tf_op jit(solution)/shard_map/broadcast_in_dim | solution.py:137
  84.9 6.9 %scatter_fusion = bf16[32,512,128]{2,1,0:T(8,128)(2,1)} fusion(bf16[32,512,128]{2,1,0:T(8,128)(2,1)} %broadcast_in_dim.62, s32[24]{0:T(128)S(1)} %copy-done.6, bf16[24,512,128]{2,1,0:T(8,128)(2,1)S(1)} %bitcast.73), kind=kCustom, calls=%fused_computation.1 | custom fusion | bytes 9437280 | tf_op jit(solution)/shard_map/scatter | solution.py:139
  91.8 5.2 %all-to-all-start.1 = ((bf16[16,2,512,128]{3,2,1,0:T(8,128)(2,1)}), bf16[16,2,512,128]{3,2,1,0:T(8,128)(2,1)}, u32[]{:S(2)}, u32[]{:S(2)}) async-start(bf16[16,2,512,128]{3,2,1,0:T(8,128)(2,1)} %bitcast.72), calls=%async_computation.1 | async-start | bytes 8388608 | tf_op jit(solution)/shard_map/all_to_all | solution.py:145
  98.2 92.3 %all-to-all-done.1 = bf16[16,2,512,128]{3,2,1,0:T(8,128)(2,1)} async-done(((bf16[16,2,512,128]{3,2,1,0:T(8,128)(2,1)}), bf16[16,2,512,128]{3,2,1,0:T(8,128)(2,1)}, u32[]{:S(2)}, u32[]{:S(2)}) %all-to-all-start.1) | async-done | bytes 4194336 | tf_op jit(solution)/shard_map/all_to_all | solution.py:145
  190.9 6.3 %scatter_fusion.1 = bf16[16,512,128]{2,1,0:T(8,128)(2,1)S(1)} fusion(bf16[16,512,128]{2,1,0:T(8,128)(2,1)S(1)} %broadcast_in_dim.31, s32[32]{0:T(128)S(1)} %fusion.44, bf16[32,512,128]{2,1,0:T(8,128)(2,1)} %bitcast.42), kind=kCustom, calls=%fused_computation.2 | custom fusion | bytes 12583040 | tf_op jit(solution)/shard_map/scatter | solution.py:162
  197.2 1.3 copy-done
  (45 shorter events, 6.0 us)
Async XLA Ops:
  6.5 2.7 %copy-start.1 = (bf16[1,1,1,3,8,8,8,256]{7,6,5,4,3,2,1,0:T(8,128)(2,1)S(1)}, bf16[1,1,1,3,8,8,8,256]{7,6,5,4,3,2,1,0:T(8,128)(2,1)}, u32[]{:S(2)}) copy-start(bf16[1,1,1,3,8,8,8,256]{7,6,5,4,3,2,1,0:T(8,128)(2,1)} %param.20) | copy-start | bytes 2359300
  6.5 52.9 %all-gather.2.cloned.1.call-start = ((), (), s32[]{:S(2)}) async-start(), calls=%async_computation.2 | async-start | bytes 3760128 | tf_op jit(solution)/shard_map/all_gather | solution.py:84
  9.2 19.7 %copy-start.4 = (s32[1,1,1,3,8]{4,2,3,1,0:T(1,128)S(1)}, s32[1,1,1,3,8]{4,2,3,1,0:T(1,128)}, u32[]{:S(2)}) copy-start(s32[1,1,1,3,8]{4,2,3,1,0:T(1,128)} %param.22) | copy-start | bytes 292
  9.2 31.2 %copy-start.3 = (s32[1,1,1,3,6]{4,2,3,1,0:T(1,128)S(1)}, s32[1,1,1,3,6]{4,2,3,1,0:T(1,128)}, u32[]{:S(2)}) copy-start(s32[1,1,1,3,6]{4,2,3,1,0:T(1,128)} %param.21) | copy-start | bytes 220
  11.8 31.2 %collective-permute-start = (bf16[1,3,8,8,256]{4,1,3,2,0:T(4,128)(2,1)}, bf16[1,3,8,8,256]{4,1,3,2,0:T(4,128)(2,1)}, u32[]{:S(2)}, u32[]{:S(2)}) collective-permute-start(bf16[1,3,8,8,256]{4,1,3,2,0:T(4,128)(2,1)} %get-tuple-element.104), channel_id=1, source_target_pairs={{0,128},{128,256},{256,384},{1,129},{129,257},{257,385},{2,130},{1... | collective-permute-start | bytes 294920 | tf_op jit(solution)/shard_map/ppermute | solution.py:17
  16.4 30.1 %collective-permute-start.1 = (bf16[1,3,8,8,256]{4,1,3,2,0:T(4,128)(2,1)}, bf16[1,3,8,8,256]{4,1,3,2,0:T(4,128)(2,1)}, u32[]{:S(2)}, u32[]{:S(2)}) collective-permute-start(bf16[1,3,8,8,256]{4,1,3,2,0:T(4,128)(2,1)} %get-tuple-element.105), channel_id=1, source_target_pairs={{128,0},{256,128},{384,256},{129,1},{257,129},{385,257},{130,2},{2... | collective-permute-start | bytes 294920 | tf_op jit(solution)/shard_map/ppermute | solution.py:19
  17.9 24.6 %copy-start.2 = (bf16[8,256,128]{2,1,0:T(8,128)(2,1)S(1)}, bf16[8,256,128]{2,1,0:T(8,128)(2,1)}, u32[]{:S(2)}) copy-start(bf16[8,256,128]{2,1,0:T(8,128)(2,1)} %param.25) | copy-start | bytes 1572868
  17.9 30.4 %collective-permute-start.2 = (bf16[1,3,8,8,256]{4,1,3,2,0:T(4,128)(2,1)S(1)}, bf16[1,3,8,8,256]{4,1,3,2,0:T(4,128)(2,1)}, u32[]{:S(2)}, u32[]{:S(2)}) collective-permute-start(bf16[1,3,8,8,256]{4,1,3,2,0:T(4,128)(2,1)S(1)} %get-tuple-element.100), channel_id=1, source_target_pairs={{0,8},{8,16},{16,24},{24,32},{32,40},{40,48},{48,56},{56,64},{64,7... | collective-permute-start | bytes 294920 | tf_op jit(solution)/shard_map/ppermute | solution.py:17
  22.1 28.2 %collective-permute-start.3 = (bf16[1,3,8,8,256]{4,1,3,2,0:T(4,128)(2,1)S(1)}, bf16[1,3,8,8,256]{4,1,3,2,0:T(4,128)(2,1)}, u32[]{:S(2)}, u32[]{:S(2)}) collective-permute-start(bf16[1,3,8,8,256]{4,1,3,2,0:T(4,128)(2,1)S(1)} %get-tuple-element.101), channel_id=1, source_target_pairs={{8,0},{16,8},{24,16},{32,24},{40,32},{48,40},{56,48},{64,56},{72,6... | collective-permute-start | bytes 294920 | tf_op jit(solution)/shard_map/ppermute | solution.py:19
  26.4 25.8 %collective-permute-start.4 = (bf16[1,3,8,8,256]{4,1,3,2,0:T(4,128)(2,1)S(1)}, bf16[1,3,8,8,256]{4,1,3,2,0:T(4,128)(2,1)}, u32[]{:S(2)}, u32[]{:S(2)}) collective-permute-start(bf16[1,3,8,8,256]{4,1,3,2,0:T(4,128)(2,1)S(1)} %get-tuple-element.96), channel_id=1, source_target_pairs={{0,1},{1,2},{2,3},{3,4},{4,5},{5,6},{6,7},{8,9},{9,10},{10,11},{11... | collective-permute-start | bytes 294920 | tf_op jit(solution)/shard_map/ppermute | solution.py:17
  29.8 10.6 %copy-start.5 = (s32[24]{0:T(128)}, s32[24]{0:T(128)S(1)}, u32[]{:S(2)}) copy-start(s32[24]{0:T(128)S(1)} %fusion.43) | copy-start | bytes 292
  31.3 60.5 %all-to-all-start = ((s32[16,1,2]{2,1,0:T(1,128)}), s32[16,1,2]{2,1,0:T(1,128)S(1)}, u32[]{:S(2)}, u32[]{:S(2)}) async-start(s32[16,1,2]{2,1,0:T(1,128)} %bitcast.88), calls=%async_computation | async-start | bytes 16384 | tf_op jit(solution)/shard_map/all_to_all | solution.py:152
  43.0 11.1 %collective-permute-start.5 = (bf16[1,3,8,8,256]{4,1,3,2,0:T(4,128)(2,1)S(1)}, bf16[1,3,8,8,256]{4,1,3,2,0:T(4,128)(2,1)S(1)}, u32[]{:S(2)}, u32[]{:S(2)}) collective-permute-start(bf16[1,3,8,8,256]{4,1,3,2,0:T(4,128)(2,1)S(1)} %get-tuple-element.97), channel_id=1, source_target_pairs={{1,0},{2,1},{3,2},{4,3},{5,4},{6,5},{7,6},{9,8},{10,9},{11,10},{12... | collective-permute-start | bytes 294920 | tf_op jit(solution)/shard_map/ppermute | solution.py:19
  44.5 15.0 %copy-start.7 = (f32[256]{0:T(256)S(1)}, f32[256]{0:T(256)}, u32[]{:S(2)}) copy-start(f32[256]{0:T(256)} %param.24) | copy-start | bytes 3076
  82.0 2.9 %copy-start.6 = (s32[24]{0:T(128)S(1)}, s32[24]{0:T(128)}, u32[]{:S(2)}) copy-start(s32[24]{0:T(128)} %copy-done.5) | copy-start | bytes 292
  91.8 98.7 %all-to-all-start.1 = ((bf16[16,2,512,128]{3,2,1,0:T(8,128)(2,1)}), bf16[16,2,512,128]{3,2,1,0:T(8,128)(2,1)}, u32[]{:S(2)}, u32[]{:S(2)}) async-start(bf16[16,2,512,128]{3,2,1,0:T(8,128)(2,1)} %bitcast.72), calls=%async_computation.1 | async-start | bytes 8388608 | tf_op jit(solution)/shard_map/all_to_all | solution.py:145
  197.2 1.3 copy-start
Sparse Core Ops, SparseCore 0:
  9.5 49.9 all-gather.1
where the time goes:
time: 206 us; the launch traced here: 205 us
  waiting for transfers between devices  97.5 us (47%)
  starting transfers between devices  32.4 us (16%)
  local copies, waits for them, and re-layouts  31.2 us (15%)
  matrix products  25.3 us (12%)
  between operations  13.7 us (7%)
  other arithmetic  5.3 us (3%)
    all_to_all x1, waiting for transfers between devices, body(): lax.all_to_all(outgoing.reshape((row_count, send_cap) + item_shape), 'row...  92.3 us
    conv_general_dilated x1, matrix products, convolve(): lax.conv_general_dilated(padded, kernel, (1, 1, 1), 'VALID', dimension_nu...  17.9 us
    ppermute x3, starting transfers between devices, with_halo(): lax.ppermute(tail, axis, [(i, (i + 1) % count) for i in range(ends)])  11.3 us
    all_to_all x1, starting transfers between devices, body(): lax.all_to_all(labels.reshape(row_count, send_cap), 'row', split_axis=0,...  9.16 us
    scatter x1, local copies, waits for them, and re-layouts, body(): outgoing = jnp.zeros((row_count * send_cap,) + item_shape, jnp.bfloat16)....  6.85 us
    ppermute x3, starting transfers between devices, with_halo(): lax.ppermute(head, axis, [((i + 1) % count, i) for i in range(ends)])  6.77 us
    scatter x1, local copies, waits for them, and re-layouts, body(): upsampled = jnp.zeros((OCAP, edge_len ** 3, out_channels), jnp.bfloat16)....  6.28 us
    dot_general x6, matrix products, borrowed(): picked = jnp.dot(picker, stacked, preferred_element_type=jnp.float32)  6.27 us
  transfers between devices with their start and end apart: 9, of which 2 were waited for; matrix products, arithmetic and copies ran while one was open for 26% of the time, Pallas kernels for 0%

commit v1 on v0

v1 whole, which is shorter than its diff:
```python
import jax
import jax.numpy as jnp
from jax import lax
from jax.experimental import pallas as pl
from jax.experimental.pallas import tpu as pltpu
from jax.sharding import PartitionSpec as P

OCAP = 16
VMEM = pltpu.VMEM
SMEM = pltpu.SMEM
MB = 1024 * 1024


def whole(count):
    return [pl.BlockSpec(memory_space=VMEM)] * count


def norm_kernel(lat_ref, fi_ref, zlo_ref, zhi_ref, ylo_ref, yhi_ref, xlo_ref, xhi_ref, rows_ref):
    slots, edge, plane, _ = lat_ref.shape
    lanes = rows_ref.shape[-1]
    pieces = rows_ref.shape[0]
    for b in range(slots):
        for z in range(edge):
            v = lat_ref[b, z].astype(jnp.float32)
            mean_square = jnp.mean(v * v, axis=-1, keepdims=True)
            n = v * lax.rsqrt(mean_square + 1e-06)
            s = n / (1.0 + jnp.exp(-n))
            half = s.astype(jnp.bfloat16)
            fi_ref[b, z] = half
            if z == 0:
                zlo_ref[b] = half
            if z == edge - 1:
                zhi_ref[b] = half
            for p in range(pieces):
                rows_ref[p, pl.ds(z * plane, plane), :] = s[:, p * lanes : (p + 1) * lanes]
        for p in range(pieces):
            cols = pl.ds(p * lanes, lanes)
            xlo_ref[b, :, cols] = rows_ref[p, pl.ds(0, plane, stride=edge), :].astype(jnp.bfloat16)
            xhi_ref[b, :, cols] = rows_ref[p, pl.ds(edge - 1, plane, stride=edge), :].astype(
                jnp.bfloat16
            )
            low = [rows_ref[p, pl.ds(z * plane, edge), :] for z in range(edge)]
            ylo_ref[b, :, cols] = jnp.concatenate(low, axis=0).astype(jnp.bfloat16)
            high = [rows_ref[p, pl.ds(z * plane + plane - edge, edge), :] for z in range(edge)]
            yhi_ref[b, :, cols] = jnp.concatenate(high, axis=0).astype(jnp.bfloat16)


def columns_kernel(
    pick_ref, fi_ref, zlo, zhi, ylo, yhi, xlo, xhi, rz0, rz1, ry0, ry1, rx0, rx1, out_ref, table_ref, ybuf_ref, xbuf_ref
):
    slots, edge, plane, chan = fi_ref.shape
    near = (zhi, zlo, yhi, ylo, xhi, xlo)
    far = (rz0, rz1, ry0, ry1, rx0, rx1)
    for d in range(6):
        table_ref[d, 0:slots] = near[d][...]
        table_ref[d, slots : 2 * slots] = far[d][...]
        table_ref[d, 2 * slots] = jnp.zeros((plane, chan), jnp.bfloat16)
    at_x = lax.rem(lax.broadcasted_iota(jnp.int32, (plane + 2 * edge, chan), 0), edge)

    def put(b, z, rows, left, right):
        zero = jnp.zeros((edge, chan), jnp.float32)

        def spread(halo):
            mid = jnp.broadcast_to(halo[:, None, :], (edge, edge, chan)).reshape(plane, chan)
            return jnp.concatenate([zero, mid, zero], axis=0)

        count = plane + 2 * edge
        moved = (
            jnp.where(at_x == 0, spread(left), pltpu.roll(rows, 1, 0)),
            rows,
            jnp.where(at_x == edge - 1, spread(right), pltpu.roll(rows, count - 1, 0)),
        )
        for dx in range(3):
            for dy in range(3):
                tap = dy * 3 + dx
                out_ref[b, z, :, tap * chan : (tap + 1) * chan] = moved[dx][
                    dy * edge : dy * edge + plane
                ].astype(jnp.bfloat16)

    def brick(b, _):
        zero = jnp.zeros((edge, chan), jnp.float32)
        for side in range(2):
            cap = table_ref[side, pick_ref[b * 6 + side]].astype(jnp.float32)
            rows = jnp.concatenate([zero, cap, zero], axis=0)
            put(b, side * (edge + 1), rows, zero, zero)
            ybuf_ref[side] = table_ref[2 + side, pick_ref[b * 6 + 2 + side]].astype(jnp.float32)
            xbuf_ref[side] = table_ref[4 + side, pick_ref[b * 6 + 4 + side]].astype(jnp.float32)

        def layer(z, _):
            strip = pl.ds(pl.multiple_of(z * edge, edge), edge)
            rows = jnp.concatenate(
                [ybuf_ref[0, strip, :], fi_ref[b, z].astype(jnp.float32), ybuf_ref[1, strip, :]], axis=0
            )
            put(b, z + 1, rows, xbuf_ref[0, strip, :], xbuf_ref[1, strip, :])
            return 0

        lax.fori_loop(0, edge, layer, 0)
        return 0

    lax.fori_loop(0, slots, brick, 0)


def conv_kernel(place_ref, cols_ref, w_ref, lat_ref, emb_ref, out_ref, acc_ref):
    step = pl.program_id(0)
    slots, edge, plane, chan = lat_ref.shape
    half = edge // 2
    for b in range(slots):
        lhs = cols_ref[b, pl.ds(step, edge)].reshape(edge * plane, cols_ref.shape[-1])
        part = lax.dot_general(
            lhs, w_ref[...], (((1,), (1,)), ((), ())), preferred_element_type=jnp.float32
        )

        @pl.when(step == 0)
        def _():
            acc_ref[b] = part

        @pl.when(step > 0)
        def _():
            acc_ref[b] += part

    @pl.when(step == pl.num_programs(0) - 1)
    def _():
        in_low = lax.broadcasted_iota(jnp.int32, (edge * half // 2, edge, chan), 1) < half
        for b in range(slots):
            for kz in range(2):
                base = kz * half
                lat = lat_ref[b, base : base + half].astype(jnp.float32).reshape(half * plane, chan)
                total = acc_ref[b, base * plane : (base + half) * plane]
                refined = lat + (total + emb_ref[...])
                pairs = refined.reshape(half, 2, half // 2, 2, edge, chan)
                for ky in range(2):
                    first = pairs[:, ky, :, 0].reshape(-1, edge, chan)
                    second = pairs[:, ky, :, 1].reshape(-1, edge, chan)
                    low_mask = in_low[: first.shape[0]]
                    turned = (
                        pltpu.roll(first, half, 1),
                        pltpu.roll(second, half, 1),
                    )
                    child = (
                        jnp.where(low_mask, first, turned[1]),
                        jnp.where(low_mask, turned[0], second),
                    )
                    for kx in range(2):
                        k = b * 8 + kz * 4 + ky * 2 + kx
                        value = child[kx].reshape(half**3, chan).astype(jnp.bfloat16)

                        @pl.when(place_ref[k] >= 0)
                        def _():
                            out_ref[place_ref[k]] = value


def grow_kernel(source_ref, child_ref, up_ref, out_ref, rows_ref):
    step = pl.program_id(0)
    each = out_ref.shape[0]
    co = up_ref.shape[-1]
    voxels = child_ref.shape[1]
    lhs = jnp.concatenate([child_ref[source_ref[step * each + j]] for j in range(each)], axis=0)
    for pz in range(2):
        for py in range(2):
            p = pz * 4 + py * 2
            mats = jnp.concatenate([up_ref[p], up_ref[p + 1]], axis=1)
            res = jnp.dot(lhs, mats, preferred_element_type=jnp.float32)
            rows_ref[pl.ds(0, each * voxels, stride=2), :] = res[:, :co]
            rows_ref[pl.ds(1, each * voxels, stride=2), :] = res[:, co:]
            out_ref[:, :, pz, :, py] = (
                rows_ref[...].reshape(each, 4, 4, 8, co).astype(jnp.bfloat16)
            )


def body(latents, neighbours, owners, conv_weight, step_embed, up_weight):
    rows_n = lax.axis_size("row")
    cols_n = lax.axis_size("col")
    own_row = lax.axis_index("row")
    own_index = (lax.axis_index("depth") * rows_n + own_row) * cols_n + lax.axis_index("col")
    slots, edge, chan = latents.shape[3], latents.shape[4], latents.shape[-1]
    plane = edge * edge
    taps = conv_weight.shape[0]
    own_out = conv_weight.shape[2]
    co = up_weight.shape[-1]
    owner_ids = owners.reshape(slots * 8)

    note = jnp.zeros((own_out, 128), jnp.bfloat16)
    note = note.at[0, : slots * 8].set(owner_ids.astype(jnp.bfloat16))
    piece = conv_weight.transpose(2, 0, 1).reshape(own_out, taps * chan)
    weight = lax.all_gather(jnp.concatenate([piece, note], axis=1), "row", axis=0, tiled=True)

    lat = latents.reshape(slots, edge, plane, chan)
    face = jax.ShapeDtypeStruct((slots, plane, chan), jnp.bfloat16)
    fi, zlo, zhi, ylo, yhi, xlo, xhi = pl.pallas_call(
        norm_kernel,
        out_shape=[jax.ShapeDtypeStruct(lat.shape, jnp.bfloat16)] + [face] * 6,
        in_specs=whole(1),
        out_specs=whole(7),
        scratch_shapes=[pltpu.VMEM((chan // 128, edge * plane, 128), jnp.float32)],
        compiler_params=pltpu.CompilerParams(vmem_limit_bytes=32 * MB),
        cost_estimate=pl.CostEstimate(flops=4 * MB, bytes_accessed=2 * MB, transcendentals=MB),
    )(lat)

    def shift(face, axis, step):
        count = lax.axis_size(axis)
        pairs = [(i, i + step) for i in range(count) if 0 <= i + step < count]
        return lax.ppermute(face, axis, pairs)

    far = (
        shift(zhi, "depth", 1),
        shift(zlo, "depth", -1),
        shift(yhi, "row", 1),
        shift(ylo, "row", -1),
        shift(xhi, "col", 1),
        shift(xlo, "col", -1),
    )
    near_ids = neighbours.reshape(slots, 6)
    strides = jnp.array([-rows_n * cols_n, rows_n * cols_n, -cols_n, cols_n, -1, 1], jnp.int32)
    near_dev = near_ids // slots
    near_slot = near_ids % slots
    pick = jnp.where(
        near_ids < 0,
        2 * slots,
        jnp.where(
            near_dev == own_index,
            near_slot,
            jnp.where(near_dev == own_index + strides[None, :], slots + near_slot, 2 * slots),
        ),
    ).reshape(-1)

    columns = pl.pallas_call(
        columns_kernel,
        out_shape=jax.ShapeDtypeStruct((slots, edge + 2, plane, 9 * chan), jnp.bfloat16),
        in_specs=[pl.BlockSpec(memory_space=SMEM)] + whole(13),
        out_specs=pl.BlockSpec(memory_space=VMEM),
        scratch_shapes=[
            pltpu.VMEM((6, 2 * slots + 1, plane, chan), jnp.bfloat16),
            pltpu.VMEM((2, plane, chan), jnp.float32),
            pltpu.VMEM((2, plane, chan), jnp.float32),
        ],
        compiler_params=pltpu.CompilerParams(vmem_limit_bytes=40 * MB),
        cost_estimate=pl.CostEstimate(flops=16 * MB, bytes_accessed=12 * MB, transcendentals=0),
    )(pick, fi, zlo, zhi, ylo, yhi, xlo, xhi, *far)

    send_cap = 2
    is_valid = owner_ids >= 0
    target_row = jnp.where(is_valid, owner_ids // OCAP, -1)
    serial = jnp.arange(slots * 8, dtype=jnp.int32)
    before = serial[None, :] < serial[:, None]
    rank = jnp.sum(((target_row[None, :] == target_row[:, None]) & before).astype(jnp.int32), axis=1)
    place = jnp.where(is_valid, target_row * send_cap + rank, -1)

    outgoing = pl.pallas_call(
        conv_kernel,
        grid=(3,),
        out_shape=jax.ShapeDtypeStruct((rows_n * send_cap, plane, chan), jnp.bfloat16),
        in_specs=[
            pl.BlockSpec(memory_space=SMEM),
            pl.BlockSpec(memory_space=VMEM),
            pl.BlockSpec((chan, 9 * chan), lambda i: (0, i)),
            pl.BlockSpec(memory_space=VMEM),
            pl.BlockSpec(memory_space=VMEM),
        ],
        out_specs=pl.BlockSpec(memory_space=VMEM),
        scratch_shapes=[pltpu.VMEM((slots, edge * plane, chan), jnp.float32)],
        compiler_params=pltpu.CompilerParams(vmem_limit_bytes=48 * MB),
        cost_estimate=pl.CostEstimate(flops=5400 * MB, bytes_accessed=14 * MB, transcendentals=0),
    )(place, columns, weight, lat, step_embed.reshape(1, chan))

    arrived = lax.all_to_all(
        outgoing.reshape(rows_n, send_cap * plane, chan), "row", split_axis=0, concat_axis=0, tiled=True
    ).reshape(rows_n * send_cap, plane, chan)

    notes = weight[::own_out, taps * chan : taps * chan + slots * 8].astype(jnp.int32)
    mine = (notes >= 0) & (notes // OCAP == own_row)
    again = jnp.any(mine[:, None, :] & before[None], axis=2)
    origin = jnp.arange(rows_n, dtype=jnp.int32)[:, None] * send_cap + again.astype(jnp.int32)
    wanted = jnp.arange(OCAP, dtype=jnp.int32)[:, None, None]
    source = jnp.sum(jnp.where(mine[None] & (notes[None] % OCAP == wanted), origin[None], 0), axis=(1, 2))

    half = edge // 2
    each = 4
    grown = pl.pallas_call(
        grow_kernel,
        grid_spec=pltpu.PrefetchScalarGridSpec(
            num_scalar_prefetch=1,
            grid=(OCAP // each,),
            in_specs=whole(2),
            out_specs=pl.BlockSpec((each, half, 2, half, 2, edge, co), lambda i, s: (i, 0, 0, 0, 0, 0, 0)),
            scratch_shapes=[pltpu.VMEM((each * plane * 2, co), jnp.float32)],
        ),
        out_shape=jax.ShapeDtypeStruct((OCAP, half, 2, half, 2, edge, co), jnp.bfloat16),
        compiler_params=pltpu.CompilerParams(vmem_limit_bytes=32 * MB),
        cost_estimate=pl.CostEstimate(flops=540 * MB, bytes_accessed=4 * MB, transcendentals=0),
    )(source, arrived, up_weight)
    return grown.reshape(1, 1, 1, OCAP, edge, edge, edge, co)


def solution(mesh):
    return jax.shard_map(
        body,
        mesh=mesh,
        in_specs=(
            P("depth", "row", "col", None, None, None, None, None),
            P("depth", "row", "col", None, None),
            P("depth", "row", "col", None, None),
            P(None, None, "row"),
            P(),
            P(),
        ),
        out_specs=P("depth", "row", "col", None, None, None, None, None),
        check_vma=False,
    )
```

time: 206 us -> 121 us (0.59)
  waiting for transfers between devices: 97.5 us -> 49.6 us
  matrix products: 25.3 us -> 0 us
  local copies, waits for them, and re-layouts: 31.2 us -> 8.98 us
  Pallas kernels: 0 us -> 22.1 us
  starting transfers between devices: 32.4 us -> 21.1 us
    all_to_all x2 -> x1, waiting for transfers between devices: 92.3 us -> 26.2 us  [body(): lax.all_to_all(outgoing.reshape(rows_n, send_cap * plane, chan), 'row', s...]
    pallas_call x0 -> x4, Pallas kernels: none -> 22.1 us  [the longest x1 16.4 us: body(): pl.pallas_call(conv_kernel, grid=(3,), out_shape=jax.ShapeDtypeStruct((ro...]
    scatter x10 -> x0, local copies, waits for them, and re-layouts: 20.2 us -> none  [the longest x1 6.85 us: body(): outgoing = jnp.zeros((row_count * send_cap,) + item_shape, jnp.bfloat16)....]
    conv_general_dilated x1 -> x0, matrix products: 17.9 us -> none  [convolve(): lax.conv_general_dilated(padded, kernel, (1, 1, 1), 'VALID', dimension_nu...]
    all_gather x1, waiting for transfers between devices: 4.44 us -> 18.4 us  [body(): lax.all_gather(jnp.concatenate([piece, note], axis=1), 'row', axis=0, til...]
    all_to_all x2 -> x1, starting transfers between devices: 14.3 us -> 4.61 us  [body(): lax.all_to_all(outgoing.reshape(rows_n, send_cap * plane, chan), 'row', s...]
    dot_general x7 -> x0, matrix products: 7.46 us -> none  [the longest x6 6.27 us: borrowed(): picked = jnp.dot(picker, stacked, preferred_element_type=jnp.float32)]
    ppermute x6, waiting for transfers between devices: 0.02 us -> 5.05 us  [shift(): return lax.ppermute(face, axis, pairs)]
  transfers between devices with their start and end apart: 9 -> 8, of which waited for: 2 -> 3; matrix products, arithmetic and copies ran while one was open for 26% -> 4% of each run, Pallas kernels for 0% -> 2%
where the time goes in v1:
time: 121 us
  waiting for transfers between devices  49.6 us (41%)
  Pallas kernels  22.1 us (18%)
  starting transfers between devices  21.1 us (17%)
  between operations  13.5 us (11%)
  local copies, waits for them, and re-layouts  8.98 us (7%)
  other arithmetic  5.26 us (4%)
    all_to_all x1, waiting for transfers between devices, body(): lax.all_to_all(outgoing.reshape(rows_n, send_cap * plane, chan), 'row', s...  26.2 us
    all_gather x1, waiting for transfers between devices, body(): lax.all_gather(jnp.concatenate([piece, note], axis=1), 'row', axis=0, til...  18.4 us
    ppermute x6, starting transfers between devices, shift(): return lax.ppermute(face, axis, pairs)  16.5 us
    pallas_call x1, Pallas kernels, body(): pl.pallas_call(conv_kernel, grid=(3,), out_shape=jax.ShapeDtypeStruct((ro...  16.4 us
    unnamed x12, local copies, waits for them, and re-layouts  6.56 us
    ppermute x6, waiting for transfers between devices, shift(): return lax.ppermute(face, axis, pairs)  5.05 us
    all_to_all x1, starting transfers between devices, body(): lax.all_to_all(outgoing.reshape(rows_n, send_cap * plane, chan), 'row', s...  4.61 us
    pallas_call x1, Pallas kernels, body(): pl.pallas_call(grow_kernel, grid_spec=pltpu.PrefetchScalarGridSpec(num_sc...  3.26 us
  transfers between devices with their start and end apart: 8, of which 3 were waited for; matrix products, arithmetic and copies ran while one was open for 4% of the time, Pallas kernels for 2%

profile of v1, /device:TPU:1, one launch (start us, length us, event | category | flops | bytes accessed | tf_op | source)
XLA Modules:
  0.0 120.6 jit_solution(17053212493818543983)
XLA Ops:
  6.5 0.9 copy.11
  7.5 0.7 convert_reduce_fusion.1
  8.2 0.1 convert_element_type.25
  8.3 0.7 fusion.1
  9.0 1.1 copy-done.3
  10.1 0.7 shard_map.73
  10.8 3.9 %collective-permute-start = (bf16[3,64,256]{2,1,0:T(8,128)(2,1)S(1)}, bf16[3,64,256]{2,1,0:T(8,128)(2,1)S(1)}, u32[]{:S(2)}, u32[]{:S(2)}) collective-permute-start(bf16[3,64,256]{2,1,0:T(8,128)(2,1)S(1)} %get-tuple-element.26.zhi), channel_id=1, source_target_pairs={{0,128},{128,256},{256,384},{1,129},{129,257},{257,385},{2,130},{1... | collective-permute-start | bytes 294920 | tf_op jit(solution)/shard_map/ppermute | solution.py:202
  14.8 1.3 %collective-permute-start.1 = (bf16[3,64,256]{2,1,0:T(8,128)(2,1)S(1)}, bf16[3,64,256]{2,1,0:T(8,128)(2,1)S(1)}, u32[]{:S(2)}, u32[]{:S(2)}) collective-permute-start(bf16[3,64,256]{2,1,0:T(8,128)(2,1)S(1)} %get-tuple-element.25.zlo), channel_id=1, source_target_pairs={{128,0},{256,128},{384,256},{129,1},{257,129},{385,257},{130,2},{2... | collective-permute-start | bytes 294920 | tf_op jit(solution)/shard_map/ppermute | solution.py:202
  16.1 4.0 %collective-permute-start.2 = (bf16[3,64,256]{2,1,0:T(8,128)(2,1)S(1)}, bf16[3,64,256]{2,1,0:T(8,128)(2,1)S(1)}, u32[]{:S(2)}, u32[]{:S(2)}) collective-permute-start(bf16[3,64,256]{2,1,0:T(8,128)(2,1)S(1)} %get-tuple-element.28.yhi), channel_id=1, source_target_pairs={{0,8},{8,16},{16,24},{24,32},{32,40},{40,48},{48,56},{56,64},{64,7... | collective-permute-start | bytes 294920 | tf_op jit(solution)/shard_map/ppermute | solution.py:202
  20.2 3.4 %collective-permute-start.3 = (bf16[3,64,256]{2,1,0:T(8,128)(2,1)S(1)}, bf16[3,64,256]{2,1,0:T(8,128)(2,1)S(1)}, u32[]{:S(2)}, u32[]{:S(2)}) collective-permute-start(bf16[3,64,256]{2,1,0:T(8,128)(2,1)S(1)} %get-tuple-element.27.ylo), channel_id=1, source_target_pairs={{8,0},{16,8},{24,16},{32,24},{40,32},{48,40},{56,48},{64,56},{72,6... | collective-permute-start | bytes 294920 | tf_op jit(solution)/shard_map/ppermute | solution.py:202
  23.5 2.5 %collective-permute-start.4 = (bf16[3,64,256]{2,1,0:T(8,128)(2,1)S(1)}, bf16[3,64,256]{2,1,0:T(8,128)(2,1)S(1)}, u32[]{:S(2)}, u32[]{:S(2)}) collective-permute-start(bf16[3,64,256]{2,1,0:T(8,128)(2,1)S(1)} %get-tuple-element.30.xhi), channel_id=1, source_target_pairs={{0,1},{1,2},{2,3},{3,4},{4,5},{5,6},{6,7},{8,9},{9,10},{10,11},{11... | collective-permute-start | bytes 294920 | tf_op jit(solution)/shard_map/ppermute | solution.py:202
  26.1 0.7 broadcast_add_fusion
  26.8 0.1 eq.65
  26.9 0.7 remainder_reduce_fusion
  27.6 0.1 div.43
  27.7 0.7 compare_reduce_fusion
  28.4 0.1 lt.47
  28.6 0.7 reduce.3
  29.4 0.2 convert_reduce_fusion
  29.6 1.3 %collective-permute-start.5 = (bf16[3,64,256]{2,1,0:T(8,128)(2,1)S(1)}, bf16[3,64,256]{2,1,0:T(8,128)(2,1)S(1)}, u32[]{:S(2)}, u32[]{:S(2)}) collective-permute-start(bf16[3,64,256]{2,1,0:T(8,128)(2,1)S(1)} %get-tuple-element.29.xlo), channel_id=1, source_target_pairs={{1,0},{2,1},{3,2},{4,3},{5,4},{6,5},{7,6},{9,8},{10,9},{11,10},{12... | collective-permute-start | bytes 294920 | tf_op jit(solution)/shard_map/ppermute | solution.py:202
  31.0 5.0 %collective-permute-done.5.rx1 = bf16[3,64,256]{2,1,0:T(8,128)(2,1)S(1)} collective-permute-done((bf16[3,64,256]{2,1,0:T(8,128)(2,1)S(1)}, bf16[3,64,256]{2,1,0:T(8,128)(2,1)S(1)}, u32[]{:S(2)}, u32[]{:S(2)}) %collective-permute-start.5) | collective-permute-done | bytes 98336 | tf_op jit(solution)/shard_map/ppermute | solution.py:202
  36.0 1.7 %shard_map.74.cols_ref = bf16[3,10,64,2304]{3,2,1,0:T(8,128)(2,1)S(1)} custom-call(s32[18]{0:T(128)S(1)} %fusion.10.pick_ref, bf16[3,8,64,256]{3,2,1,0:T(8,128)(2,1)S(1)} %get-tuple-element.24.fi_ref, bf16[3,64,256]{2,1,0:T(8,128)(2,1)S(1)} %get-tuple-element.25.zlo, bf16[3,64,256]{2,1,0:T(8,128)(2,1)S(1)} %get-tuple-element.26.zhi, ...), custom_call_target="tpu_custom_call" | custom-call | flops 16777216 | bytes 12582912 | tf_op jit(solution)/shard_map/pallas_call | solution.py:226
  37.7 3.4 %copy-done = bf16[3,10,64,2304]{3,2,1,0:T(8,128)(2,1)} copy-done((bf16[3,10,64,2304]{3,2,1,0:T(8,128)(2,1)}, bf16[3,10,64,2304]{3,2,1,0:T(8,128)(2,1)S(1)}, u32[]{:S(2)}) %copy-start) | copy-done | bytes 8847384
  41.1 18.4 %all-gather.2.cloned.1.call-done.w_ref = bf16[256,7040]{1,0:T(8,128)(2,1)} async-done(((bf16[16,7040]{1,0:T(8,128)(2,1)}), bf16[256,7040]{1,0:T(8,128)(2,1)}) %all-gather.2.cloned.1.call-update) | async-done | bytes 3604496 | tf_op jit(solution)/shard_map/all_gather | solution.py:185
  59.5 2.0 %copy-done.2 = bf16[256,7040]{1,0:T(8,128)(2,1)S(1)} copy-done((bf16[256,7040]{1,0:T(8,128)(2,1)S(1)}, bf16[256,7040]{1,0:T(8,128)(2,1)}, u32[]{:S(2)}) %copy-start.2) | copy-done | bytes 3604504
  61.5 16.4 %shard_map.75 = bf16[32,64,256]{2,1,0:T(8,128)(2,1)} custom-call(s32[24]{0:T(128)S(1)} %compare_select_fusion.5.place_ref, bf16[3,10,64,2304]{3,2,1,0:T(8,128)(2,1)} %copy-done, bf16[256,7040]{1,0:T(8,128)(2,1)S(1)} %copy-done.2, bf16[3,8,64,256]{3,2,1,0:T(8,128)(2,1)S(1)} %bitcast.10, f32[1,256]{1,0:T(1,128)S(1)} %bitcast.11), custom_call_target="tpu_custom_call" | custom-call | flops 5662310400 | bytes 14680064 | tf_op jit(solution)/shard_map/pallas_call | solution.py:248
  77.9 4.6 %all-to-all-start = ((bf16[16,128,256]{2,1,0:T(8,128)(2,1)}), bf16[16,128,256]{2,1,0:T(8,128)(2,1)S(1)}, u32[]{:S(2)}, u32[]{:S(2)}) async-start(bf16[16,128,256]{2,1,0:T(8,128)(2,1)} %bitcast.3), calls=%async_computation | async-start | bytes 2097152 | tf_op jit(solution)/shard_map/all_to_all | solution.py:265
  82.6 0.9 slice.19
  83.4 0.4 and_reduce_fusion
  83.9 0.4 select_reduce_fusion.source_ref
  84.3 26.2 %all-to-all-done = bf16[16,128,256]{2,1,0:T(8,128)(2,1)S(1)} async-done(((bf16[16,128,256]{2,1,0:T(8,128)(2,1)}), bf16[16,128,256]{2,1,0:T(8,128)(2,1)S(1)}, u32[]{:S(2)}, u32[]{:S(2)}) %all-to-all-start) | async-done | bytes 1048608 | tf_op jit(solution)/shard_map/all_to_all | solution.py:265
  110.5 3.3 %shard_map.76 = bf16[16,4,2,4,2,8,128]{6,5,4,3,2,1,0:T(8,128)(2,1)} custom-call(s32[16]{0:T(128)S(1)} %select_reduce_fusion.source_ref, bf16[32,64,256]{2,1,0:T(8,128)(2,1)S(1)} %bitcast.8, bf16[8,256,128]{2,1,0:T(8,128)(2,1)S(1)} %copy-done.1), custom_call_target="tpu_custom_call" | custom-call | flops 566231040 | bytes 4194304 | tf_op jit(solution)/shard_map/pallas_call | solution.py:278
  (27 shorter events, 0.4 us)
Async XLA Ops:
  6.5 52.9 %all-gather.2.cloned.1.call-start = ((), (), s32[]{:S(2)}) async-start(), calls=%async_computation.1 | async-start | bytes 3829760 | tf_op jit(solution)/shard_map/all_gather | solution.py:185
  9.0 1.1 copy-start.3
  10.8 18.8 %collective-permute-start = (bf16[3,64,256]{2,1,0:T(8,128)(2,1)S(1)}, bf16[3,64,256]{2,1,0:T(8,128)(2,1)S(1)}, u32[]{:S(2)}, u32[]{:S(2)}) collective-permute-start(bf16[3,64,256]{2,1,0:T(8,128)(2,1)S(1)} %get-tuple-element.26.zhi), channel_id=1, source_target_pairs={{0,128},{128,256},{256,384},{1,129},{129,257},{257,385},{2,130},{1... | collective-permute-start | bytes 294920 | tf_op jit(solution)/shard_map/ppermute | solution.py:202
  14.8 16.1 %collective-permute-start.1 = (bf16[3,64,256]{2,1,0:T(8,128)(2,1)S(1)}, bf16[3,64,256]{2,1,0:T(8,128)(2,1)S(1)}, u32[]{:S(2)}, u32[]{:S(2)}) collective-permute-start(bf16[3,64,256]{2,1,0:T(8,128)(2,1)S(1)} %get-tuple-element.25.zlo), channel_id=1, source_target_pairs={{128,0},{256,128},{384,256},{129,1},{257,129},{385,257},{130,2},{2... | collective-permute-start | bytes 294920 | tf_op jit(solution)/shard_map/ppermute | solution.py:202
  16.1 14.8 %collective-permute-start.2 = (bf16[3,64,256]{2,1,0:T(8,128)(2,1)S(1)}, bf16[3,64,256]{2,1,0:T(8,128)(2,1)S(1)}, u32[]{:S(2)}, u32[]{:S(2)}) collective-permute-start(bf16[3,64,256]{2,1,0:T(8,128)(2,1)S(1)} %get-tuple-element.28.yhi), channel_id=1, source_target_pairs={{0,8},{8,16},{16,24},{24,32},{32,40},{40,48},{48,56},{56,64},{64,7... | collective-permute-start | bytes 294920 | tf_op jit(solution)/shard_map/ppermute | solution.py:202
  20.2 10.8 %collective-permute-start.3 = (bf16[3,64,256]{2,1,0:T(8,128)(2,1)S(1)}, bf16[3,64,256]{2,1,0:T(8,128)(2,1)S(1)}, u32[]{:S(2)}, u32[]{:S(2)}) collective-permute-start(bf16[3,64,256]{2,1,0:T(8,128)(2,1)S(1)} %get-tuple-element.27.ylo), channel_id=1, source_target_pairs={{8,0},{16,8},{24,16},{32,24},{40,32},{48,40},{56,48},{64,56},{72,6... | collective-permute-start | bytes 294920 | tf_op jit(solution)/shard_map/ppermute | solution.py:202
  23.5 7.4 %collective-permute-start.4 = (bf16[3,64,256]{2,1,0:T(8,128)(2,1)S(1)}, bf16[3,64,256]{2,1,0:T(8,128)(2,1)S(1)}, u32[]{:S(2)}, u32[]{:S(2)}) collective-permute-start(bf16[3,64,256]{2,1,0:T(8,128)(2,1)S(1)} %get-tuple-element.30.xhi), channel_id=1, source_target_pairs={{0,1},{1,2},{2,3},{3,4},{4,5},{5,6},{6,7},{8,9},{9,10},{10,11},{11... | collective-permute-start | bytes 294920 | tf_op jit(solution)/shard_map/ppermute | solution.py:202
  29.6 6.4 %collective-permute-start.5 = (bf16[3,64,256]{2,1,0:T(8,128)(2,1)S(1)}, bf16[3,64,256]{2,1,0:T(8,128)(2,1)S(1)}, u32[]{:S(2)}, u32[]{:S(2)}) collective-permute-start(bf16[3,64,256]{2,1,0:T(8,128)(2,1)S(1)} %get-tuple-element.29.xlo), channel_id=1, source_target_pairs={{1,0},{2,1},{3,2},{4,3},{5,4},{6,5},{7,6},{9,8},{10,9},{11,10},{12... | collective-permute-start | bytes 294920 | tf_op jit(solution)/shard_map/ppermute | solution.py:202
  36.0 23.5 %copy-start.4 = (bf16[1,1,1,3,8,8,8,256]{7,6,5,4,3,2,1,0:T(8,128)(2,1)S(1)}, bf16[1,1,1,3,8,8,8,256]{7,6,5,4,3,2,1,0:T(8,128)(2,1)}, u32[]{:S(2)}) copy-start(bf16[1,1,1,3,8,8,8,256]{7,6,5,4,3,2,1,0:T(8,128)(2,1)} %param.9) | copy-start | bytes 2359300
  36.0 23.5 %copy-start.5 = (f32[256]{0:T(256)S(1)}, f32[256]{0:T(256)}, u32[]{:S(2)}) copy-start(f32[256]{0:T(256)} %param.13) | copy-start | bytes 3076
  37.7 3.4 %copy-start = (bf16[3,10,64,2304]{3,2,1,0:T(8,128)(2,1)}, bf16[3,10,64,2304]{3,2,1,0:T(8,128)(2,1)S(1)}, u32[]{:S(2)}) copy-start(bf16[3,10,64,2304]{3,2,1,0:T(8,128)(2,1)S(1)} %shard_map.74.cols_ref) | copy-start | bytes 26542084
  59.5 2.0 %copy-start.2 = (bf16[256,7040]{1,0:T(8,128)(2,1)S(1)}, bf16[256,7040]{1,0:T(8,128)(2,1)}, u32[]{:S(2)}) copy-start(bf16[256,7040]{1,0:T(8,128)(2,1)} %all-gather.2.cloned.1.call-done.w_ref) | copy-start | bytes 10813444
  61.5 49.0 %copy-start.1 = (bf16[8,256,128]{2,1,0:T(8,128)(2,1)S(1)}, bf16[8,256,128]{2,1,0:T(8,128)(2,1)}, u32[]{:S(2)}) copy-start(bf16[8,256,128]{2,1,0:T(8,128)(2,1)} %up_ref.1) | copy-start | bytes 1572868
  77.9 32.5 %all-to-all-start = ((bf16[16,128,256]{2,1,0:T(8,128)(2,1)}), bf16[16,128,256]{2,1,0:T(8,128)(2,1)S(1)}, u32[]{:S(2)}, u32[]{:S(2)}) async-start(bf16[16,128,256]{2,1,0:T(8,128)(2,1)} %bitcast.3), calls=%async_computation | async-start | bytes 2097152 | tf_op jit(solution)/shard_map/all_to_all | solution.py:265
Sparse Core Ops, SparseCore 0:
  9.5 49.9 all-gather.1

commit v2 on v1

v2 whole, which is shorter than its diff:
```python
import jax
import jax.numpy as jnp
from jax import lax
from jax.experimental import pallas as pl
from jax.experimental.pallas import tpu as pltpu
from jax.sharding import PartitionSpec as P

OCAP = 16
VMEM = pltpu.VMEM
SMEM = pltpu.SMEM
MB = 1024 * 1024


def whole(count):
    return [pl.BlockSpec(memory_space=VMEM)] * count


def norm_kernel(lat_ref, fi_ref, zlo_ref, zhi_ref, ylo_ref, yhi_ref, xlo_ref, xhi_ref, rows_ref):
    slots, edge, plane, _ = lat_ref.shape
    lanes = rows_ref.shape[-1]
    pieces = rows_ref.shape[0]
    for b in range(slots):
        for z in range(edge):
            v = lat_ref[b, z].astype(jnp.float32)
            mean_square = jnp.mean(v * v, axis=-1, keepdims=True)
            n = v * lax.rsqrt(mean_square + 1e-06)
            s = n / (1.0 + jnp.exp(-n))
            half = s.astype(jnp.bfloat16)
            fi_ref[b, z] = half
            if z == 0:
                zlo_ref[b] = half
            if z == edge - 1:
                zhi_ref[b] = half
            for p in range(pieces):
                rows_ref[p, pl.ds(z * plane, plane), :] = s[:, p * lanes : (p + 1) * lanes]
        for p in range(pieces):
            cols = pl.ds(p * lanes, lanes)
            xlo_ref[b, :, cols] = rows_ref[p, pl.ds(0, plane, stride=edge), :].astype(jnp.bfloat16)
            xhi_ref[b, :, cols] = rows_ref[p, pl.ds(edge - 1, plane, stride=edge), :].astype(
                jnp.bfloat16
            )
            low = [rows_ref[p, pl.ds(z * plane, edge), :] for z in range(edge)]
            ylo_ref[b, :, cols] = jnp.concatenate(low, axis=0).astype(jnp.bfloat16)
            high = [rows_ref[p, pl.ds(z * plane + plane - edge, edge), :] for z in range(edge)]
            yhi_ref[b, :, cols] = jnp.concatenate(high, axis=0).astype(jnp.bfloat16)


def quarter_kernel(owners_ref, weight_ref, out_ref):
    taps, rows, chan = weight_ref.shape
    count = out_ref.shape[1] // chan
    wide = out_ref.shape[1] - count * chan
    first = colour_here() * count
    lane = lax.broadcasted_iota(jnp.int32, (rows, wide), 1)
    note = jnp.zeros((rows, wide), jnp.int32)
    children = owners_ref.shape[-1]
    for i in range(owners_ref.shape[-2] * children):
        note = jnp.where(lane == i, owners_ref[0, 0, 0, i // children, i % children], note)
    for j in range(count):
        out_ref[:, j * chan : (j + 1) * chan] = weight_ref[jnp.minimum(first + j, taps - 1)]
    out_ref[:, count * chan :] = note.astype(jnp.float32).astype(jnp.bfloat16)


def columns_kernel(
    near_ref, fi_ref, zlo, zhi, ylo, yhi, xlo, xhi, rz0, rz1, ry0, ry1, rx0, rx1, out_ref, table_ref, ybuf_ref, xbuf_ref
):
    slots, edge, plane, chan = fi_ref.shape
    near = (zhi, zlo, yhi, ylo, xhi, xlo)
    far = (rz0, rz1, ry0, ry1, rx0, rx1)
    for d in range(6):
        table_ref[d, 0:slots] = near[d][...]
        table_ref[d, slots : 2 * slots] = far[d][...]
        table_ref[d, 2 * slots] = jnp.zeros((plane, chan), jnp.bfloat16)
    out_ref[9] = jnp.zeros(out_ref.shape[1:], jnp.bfloat16)
    at_x = lax.rem(lax.broadcasted_iota(jnp.int32, (plane + 2 * edge, chan), 0), edge)
    rows_n = lax.axis_size("row")
    cols_n = lax.axis_size("col")
    own = (lax.axis_index("depth") * rows_n + lax.axis_index("row")) * cols_n + lax.axis_index("col")
    steps = (-rows_n * cols_n, rows_n * cols_n, -cols_n, cols_n, -1, 1)

    def chosen(b, d):
        named = near_ref[0, 0, 0, b, d]
        here = named - own * slots
        there = named - (own + steps[d]) * slots
        is_here = (named >= 0) & (here >= 0) & (here < slots)
        is_there = (named >= 0) & (there >= 0) & (there < slots)
        index = jnp.where(is_here, here, jnp.where(is_there, slots + there, 2 * slots))
        return table_ref[d, index].astype(jnp.float32)

    def put(b, z, rows, left, right):
        zero = jnp.zeros((edge, chan), jnp.float32)

        def spread(halo):
            mid = jnp.broadcast_to(halo[:, None, :], (edge, edge, chan)).reshape(plane, chan)
            return jnp.concatenate([zero, mid, zero], axis=0)

        count = plane + 2 * edge
        moved = (
            jnp.where(at_x == 0, spread(left), pltpu.roll(rows, 1, 0)),
            rows,
            jnp.where(at_x == edge - 1, spread(right), pltpu.roll(rows, count - 1, 0)),
        )
        for dx in range(3):
            for dy in range(3):
                out_ref[dy * 3 + dx, b, z] = moved[dx][dy * edge : dy * edge + plane].astype(
                    jnp.bfloat16
                )

    def brick(b, _):
        zero = jnp.zeros((edge, chan), jnp.float32)
        for side in range(2):
            rows = jnp.concatenate([zero, chosen(b, side), zero], axis=0)
            put(b, side * (edge + 1), rows, zero, zero)
            ybuf_ref[side] = chosen(b, 2 + side)
            xbuf_ref[side] = chosen(b, 4 + side)

        def layer(z, _):
            strip = pl.ds(pl.multiple_of(z * edge, edge), edge)
            rows = jnp.concatenate(
                [ybuf_ref[0, strip, :], fi_ref[b, z].astype(jnp.float32), ybuf_ref[1, strip, :]], axis=0
            )
            put(b, z + 1, rows, xbuf_ref[0, strip, :], xbuf_ref[1, strip, :])
            return 0

        lax.fori_loop(0, edge, layer, 0)
        return 0

    lax.fori_loop(0, slots, brick, 0)


def colour_here():
    return lax.rem(lax.axis_index("depth") + 2 * lax.axis_index("col"), 4)


def core_here():
    return lax.rem(lax.axis_index("row"), 2)


def tap_rows(cols_ref, b, first, count):
    edge, plane, chan = cols_ref.shape[2] - 2, cols_ref.shape[3], cols_ref.shape[4]
    out = []
    for j in range(count):
        tap = first + j
        live = tap < 27
        which = jnp.where(live, lax.rem(tap, 9), 9)
        layer = jnp.where(live, lax.div(tap, 9), 0)
        out.append(cols_ref[which, b, pl.ds(layer, edge)].reshape(edge * plane, chan))
    return out


def times(lhs, weight):
    return lax.dot_general(
        jnp.concatenate(lhs, axis=1), weight, (((1,), (1,)), ((), ())), preferred_element_type=jnp.float32
    )


def own_kernel(cols_ref, own_ref, acc_ref):
    chan = cols_ref.shape[4]
    count = own_ref.shape[1] // chan
    first = colour_here() * count
    for b in range(acc_ref.shape[0]):
        acc_ref[b] = times(tap_rows(cols_ref, b, first, count), own_ref[:, : count * chan])


def side_kernel(cols_ref, xw_ref, zw_ref, old_ref, acc_ref):
    chan = cols_ref.shape[4]
    count, part = xw_ref.shape[1] // chan, zw_ref.shape[1] // chan
    core, colour = core_here(), colour_here()
    x_first = lax.rem(colour + 3 + 2 * core, 4) * count
    z_first = lax.rem(colour + 2, 4) * count + core * (count - part)
    for b in range(acc_ref.shape[0]):
        got = times(tap_rows(cols_ref, b, x_first, count), xw_ref[:, : count * chan])
        got += times(tap_rows(cols_ref, b, z_first, part), zw_ref[...])
        acc_ref[b] = old_ref[b] + got


def last_kernel(owners_ref, cols_ref, xw_ref, zw_ref, lat_ref, emb_ref, old_ref, out_ref):
    slots, edge, plane, chan = lat_ref.shape
    half = edge // 2
    count, part = xw_ref.shape[1] // chan, zw_ref.shape[1] // chan
    rest = count - part
    core, colour = core_here(), colour_here()
    x_first = lax.rem(colour + 1 + 2 * core, 4) * count
    z_first = lax.rem(colour + 2, 4) * count + (1 - core) * part
    lanes = pl.ds(pl.multiple_of((1 - core) * (part - rest) * chan, chan), rest * chan)

    targets = [owners_ref[0, 0, 0, i // 8, i % 8] for i in range(slots * 8)]
    target_rows = [lax.shift_right_arithmetic(t, 4) for t in targets]
    in_low = lax.broadcasted_iota(jnp.int32, (half * half // 2, edge, chan), 1) < half
    for b in range(slots):
        got = times(tap_rows(cols_ref, b, x_first, count), xw_ref[:, : count * chan])
        got += times(tap_rows(cols_ref, b, z_first, rest), zw_ref[:, lanes])
        total = old_ref[b] + got
        lat = lat_ref[b].astype(jnp.float32).reshape(edge * plane, chan)
        refined = lat + (total + emb_ref[...])
        pairs = refined.reshape(2, half, 2, half // 2, 2, edge, chan)
        for kz in range(2):
            for ky in range(2):
                first = pairs[kz, :, ky, :, 0].reshape(-1, edge, chan)
                second = pairs[kz, :, ky, :, 1].reshape(-1, edge, chan)
                child = (
                    jnp.where(in_low, first, pltpu.roll(second, half, 1)),
                    jnp.where(in_low, pltpu.roll(first, half, 1), second),
                )
                for kx in range(2):
                    k = b * 8 + kz * 4 + ky * 2 + kx
                    value = child[kx].reshape(half**3, chan).astype(jnp.bfloat16)
                    rank = 0
                    for j in range(k):
                        rank += (target_rows[j] == target_rows[k]).astype(jnp.int32)
                    place = target_rows[k] * 2 + rank

                    @pl.when(targets[k] >= 0)
                    def _():
                        out_ref[place] = value


def grow_kernel(source_ref, child_ref, up_ref, out_ref, rows_ref):
    step = pl.program_id(0)
    each = out_ref.shape[0]
    co = up_ref.shape[-1]
    voxels = child_ref.shape[1]
    lhs = jnp.concatenate([child_ref[source_ref[step * each + j]] for j in range(each)], axis=0)
    for pz in range(2):
        for py in range(2):
            p = pz * 4 + py * 2
            mats = jnp.concatenate([up_ref[p], up_ref[p + 1]], axis=1)
            res = jnp.dot(lhs, mats, preferred_element_type=jnp.float32)
            rows_ref[pl.ds(0, each * voxels, stride=2), :] = res[:, :co]
            rows_ref[pl.ds(1, each * voxels, stride=2), :] = res[:, co:]
            out_ref[:, :, pz, :, py] = (
                rows_ref[...].reshape(each, 4, 4, 8, co).astype(jnp.bfloat16)
            )


def body(latents, neighbours, owners, conv_weight, step_embed, up_weight):
    rows_n = lax.axis_size("row")
    cols_n = lax.axis_size("col")
    slots, edge, chan = latents.shape[3], latents.shape[4], latents.shape[-1]
    plane = edge * edge
    taps = conv_weight.shape[0]
    own_out = conv_weight.shape[2]
    co = up_weight.shape[-1]
    quarter = (taps + 1) // 4
    part = quarter // 2 + 1
    core = core_here()

    smem = pl.BlockSpec(memory_space=SMEM)
    piece = pl.pallas_call(
        quarter_kernel,
        out_shape=jax.ShapeDtypeStruct((own_out, quarter * chan + 128), jnp.bfloat16),
        in_specs=[smem] + whole(1),
        out_specs=pl.BlockSpec(memory_space=VMEM),
        compiler_params=pltpu.CompilerParams(vmem_limit_bytes=4 * MB),
    )(owners, conv_weight.transpose(0, 2, 1))
    own_w = lax.all_gather(piece, "row", axis=0, tiled=True)
    depth_n = lax.axis_size("depth")
    x_pairs = [
        (d * rows_n + r, (d + 1 - 2 * (r % 2)) % depth_n * rows_n + r)
        for d in range(depth_n)
        for r in range(rows_n)
    ]
    z_pairs = [
        (r * cols_n + c, r * cols_n + (c + 1 - 2 * (r % 2)) % cols_n)
        for r in range(rows_n)
        for c in range(cols_n)
    ]
    swap = [(r, r ^ 1) for r in range(rows_n)]
    z_send = lax.dynamic_slice(own_w, (0, core * (quarter - part) * chan), (chan, part * chan))
    x_got = lax.ppermute(own_w, ("depth", "row"), x_pairs)
    z_got = lax.ppermute(z_send, ("row", "col"), z_pairs)
    lat, own_w = lax.optimization_barrier((latents.reshape(slots, edge, plane, chan), own_w))
    face = jax.ShapeDtypeStruct((slots, plane, chan), jnp.bfloat16)
    fi, zlo, zhi, ylo, yhi, xlo, xhi = pl.pallas_call(
        norm_kernel,
        out_shape=[jax.ShapeDtypeStruct(lat.shape, jnp.bfloat16)] + [face] * 6,
        in_specs=whole(1),
        out_specs=whole(7),
        scratch_shapes=[pltpu.VMEM((chan // 128, edge * plane, 128), jnp.float32)],
        compiler_params=pltpu.CompilerParams(vmem_limit_bytes=6 * MB),
        cost_estimate=pl.CostEstimate(flops=4 * MB, bytes_accessed=2 * MB, transcendentals=MB),
    )(lat)

    def shift(face, axis, step):
        count = lax.axis_size(axis)
        pairs = [(i, i + step) for i in range(count) if 0 <= i + step < count]
        return lax.ppermute(face, axis, pairs)

    far = (
        shift(zhi, "depth", 1),
        shift(zlo, "depth", -1),
        shift(yhi, "row", 1),
        shift(ylo, "row", -1),
        shift(xhi, "col", 1),
        shift(xlo, "col", -1),
    )
    x_got, z_got, far = lax.optimization_barrier((x_got, z_got, far))
    x_other = lax.ppermute(x_got, "row", swap)
    z_other = lax.ppermute(z_got, "row", swap)

    columns = pl.pallas_call(
        columns_kernel,
        out_shape=jax.ShapeDtypeStruct((10, slots, edge + 2, plane, chan), jnp.bfloat16),
        in_specs=[smem] + whole(13),
        out_specs=pl.BlockSpec(memory_space=VMEM),
        scratch_shapes=[
            pltpu.VMEM((6, 2 * slots + 1, plane, chan), jnp.bfloat16),
            pltpu.VMEM((2, plane, chan), jnp.float32),
            pltpu.VMEM((2, plane, chan), jnp.float32),
        ],
        compiler_params=pltpu.CompilerParams(vmem_limit_bytes=8 * MB),
        cost_estimate=pl.CostEstimate(flops=16 * MB, bytes_accessed=6 * MB, transcendentals=0),
    )(neighbours, fi, zlo, zhi, ylo, yhi, xlo, xhi, *far)

    send_cap = 2
    acc_shape = jax.ShapeDtypeStruct((slots, edge * plane, chan), jnp.float32)
    params = pltpu.CompilerParams(vmem_limit_bytes=10 * MB)
    acc = pl.pallas_call(
        own_kernel,
        out_shape=acc_shape,
        in_specs=whole(2),
        out_specs=pl.BlockSpec(memory_space=VMEM),
        compiler_params=params,
        cost_estimate=pl.CostEstimate(flops=1400 * MB, bytes_accessed=3 * MB, transcendentals=0),
    )(columns, own_w)
    acc = pl.pallas_call(
        side_kernel,
        out_shape=acc_shape,
        in_specs=whole(4),
        out_specs=pl.BlockSpec(memory_space=VMEM),
        compiler_params=params,
        cost_estimate=pl.CostEstimate(flops=2200 * MB, bytes_accessed=3 * MB, transcendentals=0),
    )(columns, x_got, z_got, acc)
    outgoing = pl.pallas_call(
        last_kernel,
        out_shape=jax.ShapeDtypeStruct((rows_n * send_cap, plane, chan), jnp.bfloat16),
        in_specs=[smem] + whole(6),
        out_specs=pl.BlockSpec(memory_space=VMEM),
        compiler_params=params,
        cost_estimate=pl.CostEstimate(flops=2000 * MB, bytes_accessed=3 * MB, transcendentals=0),
    )(owners, columns, x_other, z_other, lat, step_embed.reshape(1, chan), acc)

    arrived = lax.all_to_all(
        outgoing.reshape(rows_n, send_cap * plane, chan), "row", split_axis=0, concat_axis=0, tiled=True
    ).reshape(rows_n * send_cap, plane, chan)

    end = quarter * chan
    notes = own_w[::own_out, end : end + slots * 8].astype(jnp.int32)
    serial = jnp.arange(slots * 8, dtype=jnp.int32)
    before = serial[None, :] < serial[:, None]
    own_row = lax.axis_index("row")
    mine = (notes >= 0) & (notes // OCAP == own_row)
    again = jnp.any(mine[:, None, :] & before[None], axis=2)
    origin = jnp.arange(rows_n, dtype=jnp.int32)[:, None] * send_cap + again.astype(jnp.int32)
    wanted = jnp.arange(OCAP, dtype=jnp.int32)[:, None, None]
    source = jnp.sum(jnp.where(mine[None] & (notes[None] % OCAP == wanted), origin[None], 0), axis=(1, 2))

    half = edge // 2
    each = 4
    grown = pl.pallas_call(
        grow_kernel,
        grid_spec=pltpu.PrefetchScalarGridSpec(
            num_scalar_prefetch=1,
            grid=(OCAP // each,),
            in_specs=whole(2),
            out_specs=pl.BlockSpec((each, half, 2, half, 2, edge, co), lambda i, s: (i, 0, 0, 0, 0, 0, 0)),
            scratch_shapes=[pltpu.VMEM((each * plane * 2, co), jnp.float32)],
        ),
        out_shape=jax.ShapeDtypeStruct((OCAP, half, 2, half, 2, edge, co), jnp.bfloat16),
        compiler_params=pltpu.CompilerParams(vmem_limit_bytes=12 * MB),
        cost_estimate=pl.CostEstimate(flops=540 * MB, bytes_accessed=4 * MB, transcendentals=0),
    )(source, arrived, up_weight)
    return grown.reshape(1, 1, 1, OCAP, edge, edge, edge, co)


def solution(mesh):
    return jax.shard_map(
        body,
        mesh=mesh,
        in_specs=(
            P("depth", "row", "col", None, None, None, None, None),
            P("depth", "row", "col", None, None),
            P("depth", "row", "col", None, None),
            P(None, None, "row"),
            P(),
            P(),
        ),
        out_specs=P("depth", "row", "col", None, None, None, None, None),
        check_vma=False,
    )
```

time: 121 us -> 109 us (0.901)
  blocking collectives: 0 us -> 24.3 us
  waiting for transfers between devices: 49.6 us -> 32.1 us
  between operations: 13.5 us -> 0.23 us
  starting transfers between devices: 21.1 us -> 31.8 us
  local copies, waits for them, and re-layouts: 8.98 us -> 1.81 us
  Pallas kernels: 22.1 us -> 16.4 us
  other arithmetic: 5.26 us -> 0.85 us
    all_gather x0 -> x1, blocking collectives: none -> 24.3 us  [body(): own_w = lax.all_gather(piece, 'row', axis=0, tiled=True)]
    all_gather x1 -> x0, waiting for transfers between devices: 18.4 us -> none  [body(): lax.all_gather(jnp.concatenate([piece, note], axis=1), 'row', axis=0, til...]
    ppermute x0 -> x4, starting transfers between devices: none -> 16.7 us  [the longest x1 10.5 us: body(): z_got = lax.ppermute(z_send, ('row', 'col'), z_pairs)]
    ppermute x6, starting transfers between devices: 16.5 us -> 9.5 us  [shift(): return lax.ppermute(face, axis, pairs)]
    pallas_call x2 -> x5, Pallas kernels: 18.1 us -> 12.4 us  [the longest x1 5.99 us: body(): pl.pallas_call(last_kernel, out_shape=jax.ShapeDtypeStruct((rows_n * send...]
    unnamed x12, local copies, waits for them, and re-layouts: 6.56 us -> 1.71 us
  transfers between devices with their start and end apart: 8 -> 11, of which waited for: 3 -> 3; matrix products, arithmetic and copies ran while one was open for 4% -> 1% of each run, Pallas kernels for 2% -> 6%
where the time goes in v2:
time: 109 us; the launch traced here: 108 us
  waiting for transfers between devices  32.1 us (29%)
  starting transfers between devices  31.8 us (29%)
  blocking collectives  24.3 us (22%)
  Pallas kernels  16.4 us (15%)
  local copies, waits for them, and re-layouts  1.81 us (2%)
    all_to_all x1, waiting for transfers between devices, body(): lax.all_to_all(outgoing.reshape(rows_n, send_cap * plane, chan), 'row', s...  27 us
    all_gather x1, blocking collectives, body(): own_w = lax.all_gather(piece, 'row', axis=0, tiled=True)  24.3 us
    ppermute x1, starting transfers between devices, body(): z_got = lax.ppermute(z_send, ('row', 'col'), z_pairs)  10.5 us
    ppermute x6, starting transfers between devices, shift(): return lax.ppermute(face, axis, pairs)  9.5 us
    pallas_call x1, Pallas kernels, body(): pl.pallas_call(last_kernel, out_shape=jax.ShapeDtypeStruct((rows_n * send...  5.99 us
    all_to_all x1, starting transfers between devices, body(): lax.all_to_all(outgoing.reshape(rows_n, send_cap * plane, chan), 'row', s...  5.6 us
    ppermute x6, waiting for transfers between devices, shift(): return lax.ppermute(face, axis, pairs)  5.1 us
    pallas_call x1, Pallas kernels, body(): pl.pallas_call(grow_kernel, grid_spec=pltpu.PrefetchScalarGridSpec(num_sc...  3.25 us
  transfers between devices with their start and end apart: 11, of which 3 were waited for; matrix products, arithmetic and copies ran while one was open for 1% of the time, Pallas kernels for 6%

profile of v2, /device:TPU:1, one launch (start us, length us, event | category | flops | bytes accessed | tf_op | source)
XLA Modules:
  0.0 107.5 jit_solution(6719400069297765834)
XLA Ops:
  0.0 0.8 copy.10.owners_ref
  0.8 0.9 copy-done.2
  1.7 0.6 shard_map.64
  2.3 0.0 copy-start.4
  2.3 24.3 %all_gather.3.own_ref = bf16[256,1920]{1,0:T(8,128)(2,1)S(1)} all-gather(bf16[16,1920]{1,0:T(8,128)(2,1)S(1)} %shard_map.64), channel_id=1, replica_groups=mesh['depth'=4,'row'=16,'col'=8] {'row'}, dimensions={0}, use_global_device_ids=true | all-gather | bytes 1044480 | tf_op jit(solution)/shard_map/all_gather | solution.py:255
  26.6 1.9 %collective-permute-start = (bf16[256,1920]{1,0:T(8,128)(2,1)S(1)}, bf16[256,1920]{1,0:T(8,128)(2,1)S(1)}, u32[]{:S(2)}, u32[]{:S(2)}) collective-permute-start(bf16[256,1920]{1,0:T(8,128)(2,1)S(1)} %all_gather.3.own_ref), channel_id=1, source_target_pairs={{0,128},{8,392},{16,144},{24,408},{32,160},{40,424},{48,176},{56,4... | collective-permute-start | bytes 2949128 | tf_op jit(solution)/shard_map/ppermute | solution.py:269
  28.5 0.1 constant_dynamic-slice_fusion
  28.6 10.5 %collective-permute-start.1 = (bf16[256,1024]{1,0:T(8,128)(2,1)S(1)}, bf16[256,1024]{1,0:T(8,128)(2,1)S(1)}, u32[]{:S(2)}, u32[]{:S(2)}) collective-permute-start(bf16[256,1024]{1,0:T(8,128)(2,1)S(1)} %constant_dynamic-slice_fusion), channel_id=1, source_target_pairs={{0,1},{1,2},{2,3},{3,4},{4,5},{5,6},{6,7},{7,0},{8,15},{9,8},{10,9... | collective-permute-start | bytes 1572872 | tf_op jit(solution)/shard_map/ppermute | solution.py:270
  39.1 0.7 shard_map.65
  39.8 1.3 %collective-permute-start.2 = (bf16[3,64,256]{2,1,0:T(8,128)(2,1)S(1)}, bf16[3,64,256]{2,1,0:T(8,128)(2,1)S(1)}, u32[]{:S(2)}, u32[]{:S(2)}) collective-permute-start(bf16[3,64,256]{2,1,0:T(8,128)(2,1)S(1)} %get-tuple-element.26.zhi), channel_id=1, source_target_pairs={{0,128},{128,256},{256,384},{1,129},{129,257},{257,385},{2,130},{1... | collective-permute-start | bytes 294920 | tf_op jit(solution)/shard_map/ppermute | solution.py:286
  41.1 1.3 %collective-permute-start.3 = (bf16[3,64,256]{2,1,0:T(8,128)(2,1)S(1)}, bf16[3,64,256]{2,1,0:T(8,128)(2,1)S(1)}, u32[]{:S(2)}, u32[]{:S(2)}) collective-permute-start(bf16[3,64,256]{2,1,0:T(8,128)(2,1)S(1)} %get-tuple-element.25.zlo), channel_id=1, source_target_pairs={{128,0},{256,128},{384,256},{129,1},{257,129},{385,257},{130,2},{2... | collective-permute-start | bytes 294920 | tf_op jit(solution)/shard_map/ppermute | solution.py:286
  42.4 1.9 %collective-permute-start.4 = (bf16[3,64,256]{2,1,0:T(8,128)(2,1)S(1)}, bf16[3,64,256]{2,1,0:T(8,128)(2,1)S(1)}, u32[]{:S(2)}, u32[]{:S(2)}) collective-permute-start(bf16[3,64,256]{2,1,0:T(8,128)(2,1)S(1)} %get-tuple-element.28.yhi), channel_id=1, source_target_pairs={{0,8},{8,16},{16,24},{24,32},{32,40},{40,48},{48,56},{56,64},{64,7... | collective-permute-start | bytes 294920 | tf_op jit(solution)/shard_map/ppermute | solution.py:286
  44.3 0.0 collective-permute-done.2.rz0
  44.3 2.4 %collective-permute-start.5 = (bf16[3,64,256]{2,1,0:T(8,128)(2,1)S(1)}, bf16[3,64,256]{2,1,0:T(8,128)(2,1)S(1)}, u32[]{:S(2)}, u32[]{:S(2)}) collective-permute-start(bf16[3,64,256]{2,1,0:T(8,128)(2,1)S(1)} %get-tuple-element.27.ylo), channel_id=1, source_target_pairs={{8,0},{16,8},{24,16},{32,24},{40,32},{48,40},{56,48},{64,56},{72,6... | collective-permute-start | bytes 294920 | tf_op jit(solution)/shard_map/ppermute | solution.py:286
  46.7 1.3 %collective-permute-start.6 = (bf16[3,64,256]{2,1,0:T(8,128)(2,1)S(1)}, bf16[3,64,256]{2,1,0:T(8,128)(2,1)S(1)}, u32[]{:S(2)}, u32[]{:S(2)}) collective-permute-start(bf16[3,64,256]{2,1,0:T(8,128)(2,1)S(1)} %get-tuple-element.30.xhi), channel_id=1, source_target_pairs={{0,1},{1,2},{2,3},{3,4},{4,5},{5,6},{6,7},{8,9},{9,10},{10,11},{11... | collective-permute-start | bytes 294920 | tf_op jit(solution)/shard_map/ppermute | solution.py:286
  48.1 1.3 %collective-permute-start.7 = (bf16[3,64,256]{2,1,0:T(8,128)(2,1)S(1)}, bf16[3,64,256]{2,1,0:T(8,128)(2,1)S(1)}, u32[]{:S(2)}, u32[]{:S(2)}) collective-permute-start(bf16[3,64,256]{2,1,0:T(8,128)(2,1)S(1)} %get-tuple-element.29.xlo), channel_id=1, source_target_pairs={{1,0},{2,1},{3,2},{4,3},{5,4},{6,5},{7,6},{9,8},{10,9},{11,10},{12... | collective-permute-start | bytes 294920 | tf_op jit(solution)/shard_map/ppermute | solution.py:286
  49.4 0.9 collective-permute-done.5.ry1
  50.3 0.0 collective-permute-done.6.rx0
  50.3 4.2 %collective-permute-done.7.rx1 = bf16[3,64,256]{2,1,0:T(8,128)(2,1)S(1)} collective-permute-done((bf16[3,64,256]{2,1,0:T(8,128)(2,1)S(1)}, bf16[3,64,256]{2,1,0:T(8,128)(2,1)S(1)}, u32[]{:S(2)}, u32[]{:S(2)}) %collective-permute-start.7) | collective-permute-done | bytes 98336 | tf_op jit(solution)/shard_map/ppermute | solution.py:286
  54.5 2.3 %collective-permute-start.8 = (bf16[256,1920]{1,0:T(8,128)(2,1)S(1)}, bf16[256,1920]{1,0:T(8,128)(2,1)S(1)}, u32[]{:S(2)}, u32[]{:S(2)}) collective-permute-start(bf16[256,1920]{1,0:T(8,128)(2,1)S(1)} %collective-permute-done.xw_ref), channel_id=1, source_target_pairs={{0,8},{8,0},{16,24},{24,16},{32,40},{40,32},{48,56},{56,48},{64,72... | collective-permute-start | bytes 2949128 | tf_op jit(solution)/shard_map/ppermute | solution.py:297
  56.8 2.0 %collective-permute-start.9 = (bf16[256,1024]{1,0:T(8,128)(2,1)S(1)}, bf16[256,1024]{1,0:T(8,128)(2,1)S(1)}, u32[]{:S(2)}, u32[]{:S(2)}) collective-permute-start(bf16[256,1024]{1,0:T(8,128)(2,1)S(1)} %collective-permute-done.1.zw_ref), channel_id=1, source_target_pairs={{0,8},{8,0},{16,24},{24,16},{32,40},{40,32},{48,56},{56,48},{64,72... | collective-permute-start | bytes 1572872 | tf_op jit(solution)/shard_map/ppermute | solution.py:298
  58.8 1.8 %shard_map.66.cols_ref = bf16[10,3,10,64,256]{4,3,2,1,0:T(8,128)(2,1)S(1)} custom-call(s32[1,1,1,3,6]{4,3,2,1,0:T(4,128)S(1)} %copy.11.near_ref, bf16[3,8,64,256]{3,2,1,0:T(8,128)(2,1)S(1)} %get-tuple-element.24.fi_ref, bf16[3,64,256]{2,1,0:T(8,128)(2,1)S(1)} %get-tuple-element.25.zlo, bf16[3,64,256]{2,1,0:T(8,128)(2,1)S(1)} %get-tuple-element.26.zhi, ...), custom_call_target="tpu_custom_call" | custom-call | flops 16777216 | bytes 6291456 | tf_op jit(solution)/shard_map/pallas_call | solution.py:300
  60.6 1.6 %shard_map.67.old_ref = f32[3,512,256]{2,1,0:T(8,128)S(1)} custom-call(bf16[10,3,10,64,256]{4,3,2,1,0:T(8,128)(2,1)S(1)} %shard_map.66.cols_ref, bf16[256,1920]{1,0:T(8,128)(2,1)S(1)} %all_gather.3.own_ref), custom_call_target="tpu_custom_call" | custom-call | flops 1468006400 | bytes 3145728 | tf_op jit(solution)/shard_map/pallas_call | solution.py:317
  62.2 0.0 copy-start.3
  62.2 2.5 %shard_map.68.old_ref = f32[3,512,256]{2,1,0:T(8,128)S(1)} custom-call(bf16[10,3,10,64,256]{4,3,2,1,0:T(8,128)(2,1)S(1)} %shard_map.66.cols_ref, bf16[256,1920]{1,0:T(8,128)(2,1)S(1)} %collective-permute-done.xw_ref, bf16[256,1024]{1,0:T(8,128)(2,1)S(1)} %collective-permute-done.1.zw_ref, f32[3,512,256]{2,1,0:T(8,128)S(1)} %shard_map.67.old_ref), custom_call_target="tpu_custom_call" | custom-call | flops 2306867200 | bytes 3145728 | tf_op jit(solution)/shard_map/pallas_call | solution.py:325
  64.7 6.0 %shard_map.69 = bf16[32,64,256]{2,1,0:T(8,128)(2,1)} custom-call(s32[1,1,1,3,8]{4,3,2,1,0:T(4,128)S(1)} %copy.10.owners_ref, bf16[10,3,10,64,256]{4,3,2,1,0:T(8,128)(2,1)S(1)} %shard_map.66.cols_ref, bf16[256,1920]{1,0:T(8,128)(2,1)S(1)} %collective-permute-done.8.xw_ref, bf16[256,1024]{1,0:T(8,128)(2,1)S(1)} %collective-permute-done.9.zw_ref, ...), custom_call_target="tpu_custom_call" | custom-call | flops 2097152000 | bytes 3145728 | tf_op jit(solution)/shard_map/pallas_call | solution.py:333
  70.7 5.6 %all-to-all-start = ((bf16[16,128,256]{2,1,0:T(8,128)(2,1)}), bf16[16,128,256]{2,1,0:T(8,128)(2,1)S(1)}, u32[]{:S(2)}, u32[]{:S(2)}) async-start(bf16[16,128,256]{2,1,0:T(8,128)(2,1)} %bitcast.3), calls=%async_computation | async-start | bytes 2097152 | tf_op jit(solution)/shard_map/all_to_all | solution.py:342
  76.4 0.4 and_reduce_fusion
  76.8 0.1 add_select_fusion
  76.9 0.4 select_reduce_fusion.source_ref
  77.2 27.0 %all-to-all-done = bf16[16,128,256]{2,1,0:T(8,128)(2,1)S(1)} async-done(((bf16[16,128,256]{2,1,0:T(8,128)(2,1)}), bf16[16,128,256]{2,1,0:T(8,128)(2,1)S(1)}, u32[]{:S(2)}, u32[]{:S(2)}) %all-to-all-start) | async-done | bytes 1048608 | tf_op jit(solution)/shard_map/all_to_all | solution.py:342
  104.3 3.3 %shard_map.70 = bf16[16,4,2,4,2,8,128]{6,5,4,3,2,1,0:T(8,128)(2,1)} custom-call(s32[16]{0:T(128)S(1)} %select_reduce_fusion.source_ref, bf16[32,64,256]{2,1,0:T(8,128)(2,1)S(1)} %bitcast.6, bf16[8,256,128]{2,1,0:T(8,128)(2,1)S(1)} %copy-done.1), custom_call_target="tpu_custom_call" | custom-call | flops 566231040 | bytes 4194304 | tf_op jit(solution)/shard_map/pallas_call | solution.py:359
  (18 shorter events, 0.1 us)
Async XLA Ops:
  0.0 39.1 %copy-start = (bf16[1,1,1,3,8,8,8,256]{7,6,5,4,3,2,1,0:T(8,128)(2,1)S(1)}, bf16[1,1,1,3,8,8,8,256]{7,6,5,4,3,2,1,0:T(8,128)(2,1)}, u32[]{:S(2)}) copy-start(bf16[1,1,1,3,8,8,8,256]{7,6,5,4,3,2,1,0:T(8,128)(2,1)} %param.6) | copy-start | bytes 2359300
  0.8 0.9 copy-start.2
  2.3 56.5 %copy-start.4 = (s32[1,1,1,3,6]{4,2,3,1,0:T(1,128)S(1)}, s32[1,1,1,3,6]{4,2,3,1,0:T(1,128)}, u32[]{:S(2)}) copy-start(s32[1,1,1,3,6]{4,2,3,1,0:T(1,128)} %param.7) | copy-start | bytes 220
  26.6 27.9 %collective-permute-start = (bf16[256,1920]{1,0:T(8,128)(2,1)S(1)}, bf16[256,1920]{1,0:T(8,128)(2,1)S(1)}, u32[]{:S(2)}, u32[]{:S(2)}) collective-permute-start(bf16[256,1920]{1,0:T(8,128)(2,1)S(1)} %all_gather.3.own_ref), channel_id=1, source_target_pairs={{0,128},{8,392},{16,144},{24,408},{32,160},{40,424},{48,176},{56,4... | collective-permute-start | bytes 2949128 | tf_op jit(solution)/shard_map/ppermute | solution.py:269
  28.6 25.9 %collective-permute-start.1 = (bf16[256,1024]{1,0:T(8,128)(2,1)S(1)}, bf16[256,1024]{1,0:T(8,128)(2,1)S(1)}, u32[]{:S(2)}, u32[]{:S(2)}) collective-permute-start(bf16[256,1024]{1,0:T(8,128)(2,1)S(1)} %constant_dynamic-slice_fusion), channel_id=1, source_target_pairs={{0,1},{1,2},{2,3},{3,4},{4,5},{5,6},{6,7},{7,0},{8,15},{9,8},{10,9... | collective-permute-start | bytes 1572872 | tf_op jit(solution)/shard_map/ppermute | solution.py:270
  39.8 4.5 %collective-permute-start.2 = (bf16[3,64,256]{2,1,0:T(8,128)(2,1)S(1)}, bf16[3,64,256]{2,1,0:T(8,128)(2,1)S(1)}, u32[]{:S(2)}, u32[]{:S(2)}) collective-permute-start(bf16[3,64,256]{2,1,0:T(8,128)(2,1)S(1)} %get-tuple-element.26.zhi), channel_id=1, source_target_pairs={{0,128},{128,256},{256,384},{1,129},{129,257},{257,385},{2,130},{1... | collective-permute-start | bytes 294920 | tf_op jit(solution)/shard_map/ppermute | solution.py:286
  41.1 5.7 %collective-permute-start.3 = (bf16[3,64,256]{2,1,0:T(8,128)(2,1)S(1)}, bf16[3,64,256]{2,1,0:T(8,128)(2,1)S(1)}, u32[]{:S(2)}, u32[]{:S(2)}) collective-permute-start(bf16[3,64,256]{2,1,0:T(8,128)(2,1)S(1)} %get-tuple-element.25.zlo), channel_id=1, source_target_pairs={{128,0},{256,128},{384,256},{129,1},{257,129},{385,257},{130,2},{2... | collective-permute-start | bytes 294920 | tf_op jit(solution)/shard_map/ppermute | solution.py:286
  42.4 5.7 %collective-permute-start.4 = (bf16[3,64,256]{2,1,0:T(8,128)(2,1)S(1)}, bf16[3,64,256]{2,1,0:T(8,128)(2,1)S(1)}, u32[]{:S(2)}, u32[]{:S(2)}) collective-permute-start(bf16[3,64,256]{2,1,0:T(8,128)(2,1)S(1)} %get-tuple-element.28.yhi), channel_id=1, source_target_pairs={{0,8},{8,16},{16,24},{24,32},{32,40},{40,48},{48,56},{56,64},{64,7... | collective-permute-start | bytes 294920 | tf_op jit(solution)/shard_map/ppermute | solution.py:286
  44.3 5.9 %collective-permute-start.5 = (bf16[3,64,256]{2,1,0:T(8,128)(2,1)S(1)}, bf16[3,64,256]{2,1,0:T(8,128)(2,1)S(1)}, u32[]{:S(2)}, u32[]{:S(2)}) collective-permute-start(bf16[3,64,256]{2,1,0:T(8,128)(2,1)S(1)} %get-tuple-element.27.ylo), channel_id=1, source_target_pairs={{8,0},{16,8},{24,16},{32,24},{40,32},{48,40},{56,48},{64,56},{72,6... | collective-permute-start | bytes 294920 | tf_op jit(solution)/shard_map/ppermute | solution.py:286
  46.7 3.5 %collective-permute-start.6 = (bf16[3,64,256]{2,1,0:T(8,128)(2,1)S(1)}, bf16[3,64,256]{2,1,0:T(8,128)(2,1)S(1)}, u32[]{:S(2)}, u32[]{:S(2)}) collective-permute-start(bf16[3,64,256]{2,1,0:T(8,128)(2,1)S(1)} %get-tuple-element.30.xhi), channel_id=1, source_target_pairs={{0,1},{1,2},{2,3},{3,4},{4,5},{5,6},{6,7},{8,9},{9,10},{10,11},{11... | collective-permute-start | bytes 294920 | tf_op jit(solution)/shard_map/ppermute | solution.py:286
  48.1 6.4 %collective-permute-start.7 = (bf16[3,64,256]{2,1,0:T(8,128)(2,1)S(1)}, bf16[3,64,256]{2,1,0:T(8,128)(2,1)S(1)}, u32[]{:S(2)}, u32[]{:S(2)}) collective-permute-start(bf16[3,64,256]{2,1,0:T(8,128)(2,1)S(1)} %get-tuple-element.29.xlo), channel_id=1, source_target_pairs={{1,0},{2,1},{3,2},{4,3},{5,4},{6,5},{7,6},{9,8},{10,9},{11,10},{12... | collective-permute-start | bytes 294920 | tf_op jit(solution)/shard_map/ppermute | solution.py:286
  54.5 10.3 %collective-permute-start.8 = (bf16[256,1920]{1,0:T(8,128)(2,1)S(1)}, bf16[256,1920]{1,0:T(8,128)(2,1)S(1)}, u32[]{:S(2)}, u32[]{:S(2)}) collective-permute-start(bf16[256,1920]{1,0:T(8,128)(2,1)S(1)} %collective-permute-done.xw_ref), channel_id=1, source_target_pairs={{0,8},{8,0},{16,24},{24,16},{32,40},{40,32},{48,56},{56,48},{64,72... | collective-permute-start | bytes 2949128 | tf_op jit(solution)/shard_map/ppermute | solution.py:297
  56.8 8.0 %collective-permute-start.9 = (bf16[256,1024]{1,0:T(8,128)(2,1)S(1)}, bf16[256,1024]{1,0:T(8,128)(2,1)S(1)}, u32[]{:S(2)}, u32[]{:S(2)}) collective-permute-start(bf16[256,1024]{1,0:T(8,128)(2,1)S(1)} %collective-permute-done.1.zw_ref), channel_id=1, source_target_pairs={{0,8},{8,0},{16,24},{24,16},{32,40},{40,32},{48,56},{56,48},{64,72... | collective-permute-start | bytes 1572872 | tf_op jit(solution)/shard_map/ppermute | solution.py:298
  62.2 2.5 %copy-start.3 = (f32[256]{0:T(256)S(1)}, f32[256]{0:T(256)}, u32[]{:S(2)}) copy-start(f32[256]{0:T(256)} %param.10) | copy-start | bytes 3076
  70.7 33.5 %copy-start.1 = (bf16[8,256,128]{2,1,0:T(8,128)(2,1)S(1)}, bf16[8,256,128]{2,1,0:T(8,128)(2,1)}, u32[]{:S(2)}) copy-start(bf16[8,256,128]{2,1,0:T(8,128)(2,1)} %up_ref.1) | copy-start | bytes 1572868
  70.7 33.5 %all-to-all-start = ((bf16[16,128,256]{2,1,0:T(8,128)(2,1)}), bf16[16,128,256]{2,1,0:T(8,128)(2,1)S(1)}, u32[]{:S(2)}, u32[]{:S(2)}) async-start(bf16[16,128,256]{2,1,0:T(8,128)(2,1)} %bitcast.3), calls=%async_computation | async-start | bytes 2097152 | tf_op jit(solution)/shard_map/all_to_all | solution.py:342

commit v3 on v2

--- a/solution.py
+++ b/solution.py
@@ -15,7 +15,7 @@
     return [pl.BlockSpec(memory_space=VMEM)] * count
 
 
-def norm_kernel(lat_ref, fi_ref, zlo_ref, zhi_ref, ylo_ref, yhi_ref, xlo_ref, xhi_ref, rows_ref):
+def norm_kernel(lat_ref, fi_ref, faces_ref, give_ref, cross_ref, keep_ref, rows_ref):
     slots, edge, plane, _ = lat_ref.shape
     lanes = rows_ref.shape[-1]
     pieces = rows_ref.shape[0]
@@ -28,21 +28,43 @@
             half = s.astype(jnp.bfloat16)
             fi_ref[b, z] = half
             if z == 0:
-                zlo_ref[b] = half
+                faces_ref[1, b] = half
             if z == edge - 1:
-                zhi_ref[b] = half
+                faces_ref[0, b] = half
             for p in range(pieces):
                 rows_ref[p, pl.ds(z * plane, plane), :] = s[:, p * lanes : (p + 1) * lanes]
         for p in range(pieces):
             cols = pl.ds(p * lanes, lanes)
-            xlo_ref[b, :, cols] = rows_ref[p, pl.ds(0, plane, stride=edge), :].astype(jnp.bfloat16)
-            xhi_ref[b, :, cols] = rows_ref[p, pl.ds(edge - 1, plane, stride=edge), :].astype(
-                jnp.bfloat16
-            )
+            low = rows_ref[p, pl.ds(0, plane, stride=edge), :]
+            high = rows_ref[p, pl.ds(edge - 1, plane, stride=edge), :]
+            faces_ref[5, b, :, cols] = low.astype(jnp.bfloat16)
+            faces_ref[4, b, :, cols] = high.astype(jnp.bfloat16)
             low = [rows_ref[p, pl.ds(z * plane, edge), :] for z in range(edge)]
-            ylo_ref[b, :, cols] = jnp.concatenate(low, axis=0).astype(jnp.bfloat16)
+            faces_ref[3, b, :, cols] = jnp.concatenate(low, axis=0).astype(jnp.bfloat16)
             high = [rows_ref[p, pl.ds(z * plane + plane - edge, edge), :] for z in range(edge)]
-            yhi_ref[b, :, cols] = jnp.concatenate(high, axis=0).astype(jnp.bfloat16)
+            faces_ref[2, b, :, cols] = jnp.concatenate(high, axis=0).astype(jnp.bfloat16)
+    core = core_here()
+    for kind in range(2):
+        keep_ref[kind] = faces_ref[4 * kind + core]
+        give_ref[kind] = faces_ref[4 * kind + 1 - core]
+    give_ref[2] = faces_ref[2 + core]
+    cross_ref[...] = faces_ref[3 - core]
+
+
+def pack_kernel(own_ref, keep_ref, met_ref, x_ref, z_ref):
+    chan = keep_ref.shape[-1]
+    face = keep_ref.shape[1] * keep_ref.shape[2]
+    wide = x_ref.shape[1] - 2 * chan
+    part = z_ref.shape[1] - 2 * chan
+    x_ref[:, :wide] = own_ref[:, :wide]
+    start = core_here() * ((wide - part) // chan) * chan
+    z_ref[:, :part] = own_ref[:, pl.ds(pl.multiple_of(start, chan), part)]
+    for kind, out_ref in ((0, x_ref), (1, z_ref)):
+        left = out_ref.shape[1] - 2 * chan
+        rest = out_ref.shape[0] - face
+        out_ref[:face, left : left + chan] = keep_ref[kind].reshape(face, chan)
+        out_ref[:face, left + chan :] = met_ref[kind].reshape(face, chan)
+        out_ref[face:, left:] = jnp.zeros((rest, 2 * chan), jnp.bfloat16)
 
 
 def quarter_kernel(owners_ref, weight_ref, out_ref):
@@ -61,15 +83,25 @@
 
 
 def columns_kernel(
-    near_ref, fi_ref, zlo, zhi, ylo, yhi, xlo, xhi, rz0, rz1, ry0, ry1, rx0, rx1, out_ref, table_ref, ybuf_ref, xbuf_ref
+    near_ref, fi_ref, faces_ref, met_ref, crossed_ref, x_ref, z_ref, xo_ref, zo_ref, out_ref, table_ref, ybuf_ref, xbuf_ref
 ):
     slots, edge, plane, chan = fi_ref.shape
-    near = (zhi, zlo, yhi, ylo, xhi, xlo)
-    far = (rz0, rz1, ry0, ry1, rx0, rx1)
+    core = core_here()
+
+    def ridden(ref, which):
+        left = ref.shape[1] - (2 - which) * chan
+        return ref[: slots * plane, left : left + chan].reshape(slots, plane, chan)
+
+    far = pl.ds(slots, slots)
     for d in range(6):
-        table_ref[d, 0:slots] = near[d][...]
-        table_ref[d, slots : 2 * slots] = far[d][...]
+        table_ref[d, 0:slots] = faces_ref[d]
         table_ref[d, 2 * slots] = jnp.zeros((plane, chan), jnp.bfloat16)
+    table_ref[core, far] = ridden(x_ref, 0)
+    table_ref[1 - core, far] = ridden(xo_ref, 1)
+    table_ref[2 + core, far] = crossed_ref[...]
+    table_ref[3 - core, far] = met_ref[2]
+    table_ref[4 + core, far] = ridden(z_ref, 0)
+    table_ref[5 - core, far] = ridden(zo_ref, 1)
     out_ref[9] = jnp.zeros(out_ref.shape[1:], jnp.bfloat16)
     at_x = lax.rem(lax.broadcasted_iota(jnp.int32, (plane + 2 * edge, chan), 0), edge)
     rows_n = lax.axis_size("row")
@@ -100,10 +132,9 @@
             jnp.where(at_x == edge - 1, spread(right), pltpu.roll(rows, count - 1, 0)),
         )
         for dx in range(3):
+            low, high = paired(moved[dx])
             for dy in range(3):
-                out_ref[dy * 3 + dx, b, z] = moved[dx][dy * edge : dy * edge + plane].astype(
-                    jnp.bfloat16
-                )
+                out_ref[dy * 3 + dx, b, z] = octant_rows(low, high, dy).astype(jnp.bfloat16)
 
     def brick(b, _):
         zero = jnp.zeros((edge, chan), jnp.float32)
@@ -125,6 +156,30 @@
         return 0
 
     lax.fori_loop(0, slots, brick, 0)
+
+
+def paired(rows):
+    edge = 8
+    half = edge // 2
+    lines = rows.shape[0] // edge
+    in_low = lax.rem(lax.broadcasted_iota(jnp.int32, ((lines - 1) * edge, rows.shape[1]), 0), edge) < half
+    turned = pltpu.roll(rows.reshape(lines, edge, -1), half, 1).reshape(rows.shape)
+    first, second = slice(0, (lines - 1) * edge), slice(edge, lines * edge)
+    low = jnp.where(in_low, rows[first], turned[second])
+    high = jnp.where(in_low, turned[first], rows[second])
+    return low, high
+
+
+def octant_rows(low, high, start):
+    edge = 8
+    half = edge // 2
+    out = []
+    for ky in range(2):
+        for side in (low, high):
+            for y in range(0, half, 2):
+                at = (ky * half + y + start) * edge
+                out.append(side[at : at + edge])
+    return jnp.concatenate(out, axis=0)
 
 
 def colour_here():
@@ -153,30 +208,37 @@
     )
 
 
-def own_kernel(cols_ref, own_ref, acc_ref):
-    chan = cols_ref.shape[4]
+def own_kernel(cols_ref, own_ref, lat_ref, emb_ref, acc_ref):
+    slots, edge, plane, chan = lat_ref.shape
     count = own_ref.shape[1] // chan
     first = colour_here() * count
-    for b in range(acc_ref.shape[0]):
-        acc_ref[b] = times(tap_rows(cols_ref, b, first, count), own_ref[:, : count * chan])
+    for b in range(slots):
+        got = times(tap_rows(cols_ref, b, first, count), own_ref[:, : count * chan])
+        acc_ref[b] = got + emb_ref[...]
+        for z in range(edge):
+            lat = lat_ref[b, z].astype(jnp.float32)
+            low, high = paired(lat)
+            acc_ref[b, z * plane : (z + 1) * plane] += octant_rows(low, high, 0)
 
 
 def side_kernel(cols_ref, xw_ref, zw_ref, old_ref, acc_ref):
     chan = cols_ref.shape[4]
-    count, part = xw_ref.shape[1] // chan, zw_ref.shape[1] // chan
+    count, part = xw_ref.shape[1] // chan - 2, zw_ref.shape[1] // chan - 2
     core, colour = core_here(), colour_here()
     x_first = lax.rem(colour + 3 + 2 * core, 4) * count
     z_first = lax.rem(colour + 2, 4) * count + core * (count - part)
     for b in range(acc_ref.shape[0]):
         got = times(tap_rows(cols_ref, b, x_first, count), xw_ref[:, : count * chan])
-        got += times(tap_rows(cols_ref, b, z_first, part), zw_ref[...])
+        got += times(tap_rows(cols_ref, b, z_first, part), zw_ref[:, : part * chan])
         acc_ref[b] = old_ref[b] + got
 
 
-def last_kernel(owners_ref, cols_ref, xw_ref, zw_ref, lat_ref, emb_ref, old_ref, out_ref):
-    slots, edge, plane, chan = lat_ref.shape
+def last_kernel(owners_ref, cols_ref, xw_ref, zw_ref, old_ref, out_ref, stash_ref, sem):
+    slots = old_ref.shape[0]
+    edge, plane, chan = cols_ref.shape[2] - 2, cols_ref.shape[3], cols_ref.shape[4]
     half = edge // 2
-    count, part = xw_ref.shape[1] // chan, zw_ref.shape[1] // chan
+    piece = half * half
+    count, part = xw_ref.shape[1] // chan - 2, zw_ref.shape[1] // chan - 2
     rest = count - part
     core, colour = core_here(), colour_here()
     x_first = lax.rem(colour + 1 + 2 * core, 4) * count
@@ -185,33 +247,23 @@
 
     targets = [owners_ref[0, 0, 0, i // 8, i % 8] for i in range(slots * 8)]
     target_rows = [lax.shift_right_arithmetic(t, 4) for t in targets]
-    in_low = lax.broadcasted_iota(jnp.int32, (half * half // 2, edge, chan), 1) < half
+    spare = out_ref.shape[0]
     for b in range(slots):
         got = times(tap_rows(cols_ref, b, x_first, count), xw_ref[:, : count * chan])
         got += times(tap_rows(cols_ref, b, z_first, rest), zw_ref[:, lanes])
-        total = old_ref[b] + got
-        lat = lat_ref[b].astype(jnp.float32).reshape(edge * plane, chan)
-        refined = lat + (total + emb_ref[...])
-        pairs = refined.reshape(2, half, 2, half // 2, 2, edge, chan)
-        for kz in range(2):
-            for ky in range(2):
-                first = pairs[kz, :, ky, :, 0].reshape(-1, edge, chan)
-                second = pairs[kz, :, ky, :, 1].reshape(-1, edge, chan)
-                child = (
-                    jnp.where(in_low, first, pltpu.roll(second, half, 1)),
-                    jnp.where(in_low, pltpu.roll(first, half, 1), second),
-                )
-                for kx in range(2):
-                    k = b * 8 + kz * 4 + ky * 2 + kx
-                    value = child[kx].reshape(half**3, chan).astype(jnp.bfloat16)
-                    rank = 0
-                    for j in range(k):
-                        rank += (target_rows[j] == target_rows[k]).astype(jnp.int32)
-                    place = target_rows[k] * 2 + rank
-
-                    @pl.when(targets[k] >= 0)
-                    def _():
-                        out_ref[place] = value
+        refined = (old_ref[b] + got).astype(jnp.bfloat16)
+        for k in range(8):
+            i = b * 8 + k
+            rank = 0
+            for j in range(i):
+                rank += (target_rows[j] == target_rows[i]).astype(jnp.int32)
+            place = jnp.where(targets[i] >= 0, target_rows[i] * 2 + rank, spare)
+            for z in range(half):
+                at = ((k // 4) * half + z) * plane + (k % 4) * piece
+                stash_ref[place, z * piece : (z + 1) * piece] = refined[at : at + piece]
+    copy = pltpu.make_async_copy(stash_ref.at[pl.ds(0, spare)], out_ref, sem)
+    copy.start()
+    copy.wait()
 
 
 def grow_kernel(source_ref, child_ref, up_ref, out_ref, rows_ref):
@@ -242,7 +294,6 @@
     co = up_weight.shape[-1]
     quarter = (taps + 1) // 4
     part = quarter // 2 + 1
-    core = core_here()
 
     smem = pl.BlockSpec(memory_space=SMEM)
     piece = pl.pallas_call(
@@ -252,7 +303,39 @@
         out_specs=pl.BlockSpec(memory_space=VMEM),
         compiler_params=pltpu.CompilerParams(vmem_limit_bytes=4 * MB),
     )(owners, conv_weight.transpose(0, 2, 1))
+    lat = latents.reshape(slots, edge, plane, chan)
+    def bf16(*shape):
+        return jax.ShapeDtypeStruct(shape, jnp.bfloat16)
+
+    fi, faces, give, cross, keep = pl.pallas_call(
+        norm_kernel,
+        out_shape=[
+            bf16(*lat.shape),
+            bf16(6, slots, plane, chan),
+            bf16(3, slots, plane, chan),
+            bf16(slots, plane, chan),
+            bf16(2, slots, plane, chan),
+        ],
+        in_specs=whole(1),
+        out_specs=whole(5),
+        scratch_shapes=[pltpu.VMEM((chan // 128, edge * plane, 128), jnp.float32)],
+        compiler_params=pltpu.CompilerParams(vmem_limit_bytes=6 * MB),
+        cost_estimate=pl.CostEstimate(flops=4 * MB, bytes_accessed=2 * MB, transcendentals=MB),
+    )(lat)
+    swap = [(r, r ^ 1) for r in range(rows_n)]
+    between = [(r, r + 1 - 2 * (1 - r % 2)) for r in range(1, rows_n - 1)]
+    met = lax.ppermute(give, "row", swap)
+    crossed = lax.ppermute(cross, "row", between)
+    piece, met = lax.optimization_barrier((piece, met))
     own_w = lax.all_gather(piece, "row", axis=0, tiled=True)
+    x_send, z_send = pl.pallas_call(
+        pack_kernel,
+        out_shape=[bf16(chan, (quarter + 2) * chan), bf16(chan, (part + 2) * chan)],
+        in_specs=whole(3),
+        out_specs=whole(2),
+        compiler_params=pltpu.CompilerParams(vmem_limit_bytes=4 * MB),
+        cost_estimate=pl.CostEstimate(flops=0, bytes_accessed=4 * MB, transcendentals=0),
+    )(own_w, keep, met)
     depth_n = lax.axis_size("depth")
     x_pairs = [
         (d * rows_n + r, (d + 1 - 2 * (r % 2)) % depth_n * rows_n + r)
@@ -264,43 +347,15 @@
         for r in range(rows_n)
         for c in range(cols_n)
     ]
-    swap = [(r, r ^ 1) for r in range(rows_n)]
-    z_send = lax.dynamic_slice(own_w, (0, core * (quarter - part) * chan), (chan, part * chan))
-    x_got = lax.ppermute(own_w, ("depth", "row"), x_pairs)
+    x_got = lax.ppermute(x_send, ("depth", "row"), x_pairs)
     z_got = lax.ppermute(z_send, ("row", "col"), z_pairs)
-    lat, own_w = lax.optimization_barrier((latents.reshape(slots, edge, plane, chan), own_w))
-    face = jax.ShapeDtypeStruct((slots, plane, chan), jnp.bfloat16)
-    fi, zlo, zhi, ylo, yhi, xlo, xhi = pl.pallas_call(
-        norm_kernel,
-        out_shape=[jax.ShapeDtypeStruct(lat.shape, jnp.bfloat16)] + [face] * 6,
-        in_specs=whole(1),
-        out_specs=whole(7),
-        scratch_shapes=[pltpu.VMEM((chan // 128, edge * plane, 128), jnp.float32)],
-        compiler_params=pltpu.CompilerParams(vmem_limit_bytes=6 * MB),
-        cost_estimate=pl.CostEstimate(flops=4 * MB, bytes_accessed=2 * MB, transcendentals=MB),
-    )(lat)
-
-    def shift(face, axis, step):
-        count = lax.axis_size(axis)
-        pairs = [(i, i + step) for i in range(count) if 0 <= i + step < count]
-        return lax.ppermute(face, axis, pairs)
-
-    far = (
-        shift(zhi, "depth", 1),
-        shift(zlo, "depth", -1),
-        shift(yhi, "row", 1),
-        shift(ylo, "row", -1),
-        shift(xhi, "col", 1),
-        shift(xlo, "col", -1),
-    )
-    x_got, z_got, far = lax.optimization_barrier((x_got, z_got, far))
     x_other = lax.ppermute(x_got, "row", swap)
     z_other = lax.ppermute(z_got, "row", swap)
 
     columns = pl.pallas_call(
         columns_kernel,
         out_shape=jax.ShapeDtypeStruct((10, slots, edge + 2, plane, chan), jnp.bfloat16),
-        in_specs=[smem] + whole(13),
+        in_specs=[smem] + whole(8),
         out_specs=pl.BlockSpec(memory_space=VMEM),
         scratch_shapes=[
             pltpu.VMEM((6, 2 * slots + 1, plane, chan), jnp.bfloat16),
@@ -309,7 +364,7 @@
         ],
         compiler_params=pltpu.CompilerParams(vmem_limit_bytes=8 * MB),
         cost_estimate=pl.CostEstimate(flops=16 * MB, bytes_accessed=6 * MB, transcendentals=0),
-    )(neighbours, fi, zlo, zhi, ylo, yhi, xlo, xhi, *far)
+    )(neighbours, fi, faces, met, crossed, x_got, z_got, x_other, z_other)
 
     send_cap = 2
     acc_shape = jax.ShapeDtypeStruct((slots, edge * plane, chan), jnp.float32)
@@ -317,11 +372,11 @@
     acc = pl.pallas_call(
         own_kernel,
         out_shape=acc_shape,
-        in_specs=whole(2),
+        in_specs=whole(4),
         out_specs=pl.BlockSpec(memory_space=VMEM),
         compiler_params=params,
         cost_estimate=pl.CostEstimate(flops=1400 * MB, bytes_accessed=3 * MB, transcendentals=0),
-    )(columns, own_w)
+    )(columns, own_w, lat, step_embed.reshape(1, chan))
     acc = pl.pallas_call(
         side_kernel,
         out_shape=acc_shape,
@@ -333,11 +388,15 @@
     outgoing = pl.pallas_call(
         last_kernel,
         out_shape=jax.ShapeDtypeStruct((rows_n * send_cap, plane, chan), jnp.bfloat16),
-        in_specs=[smem] + whole(6),
-        out_specs=pl.BlockSpec(memory_space=VMEM),
+        in_specs=[smem] + whole(4),
+        out_specs=pl.BlockSpec(memory_space=pl.ANY),
+        scratch_shapes=[
+            pltpu.VMEM((rows_n * send_cap + 1, plane, chan), jnp.bfloat16),
+            pltpu.SemaphoreType.DMA,
+        ],
         compiler_params=params,
         cost_estimate=pl.CostEstimate(flops=2000 * MB, bytes_accessed=3 * MB, transcendentals=0),
-    )(owners, columns, x_other, z_other, lat, step_embed.reshape(1, chan), acc)
+    )(owners, columns, x_other, z_other, acc)
 
     arrived = lax.all_to_all(
         outgoing.reshape(rows_n, send_cap * plane, chan), "row", split_axis=0, concat_axis=0, tiled=True

time: 109 us -> 108 us (level)
  blocking collectives: 24.3 us -> 17.5 us
  starting transfers between devices: 31.8 us -> 36.6 us
  waiting for transfers between devices: 32.1 us -> 35.3 us
    all_gather x1, blocking collectives: 24.3 us -> 17.5 us  [body(): own_w = lax.all_gather(piece, 'row', axis=0, tiled=True)]
    ppermute x7 -> x3, waiting for transfers between devices: 5.1 us -> 8.09 us  [the longest x1 4.56 us: body(): x_got = lax.ppermute(x_send, ('depth', 'row'), x_pairs)]
    ppermute x7 -> x3, starting transfers between devices: 11.4 us -> 13.7 us  [the longest x1 8.79 us: body(): met = lax.ppermute(give, 'row', swap)]
    pallas_call x1, Pallas kernels: 5.99 us -> 3.96 us  [body(): pl.pallas_call(last_kernel, out_shape=jax.ShapeDtypeStruct((rows_n * send...]
    ppermute x1, starting transfers between devices: 2.29 us -> 4.12 us  [body(): x_other = lax.ppermute(x_got, 'row', swap)]
    pallas_call x2 -> x3, Pallas kernels: 2.33 us -> 2.57 us  [the longest x1 1.65 us: body(): pl.pallas_call(own_kernel, out_shape=acc_shape, in_specs=whole(4), out_sp...]
  transfers between devices with their start and end apart: 11 -> 7, of which waited for: 3 -> 5; matrix products, arithmetic and copies ran while one was open for 1% -> 1% of each run, Pallas kernels for 6% -> 1%
where the time goes in v3:
time: 108 us; the launch traced here: 107 us
  starting transfers between devices  36.6 us (34%)
  waiting for transfers between devices  35.3 us (33%)
  blocking collectives  17.5 us (16%)
  Pallas kernels  15.4 us (14%)
  local copies, waits for them, and re-layouts  1.22 us (1%)
    all_to_all x1, waiting for transfers between devices, body(): lax.all_to_all(outgoing.reshape(rows_n, send_cap * plane, chan), 'row', s...  27 us
    all_gather x1, blocking collectives, body(): own_w = lax.all_gather(piece, 'row', axis=0, tiled=True)  17.5 us
    ppermute x1, starting transfers between devices, body(): z_got = lax.ppermute(z_send, ('row', 'col'), z_pairs)  10.7 us
    ppermute x1, starting transfers between devices, body(): met = lax.ppermute(give, 'row', swap)  8.79 us
    all_to_all x1, starting transfers between devices, body(): lax.all_to_all(outgoing.reshape(rows_n, send_cap * plane, chan), 'row', s...  5.7 us
    ppermute x1, waiting for transfers between devices, body(): x_got = lax.ppermute(x_send, ('depth', 'row'), x_pairs)  4.56 us
    ppermute x1, starting transfers between devices, body(): x_other = lax.ppermute(x_got, 'row', swap)  4.12 us
    pallas_call x1, Pallas kernels, body(): pl.pallas_call(last_kernel, out_shape=jax.ShapeDtypeStruct((rows_n * send...  3.96 us
  transfers between devices with their start and end apart: 7, of which 5 were waited for; matrix products, arithmetic and copies ran while one was open for 1% of the time, Pallas kernels for 1%

profile of v3, /device:TPU:1, one launch (start us, length us, event | category | flops | bytes accessed | tf_op | source)
XLA Modules:
  0.0 107.2 jit_solution(2713815653317757691)
XLA Ops:
  0.0 1.1 %copy-done = bf16[1,1,1,3,8,8,8,256]{7,6,5,4,3,2,1,0:T(8,128)(2,1)S(1)} copy-done((bf16[1,1,1,3,8,8,8,256]{7,6,5,4,3,2,1,0:T(8,128)(2,1)S(1)}, bf16[1,1,1,3,8,8,8,256]{7,6,5,4,3,2,1,0:T(8,128)(2,1)}, u32[]{:S(2)}) %copy-start) | copy-done | bytes 786456
  1.2 0.8 shard_map.65
  1.9 0.0 copy-start.6
  2.0 8.8 %collective-permute-start = (bf16[3,3,64,256]{3,2,1,0:T(8,128)(2,1)S(1)}, bf16[3,3,64,256]{3,2,1,0:T(8,128)(2,1)S(1)}, u32[]{:S(2)}, u32[]{:S(2)}) collective-permute-start(bf16[3,3,64,256]{3,2,1,0:T(8,128)(2,1)S(1)} %get-tuple-element.14), channel_id=1, source_target_pairs={{0,8},{8,0},{16,24},{24,16},{32,40},{40,32},{48,56},{56,48},{64,72... | collective-permute-start | bytes 884744 | tf_op jit(solution)/shard_map/ppermute | solution.py:327
  10.8 0.0 copy-done.3
  10.8 0.6 shard_map.64
  11.4 0.6 collective-permute-done.met_ref
  12.0 17.5 %all_gather.3.own_ref = bf16[256,1920]{1,0:T(8,128)(2,1)S(1)} all-gather(bf16[16,1920]{1,0:T(8,128)(2,1)S(1)} %shard_map.64), channel_id=1, replica_groups=mesh['depth'=4,'row'=16,'col'=8] {'row'}, dimensions={0}, use_global_device_ids=true | all-gather | bytes 1044480 | tf_op jit(solution)/shard_map/all_gather | solution.py:330
  29.4 0.1 shard_map.66
  29.6 2.0 %collective-permute-start.2 = (bf16[256,2304]{1,0:T(8,128)(2,1)S(1)}, bf16[256,2304]{1,0:T(8,128)(2,1)S(1)}, u32[]{:S(2)}, u32[]{:S(2)}) collective-permute-start(bf16[256,2304]{1,0:T(8,128)(2,1)S(1)} %get-tuple-element.21), channel_id=1, source_target_pairs={{0,128},{8,392},{16,144},{24,408},{32,160},{40,424},{48,176},{56,4... | collective-permute-start | bytes 3538952 | tf_op jit(solution)/shard_map/ppermute | solution.py:350
  31.6 10.7 %collective-permute-start.3 = (bf16[256,1536]{1,0:T(8,128)(2,1)S(1)}, bf16[256,1536]{1,0:T(8,128)(2,1)S(1)}, u32[]{:S(2)}, u32[]{:S(2)}) collective-permute-start(bf16[256,1536]{1,0:T(8,128)(2,1)S(1)} %get-tuple-element.22), channel_id=1, source_target_pairs={{0,1},{1,2},{2,3},{3,4},{4,5},{5,6},{6,7},{7,0},{8,15},{9,8},{10,9... | collective-permute-start | bytes 2359304 | tf_op jit(solution)/shard_map/ppermute | solution.py:351
  42.3 4.6 %collective-permute-done.2.x_ref.xw_ref = bf16[256,2304]{1,0:T(8,128)(2,1)S(1)} collective-permute-done((bf16[256,2304]{1,0:T(8,128)(2,1)S(1)}, bf16[256,2304]{1,0:T(8,128)(2,1)S(1)}, u32[]{:S(2)}, u32[]{:S(2)}) %collective-permute-start.2) | collective-permute-done | bytes 1179680 | tf_op jit(solution)/shard_map/ppermute | solution.py:350
  46.8 4.1 %collective-permute-start.4 = (bf16[256,2304]{1,0:T(8,128)(2,1)S(1)}, bf16[256,2304]{1,0:T(8,128)(2,1)S(1)}, u32[]{:S(2)}, u32[]{:S(2)}) collective-permute-start(bf16[256,2304]{1,0:T(8,128)(2,1)S(1)} %collective-permute-done.2.x_ref.xw_ref), channel_id=1, source_target_pairs={{0,8},{8,0},{16,24},{24,16},{32,40},{40,32},{48,56},{56,48},{64,72... | collective-permute-start | bytes 3538952 | tf_op jit(solution)/shard_map/ppermute | solution.py:352
  50.9 0.2 collective-permute-done.3.z_ref.zw_ref
  51.2 2.4 %collective-permute-start.5 = (bf16[256,1536]{1,0:T(8,128)(2,1)S(1)}, bf16[256,1536]{1,0:T(8,128)(2,1)S(1)}, u32[]{:S(2)}, u32[]{:S(2)}) collective-permute-start(bf16[256,1536]{1,0:T(8,128)(2,1)S(1)} %collective-permute-done.3.z_ref.zw_ref), channel_id=1, source_target_pairs={{0,8},{8,0},{16,24},{24,16},{32,40},{40,32},{48,56},{56,48},{64,72... | collective-permute-start | bytes 2359304 | tf_op jit(solution)/shard_map/ppermute | solution.py:353
  53.6 2.9 %collective-permute-start.1 = (bf16[3,64,256]{2,1,0:T(8,128)(2,1)S(1)}, bf16[3,64,256]{2,1,0:T(8,128)(2,1)S(1)}, u32[]{:S(2)}, u32[]{:S(2)}) collective-permute-start(bf16[3,64,256]{2,1,0:T(8,128)(2,1)S(1)} %get-tuple-element.19), channel_id=1, source_target_pairs={{8,16},{16,8},{24,32},{32,24},{40,48},{48,40},{56,64},{64,56},{72,... | collective-permute-start | bytes 294920 | tf_op jit(solution)/shard_map/ppermute | solution.py:328
  56.5 0.0 copy-done.6
  56.5 3.0 %collective-permute-done.1.crossed_ref = bf16[3,64,256]{2,1,0:T(8,128)(2,1)S(1)} collective-permute-done((bf16[3,64,256]{2,1,0:T(8,128)(2,1)S(1)}, bf16[3,64,256]{2,1,0:T(8,128)(2,1)S(1)}, u32[]{:S(2)}, u32[]{:S(2)}) %collective-permute-start.1) | collective-permute-done | bytes 98336 | tf_op jit(solution)/shard_map/ppermute | solution.py:328
  59.5 0.0 collective-permute-done.5.zo_ref.zw_ref
  59.5 0.0 collective-permute-done.4.xo_ref.xw_ref
  59.5 0.0 copy-start.4
  59.5 2.6 %shard_map.67.cols_ref = bf16[10,3,10,64,256]{4,3,2,1,0:T(8,128)(2,1)S(1)} custom-call(s32[1,1,1,3,6]{4,3,2,1,0:T(4,128)S(1)} %copy.11.near_ref, bf16[3,8,64,256]{3,2,1,0:T(8,128)(2,1)S(1)} %get-tuple-element.16.fi_ref, bf16[6,3,64,256]{3,2,1,0:T(8,128)(2,1)S(1)} %get-tuple-element.17.faces_ref, bf16[3,3,64,256]{3,2,1,0:T(8,128)(2,1)S(1)} %collective-permute-done.met_ref, ...), custom_call_target="tpu_custom_call" | custom-call | flops 16777216 | bytes 6291456 | tf_op jit(solution)/shard_map/pallas_call | solution.py:355
  62.2 1.6 %shard_map.68.old_ref = f32[3,512,256]{2,1,0:T(8,128)S(1)} custom-call(bf16[10,3,10,64,256]{4,3,2,1,0:T(8,128)(2,1)S(1)} %shard_map.67.cols_ref, bf16[256,1920]{1,0:T(8,128)(2,1)S(1)} %all_gather.3.own_ref, bf16[3,8,64,256]{3,2,1,0:T(8,128)(2,1)S(1)} %bitcast.8, f32[1,256]{1,0:T(1,128)S(1)} %bitcast.10), custom_call_target="tpu_custom_call" | custom-call | flops 1468006400 | bytes 3145728 | tf_op jit(solution)/shard_map/pallas_call | solution.py:372
  63.8 2.4 %shard_map.69.old_ref = f32[3,512,256]{2,1,0:T(8,128)S(1)} custom-call(bf16[10,3,10,64,256]{4,3,2,1,0:T(8,128)(2,1)S(1)} %shard_map.67.cols_ref, bf16[256,2304]{1,0:T(8,128)(2,1)S(1)} %collective-permute-done.2.x_ref.xw_ref, bf16[256,1536]{1,0:T(8,128)(2,1)S(1)} %collective-permute-done.3.z_ref.zw_ref, f32[3,512,256]{2,1,0:T(8,128)S(1)} %shard_map.68.old_ref), custom_call_target="tpu_custom_call" | custom-call | flops 2306867200 | bytes 3145728 | tf_op jit(solution)/shard_map/pallas_call | solution.py:380
  66.3 4.0 %shard_map.70 = bf16[32,64,256]{2,1,0:T(8,128)(2,1)} custom-call(s32[1,1,1,3,8]{4,3,2,1,0:T(4,128)S(1)} %copy.10.owners_ref, bf16[10,3,10,64,256]{4,3,2,1,0:T(8,128)(2,1)S(1)} %shard_map.67.cols_ref, bf16[256,2304]{1,0:T(8,128)(2,1)S(1)} %collective-permute-done.4.xo_ref.xw_ref, bf16[256,1536]{1,0:T(8,128)(2,1)S(1)} %collective-permute-done.5.zo_ref.zw_ref, ...), custom_call_target="tpu_custom_call" | custom-call | flops 2097152000 | bytes 3145728 | tf_op jit(solution)/shard_map/pallas_call | solution.py:388
  70.2 0.0 copy-start.2
  70.3 5.7 %all-to-all-start = ((bf16[16,128,256]{2,1,0:T(8,128)(2,1)}), bf16[16,128,256]{2,1,0:T(8,128)(2,1)S(1)}, u32[]{:S(2)}, u32[]{:S(2)}) async-start(bf16[16,128,256]{2,1,0:T(8,128)(2,1)} %bitcast.3), calls=%async_computation | async-start | bytes 2097152 | tf_op jit(solution)/shard_map/all_to_all | solution.py:401
  76.0 0.4 and_reduce_fusion
  76.4 0.1 convert_add_fusion
  76.5 0.4 select_reduce_fusion.source_ref
  76.9 27.0 %all-to-all-done = bf16[16,128,256]{2,1,0:T(8,128)(2,1)S(1)} async-done(((bf16[16,128,256]{2,1,0:T(8,128)(2,1)}), bf16[16,128,256]{2,1,0:T(8,128)(2,1)S(1)}, u32[]{:S(2)}, u32[]{:S(2)}) %all-to-all-start) | async-done | bytes 1048608 | tf_op jit(solution)/shard_map/all_to_all | solution.py:401
  103.9 3.3 %shard_map.71 = bf16[16,4,2,4,2,8,128]{6,5,4,3,2,1,0:T(8,128)(2,1)} custom-call(s32[16]{0:T(128)S(1)} %select_reduce_fusion.source_ref, bf16[32,64,256]{2,1,0:T(8,128)(2,1)S(1)} %bitcast.6, bf16[8,256,128]{2,1,0:T(8,128)(2,1)S(1)} %copy-done.2), custom_call_target="tpu_custom_call" | custom-call | flops 566231040 | bytes 4194304 | tf_op jit(solution)/shard_map/pallas_call | solution.py:418
  (15 shorter events, 0.1 us)
Async XLA Ops:
  0.0 10.8 %copy-start.5 = (s32[1,1,1,3,8]{4,2,3,1,0:T(1,128)S(1)}, s32[1,1,1,3,8]{4,2,3,1,0:T(1,128)}, u32[]{:S(2)}) copy-start(s32[1,1,1,3,8]{4,2,3,1,0:T(1,128)} %param.8) | copy-start | bytes 292
  0.0 1.1 %copy-start = (bf16[1,1,1,3,8,8,8,256]{7,6,5,4,3,2,1,0:T(8,128)(2,1)S(1)}, bf16[1,1,1,3,8,8,8,256]{7,6,5,4,3,2,1,0:T(8,128)(2,1)}, u32[]{:S(2)}) copy-start(bf16[1,1,1,3,8,8,8,256]{7,6,5,4,3,2,1,0:T(8,128)(2,1)} %param.6) | copy-start | bytes 2359300
  1.1 9.6 %copy-start.3 = (bf16[27,256,16]{1,2,0:T(8,128)(2,1)S(1)}, bf16[27,256,16]{1,2,0:T(8,128)(2,1)}, u32[]{:S(2)}) copy-start(bf16[27,256,16]{1,2,0:T(8,128)(2,1)} %param.9) | copy-start | bytes 663556
  1.9 54.6 %copy-start.6 = (s32[1,1,1,3,6]{4,2,3,1,0:T(1,128)S(1)}, s32[1,1,1,3,6]{4,2,3,1,0:T(1,128)}, u32[]{:S(2)}) copy-start(s32[1,1,1,3,6]{4,2,3,1,0:T(1,128)} %param.7) | copy-start | bytes 220
  2.0 10.0 %collective-permute-start = (bf16[3,3,64,256]{3,2,1,0:T(8,128)(2,1)S(1)}, bf16[3,3,64,256]{3,2,1,0:T(8,128)(2,1)S(1)}, u32[]{:S(2)}, u32[]{:S(2)}) collective-permute-start(bf16[3,3,64,256]{3,2,1,0:T(8,128)(2,1)S(1)} %get-tuple-element.14), channel_id=1, source_target_pairs={{0,8},{8,0},{16,24},{24,16},{32,40},{40,32},{48,56},{56,48},{64,72... | collective-permute-start | bytes 884744 | tf_op jit(solution)/shard_map/ppermute | solution.py:327
  29.6 17.2 %collective-permute-start.2 = (bf16[256,2304]{1,0:T(8,128)(2,1)S(1)}, bf16[256,2304]{1,0:T(8,128)(2,1)S(1)}, u32[]{:S(2)}, u32[]{:S(2)}) collective-permute-start(bf16[256,2304]{1,0:T(8,128)(2,1)S(1)} %get-tuple-element.21), channel_id=1, source_target_pairs={{0,128},{8,392},{16,144},{24,408},{32,160},{40,424},{48,176},{56,4... | collective-permute-start | bytes 3538952 | tf_op jit(solution)/shard_map/ppermute | solution.py:350
  31.6 19.6 %collective-permute-start.3 = (bf16[256,1536]{1,0:T(8,128)(2,1)S(1)}, bf16[256,1536]{1,0:T(8,128)(2,1)S(1)}, u32[]{:S(2)}, u32[]{:S(2)}) collective-permute-start(bf16[256,1536]{1,0:T(8,128)(2,1)S(1)} %get-tuple-element.22), channel_id=1, source_target_pairs={{0,1},{1,2},{2,3},{3,4},{4,5},{5,6},{6,7},{7,0},{8,15},{9,8},{10,9... | collective-permute-start | bytes 2359304 | tf_op jit(solution)/shard_map/ppermute | solution.py:351
  46.8 12.7 %collective-permute-start.4 = (bf16[256,2304]{1,0:T(8,128)(2,1)S(1)}, bf16[256,2304]{1,0:T(8,128)(2,1)S(1)}, u32[]{:S(2)}, u32[]{:S(2)}) collective-permute-start(bf16[256,2304]{1,0:T(8,128)(2,1)S(1)} %collective-permute-done.2.x_ref.xw_ref), channel_id=1, source_target_pairs={{0,8},{8,0},{16,24},{24,16},{32,40},{40,32},{48,56},{56,48},{64,72... | collective-permute-start | bytes 3538952 | tf_op jit(solution)/shard_map/ppermute | solution.py:352
  51.2 8.3 %collective-permute-start.5 = (bf16[256,1536]{1,0:T(8,128)(2,1)S(1)}, bf16[256,1536]{1,0:T(8,128)(2,1)S(1)}, u32[]{:S(2)}, u32[]{:S(2)}) collective-permute-start(bf16[256,1536]{1,0:T(8,128)(2,1)S(1)} %collective-permute-done.3.z_ref.zw_ref), channel_id=1, source_target_pairs={{0,8},{8,0},{16,24},{24,16},{32,40},{40,32},{48,56},{56,48},{64,72... | collective-permute-start | bytes 2359304 | tf_op jit(solution)/shard_map/ppermute | solution.py:353
  53.6 5.9 %collective-permute-start.1 = (bf16[3,64,256]{2,1,0:T(8,128)(2,1)S(1)}, bf16[3,64,256]{2,1,0:T(8,128)(2,1)S(1)}, u32[]{:S(2)}, u32[]{:S(2)}) collective-permute-start(bf16[3,64,256]{2,1,0:T(8,128)(2,1)S(1)} %get-tuple-element.19), channel_id=1, source_target_pairs={{8,16},{16,8},{24,32},{32,24},{40,48},{48,40},{56,64},{64,56},{72,... | collective-permute-start | bytes 294920 | tf_op jit(solution)/shard_map/ppermute | solution.py:328
  59.5 2.6 %copy-start.1 = (bf16[1,1,1,3,8,8,8,256]{7,6,5,4,3,2,1,0:T(8,128)(2,1)S(1)}, bf16[1,1,1,3,8,8,8,256]{7,6,5,4,3,2,1,0:T(8,128)(2,1)}, u32[]{:S(2)}) copy-start(bf16[1,1,1,3,8,8,8,256]{7,6,5,4,3,2,1,0:T(8,128)(2,1)} %param.6) | copy-start | bytes 2359300
  59.5 2.7 %copy-start.4 = (f32[256]{0:T(256)S(1)}, f32[256]{0:T(256)}, u32[]{:S(2)}) copy-start(f32[256]{0:T(256)} %param.10) | copy-start | bytes 3076
  70.2 33.7 %copy-start.2 = (bf16[8,256,128]{2,1,0:T(8,128)(2,1)S(1)}, bf16[8,256,128]{2,1,0:T(8,128)(2,1)}, u32[]{:S(2)}) copy-start(bf16[8,256,128]{2,1,0:T(8,128)(2,1)} %up_ref.1) | copy-start | bytes 1572868
  70.3 33.6 %all-to-all-start = ((bf16[16,128,256]{2,1,0:T(8,128)(2,1)}), bf16[16,128,256]{2,1,0:T(8,128)(2,1)S(1)}, u32[]{:S(2)}, u32[]{:S(2)}) async-start(bf16[16,128,256]{2,1,0:T(8,128)(2,1)} %bitcast.3), calls=%async_computation | async-start | bytes 2097152 | tf_op jit(solution)/shard_map/all_to_all | solution.py:401

commit v4 on v3

--- a/solution.py
+++ b/solution.py
@@ -6,6 +6,8 @@
 from jax.sharding import PartitionSpec as P
 
 OCAP = 16
+SHARE = 7
+PART = 4
 VMEM = pltpu.VMEM
 SMEM = pltpu.SMEM
 MB = 1024 * 1024
@@ -53,15 +55,15 @@
 
 def pack_kernel(own_ref, keep_ref, met_ref, x_ref, z_ref):
     chan = keep_ref.shape[-1]
+    lanes = chan // 2
     face = keep_ref.shape[1] * keep_ref.shape[2]
-    wide = x_ref.shape[1] - 2 * chan
-    part = z_ref.shape[1] - 2 * chan
-    x_ref[:, :wide] = own_ref[:, :wide]
-    start = core_here() * ((wide - part) // chan) * chan
-    z_ref[:, :part] = own_ref[:, pl.ds(pl.multiple_of(start, chan), part)]
+    full, some = SHARE * lanes, PART * lanes
+    left = full + some
     for kind, out_ref in ((0, x_ref), (1, z_ref)):
-        left = out_ref.shape[1] - 2 * chan
+        start = (1 - kind) * full + core_here() * (full - some)
         rest = out_ref.shape[0] - face
+        out_ref[:, :full] = own_ref[:, kind * full : (kind + 1) * full]
+        out_ref[:, full:left] = own_ref[:, pl.ds(pl.multiple_of(start, lanes), some)]
         out_ref[:face, left : left + chan] = keep_ref[kind].reshape(face, chan)
         out_ref[:face, left + chan :] = met_ref[kind].reshape(face, chan)
         out_ref[face:, left:] = jnp.zeros((rest, 2 * chan), jnp.bfloat16)
@@ -69,17 +71,21 @@
 
 def quarter_kernel(owners_ref, weight_ref, out_ref):
     taps, rows, chan = weight_ref.shape
-    count = out_ref.shape[1] // chan
-    wide = out_ref.shape[1] - count * chan
-    first = colour_here() * count
-    lane = lax.broadcasted_iota(jnp.int32, (rows, wide), 1)
-    note = jnp.zeros((rows, wide), jnp.int32)
+    lanes = chan // 2
     children = owners_ref.shape[-1]
+    lane = lax.broadcasted_iota(jnp.int32, (rows, lanes), 1)
+    note = jnp.zeros((rows, lanes), jnp.int32)
     for i in range(owners_ref.shape[-2] * children):
         note = jnp.where(lane == i, owners_ref[0, 0, 0, i // children, i % children], note)
-    for j in range(count):
-        out_ref[:, j * chan : (j + 1) * chan] = weight_ref[jnp.minimum(first + j, taps - 1)]
-    out_ref[:, count * chan :] = note.astype(jnp.float32).astype(jnp.bfloat16)
+    out_ref[:, 2 * SHARE * lanes :] = note.astype(jnp.float32).astype(jnp.bfloat16)
+    for half in range(2):
+        first = half * 4 * SHARE + colours()[half] * SHARE
+        for j in range(SHARE):
+            unit = first + j
+            taken = weight_ref[jnp.minimum(lax.div(unit, 2), taps - 1)]
+            odd = lax.rem(unit, 2) == 1
+            at = (half * SHARE + j) * lanes
+            out_ref[:, at : at + lanes] = jnp.where(odd, taken[:, lanes:], taken[:, :lanes])
 
 
 def columns_kernel(
@@ -102,7 +108,7 @@
     table_ref[3 - core, far] = met_ref[2]
     table_ref[4 + core, far] = ridden(z_ref, 0)
     table_ref[5 - core, far] = ridden(zo_ref, 1)
-    out_ref[9] = jnp.zeros(out_ref.shape[1:], jnp.bfloat16)
+    out_ref[18] = jnp.zeros(out_ref.shape[1:], jnp.bfloat16)
     at_x = lax.rem(lax.broadcasted_iota(jnp.int32, (plane + 2 * edge, chan), 0), edge)
     rows_n = lax.axis_size("row")
     cols_n = lax.axis_size("col")
@@ -134,7 +140,10 @@
         for dx in range(3):
             low, high = paired(moved[dx])
             for dy in range(3):
-                out_ref[dy * 3 + dx, b, z] = octant_rows(low, high, dy).astype(jnp.bfloat16)
+                full = octant_rows(low, high, dy).astype(jnp.bfloat16)
+                unit = (dy * 3 + dx) * 2
+                out_ref[unit, b, z] = full[:, : chan // 2]
+                out_ref[unit + 1, b, z] = full[:, chan // 2 :]
 
     def brick(b, _):
         zero = jnp.zeros((edge, chan), jnp.float32)
@@ -182,85 +191,79 @@
     return jnp.concatenate(out, axis=0)
 
 
-def colour_here():
-    return lax.rem(lax.axis_index("depth") + 2 * lax.axis_index("col"), 4)
+def colours():
+    depth, col = lax.axis_index("depth"), lax.axis_index("col")
+    return lax.rem(depth + 2 * col, 4), lax.rem(col + 2 * depth, 4)
 
 
 def core_here():
     return lax.rem(lax.axis_index("row"), 2)
 
 
-def tap_rows(cols_ref, b, first, count):
-    edge, plane, chan = cols_ref.shape[2] - 2, cols_ref.shape[3], cols_ref.shape[4]
+def unit_rows(cols_ref, b, first, count):
+    edge, plane, lanes = cols_ref.shape[2] - 2, cols_ref.shape[3], cols_ref.shape[4]
     out = []
     for j in range(count):
-        tap = first + j
-        live = tap < 27
-        which = jnp.where(live, lax.rem(tap, 9), 9)
-        layer = jnp.where(live, lax.div(tap, 9), 0)
-        out.append(cols_ref[which, b, pl.ds(layer, edge)].reshape(edge * plane, chan))
+        unit = first + j
+        live = unit < 54
+        which = jnp.where(live, lax.rem(unit, 18), 18)
+        layer = jnp.where(live, lax.div(unit, 18), 0)
+        out.append(cols_ref[which, b, pl.ds(layer, edge)].reshape(edge * plane, lanes))
     return out
 
 
-def times(lhs, weight):
-    return lax.dot_general(
-        jnp.concatenate(lhs, axis=1), weight, (((1,), (1,)), ((), ())), preferred_element_type=jnp.float32
-    )
-
-
-def own_kernel(cols_ref, own_ref, lat_ref, emb_ref, acc_ref):
+def conv_kernel(
+    owners_ref, cols_ref, own_ref, x_ref, z_ref, xo_ref, zo_ref, lat_ref, emb_ref, out_ref, stash_ref, sem
+):
     slots, edge, plane, chan = lat_ref.shape
-    count = own_ref.shape[1] // chan
-    first = colour_here() * count
-    for b in range(slots):
-        got = times(tap_rows(cols_ref, b, first, count), own_ref[:, : count * chan])
-        acc_ref[b] = got + emb_ref[...]
-        for z in range(edge):
-            lat = lat_ref[b, z].astype(jnp.float32)
-            low, high = paired(lat)
-            acc_ref[b, z * plane : (z + 1) * plane] += octant_rows(low, high, 0)
-
-
-def side_kernel(cols_ref, xw_ref, zw_ref, old_ref, acc_ref):
-    chan = cols_ref.shape[4]
-    count, part = xw_ref.shape[1] // chan - 2, zw_ref.shape[1] // chan - 2
-    core, colour = core_here(), colour_here()
-    x_first = lax.rem(colour + 3 + 2 * core, 4) * count
-    z_first = lax.rem(colour + 2, 4) * count + core * (count - part)
-    for b in range(acc_ref.shape[0]):
-        got = times(tap_rows(cols_ref, b, x_first, count), xw_ref[:, : count * chan])
-        got += times(tap_rows(cols_ref, b, z_first, part), zw_ref[:, : part * chan])
-        acc_ref[b] = old_ref[b] + got
-
-
-def last_kernel(owners_ref, cols_ref, xw_ref, zw_ref, old_ref, out_ref, stash_ref, sem):
-    slots = old_ref.shape[0]
-    edge, plane, chan = cols_ref.shape[2] - 2, cols_ref.shape[3], cols_ref.shape[4]
+    lanes = cols_ref.shape[4]
     half = edge // 2
     piece = half * half
-    count, part = xw_ref.shape[1] // chan - 2, zw_ref.shape[1] // chan - 2
-    rest = count - part
-    core, colour = core_here(), colour_here()
-    x_first = lax.rem(colour + 1 + 2 * core, 4) * count
-    z_first = lax.rem(colour + 2, 4) * count + (1 - core) * part
-    lanes = pl.ds(pl.multiple_of((1 - core) * (part - rest) * chan, chan), rest * chan)
+    core = core_here()
+    full, some, rest = SHARE * lanes, PART * lanes, (SHARE - PART) * lanes
+    spans = []
+    weights = [own_ref[:, : 2 * full]]
+    for kind, colour in enumerate(colours()):
+        spans.append((kind * 4 * SHARE + colour * SHARE, SHARE))
+    late = pl.ds(pl.multiple_of(full + (1 - core) * (some - rest), lanes), rest)
+    for kind, got_ref, other_ref in ((0, x_ref, xo_ref), (1, z_ref, zo_ref)):
+        near = kind * 4 * SHARE
+        cross = (1 - kind) * 4 * SHARE + lax.rem(colours()[1 - kind] + 2, 4) * SHARE
+        colour = colours()[kind]
+        spans.append((near + lax.rem(colour + 3 + 2 * core, 4) * SHARE, SHARE))
+        spans.append((cross + core * (SHARE - PART), PART))
+        spans.append((near + lax.rem(colour + 1 + 2 * core, 4) * SHARE, SHARE))
+        spans.append((cross + (1 - core) * PART, SHARE - PART))
+        weights += [got_ref[:, : full + some], other_ref[:, :full], other_ref[:, late]]
+    weight = jnp.concatenate(weights, axis=1)
 
     targets = [owners_ref[0, 0, 0, i // 8, i % 8] for i in range(slots * 8)]
     target_rows = [lax.shift_right_arithmetic(t, 4) for t in targets]
     spare = out_ref.shape[0]
     for b in range(slots):
-        got = times(tap_rows(cols_ref, b, x_first, count), xw_ref[:, : count * chan])
-        got += times(tap_rows(cols_ref, b, z_first, rest), zw_ref[:, lanes])
-        refined = (old_ref[b] + got).astype(jnp.bfloat16)
+        rows = []
+        for first, count in spans:
+            rows += unit_rows(cols_ref, b, first, count)
+        total = lax.dot_general(
+            jnp.concatenate(rows, axis=1), weight, (((1,), (1,)), ((), ())), preferred_element_type=jnp.float32
+        )
+        total += emb_ref[...]
+        places = []
         for k in range(8):
             i = b * 8 + k
             rank = 0
             for j in range(i):
                 rank += (target_rows[j] == target_rows[i]).astype(jnp.int32)
-            place = jnp.where(targets[i] >= 0, target_rows[i] * 2 + rank, spare)
-            for z in range(half):
-                at = ((k // 4) * half + z) * plane + (k % 4) * piece
-                stash_ref[place, z * piece : (z + 1) * piece] = refined[at : at + piece]
+            places.append(jnp.where(targets[i] >= 0, target_rows[i] * 2 + rank, spare))
+        for z in range(edge):
+            low, high = paired(lat_ref[b, z].astype(jnp.float32))
+            refined = total[z * plane : (z + 1) * plane] + octant_rows(low, high, 0)
+            refined = refined.astype(jnp.bfloat16)
+            at = (z % half) * piece
+            for side in range(4):
+                stash_ref[places[z // half * 4 + side], at : at + piece] = refined[
+                    side * piece : (side + 1) * piece
+                ]
     copy = pltpu.make_async_copy(stash_ref.at[pl.ds(0, spare)], out_ref, sem)
     copy.start()
     copy.wait()
@@ -289,16 +292,12 @@
     cols_n = lax.axis_size("col")
     slots, edge, chan = latents.shape[3], latents.shape[4], latents.shape[-1]
     plane = edge * edge
-    taps = conv_weight.shape[0]
     own_out = conv_weight.shape[2]
     co = up_weight.shape[-1]
-    quarter = (taps + 1) // 4
-    part = quarter // 2 + 1
-
     smem = pl.BlockSpec(memory_space=SMEM)
     piece = pl.pallas_call(
         quarter_kernel,
-        out_shape=jax.ShapeDtypeStruct((own_out, quarter * chan + 128), jnp.bfloat16),
+        out_shape=jax.ShapeDtypeStruct((own_out, SHARE * chan + chan // 2), jnp.bfloat16),
         in_specs=[smem] + whole(1),
         out_specs=pl.BlockSpec(memory_space=VMEM),
         compiler_params=pltpu.CompilerParams(vmem_limit_bytes=4 * MB),
@@ -330,7 +329,7 @@
     own_w = lax.all_gather(piece, "row", axis=0, tiled=True)
     x_send, z_send = pl.pallas_call(
         pack_kernel,
-        out_shape=[bf16(chan, (quarter + 2) * chan), bf16(chan, (part + 2) * chan)],
+        out_shape=[bf16(chan, (SHARE + PART) * chan // 2 + 2 * chan)] * 2,
         in_specs=whole(3),
         out_specs=whole(2),
         compiler_params=pltpu.CompilerParams(vmem_limit_bytes=4 * MB),
@@ -349,12 +348,13 @@
     ]
     x_got = lax.ppermute(x_send, ("depth", "row"), x_pairs)
     z_got = lax.ppermute(z_send, ("row", "col"), z_pairs)
+    x_got, crossed = lax.optimization_barrier((x_got, crossed))
     x_other = lax.ppermute(x_got, "row", swap)
     z_other = lax.ppermute(z_got, "row", swap)
 
     columns = pl.pallas_call(
         columns_kernel,
-        out_shape=jax.ShapeDtypeStruct((10, slots, edge + 2, plane, chan), jnp.bfloat16),
+        out_shape=bf16(19, slots, edge + 2, plane, chan // 2),
         in_specs=[smem] + whole(8),
         out_specs=pl.BlockSpec(memory_space=VMEM),
         scratch_shapes=[
@@ -367,42 +367,24 @@
     )(neighbours, fi, faces, met, crossed, x_got, z_got, x_other, z_other)
 
     send_cap = 2
-    acc_shape = jax.ShapeDtypeStruct((slots, edge * plane, chan), jnp.float32)
-    params = pltpu.CompilerParams(vmem_limit_bytes=10 * MB)
-    acc = pl.pallas_call(
-        own_kernel,
-        out_shape=acc_shape,
-        in_specs=whole(4),
-        out_specs=pl.BlockSpec(memory_space=VMEM),
-        compiler_params=params,
-        cost_estimate=pl.CostEstimate(flops=1400 * MB, bytes_accessed=3 * MB, transcendentals=0),
-    )(columns, own_w, lat, step_embed.reshape(1, chan))
-    acc = pl.pallas_call(
-        side_kernel,
-        out_shape=acc_shape,
-        in_specs=whole(4),
-        out_specs=pl.BlockSpec(memory_space=VMEM),
-        compiler_params=params,
-        cost_estimate=pl.CostEstimate(flops=2200 * MB, bytes_accessed=3 * MB, transcendentals=0),
-    )(columns, x_got, z_got, acc)
     outgoing = pl.pallas_call(
-        last_kernel,
-        out_shape=jax.ShapeDtypeStruct((rows_n * send_cap, plane, chan), jnp.bfloat16),
-        in_specs=[smem] + whole(4),
+        conv_kernel,
+        out_shape=bf16(rows_n * send_cap, plane, chan),
+        in_specs=[smem] + whole(8),
         out_specs=pl.BlockSpec(memory_space=pl.ANY),
         scratch_shapes=[
             pltpu.VMEM((rows_n * send_cap + 1, plane, chan), jnp.bfloat16),
             pltpu.SemaphoreType.DMA,
         ],
-        compiler_params=params,
-        cost_estimate=pl.CostEstimate(flops=2000 * MB, bytes_accessed=3 * MB, transcendentals=0),
-    )(owners, columns, x_other, z_other, acc)
+        compiler_params=pltpu.CompilerParams(vmem_limit_bytes=26 * MB),
+        cost_estimate=pl.CostEstimate(flops=5600 * MB, bytes_accessed=8 * MB, transcendentals=0),
+    )(owners, columns, own_w, x_got, z_got, x_other, z_other, lat, step_embed.reshape(1, chan))
 
     arrived = lax.all_to_all(
         outgoing.reshape(rows_n, send_cap * plane, chan), "row", split_axis=0, concat_axis=0, tiled=True
     ).reshape(rows_n * send_cap, plane, chan)
 
-    end = quarter * chan
+    end = SHARE * chan
     notes = own_w[::own_out, end : end + slots * 8].astype(jnp.int32)
     serial = jnp.arange(slots * 8, dtype=jnp.int32)
     before = serial[None, :] < serial[:, None]

time: 108 us -> 106 us (0.981)
  starting transfers between devices: 36.6 us -> 32.5 us
  local copies, waits for them, and re-layouts: 1.22 us -> 3.49 us
    ppermute x1, waiting for transfers between devices: 4.56 us -> 0.01 us  [body(): x_got = lax.ppermute(x_send, ('depth', 'row'), x_pairs)]
    ppermute x1, waiting for transfers between devices: 0.22 us -> 2.87 us  [body(): z_got = lax.ppermute(z_send, ('row', 'col'), z_pairs)]
    unnamed x16 -> x12, local copies, waits for them, and re-layouts: 1.18 us -> 3.45 us
    ppermute x1, starting transfers between devices: 4.12 us -> 1.91 us  [body(): x_other = lax.ppermute(x_got, 'row', swap)]
    ppermute x1, waiting for transfers between devices: 0.01 us -> 1.48 us  [body(): z_other = lax.ppermute(z_got, 'row', swap)]
    ppermute x1, waiting for transfers between devices: 2.97 us -> 4.3 us  [body(): crossed = lax.ppermute(cross, 'row', between)]
    pallas_call x6 -> x4, Pallas kernels: 11.4 us -> 11.2 us  [the longest x1 7.65 us: body(): pl.pallas_call(conv_kernel, out_shape=bf16(rows_n * send_cap, plane, chan...]
  transfers between devices with their start and end apart: 7 -> 7, of which waited for: 5 -> 4; matrix products, arithmetic and copies ran while one was open for 1% -> 2% of each run, Pallas kernels for 1% -> 1%
where the time goes in v4:
time: 106 us; the launch traced here: 105 us
  waiting for transfers between devices  35.7 us (34%)
  starting transfers between devices  32.5 us (31%)
  blocking collectives  17.2 us (16%)
  Pallas kernels  15.3 us (14%)
  local copies, waits for them, and re-layouts  3.49 us (3%)
    all_to_all x1, waiting for transfers between devices, body(): lax.all_to_all(outgoing.reshape(rows_n, send_cap * plane, chan), 'row', s...  27 us
    all_gather x1, blocking collectives, body(): own_w = lax.all_gather(piece, 'row', axis=0, tiled=True)  17.2 us
    ppermute x1, starting transfers between devices, body(): z_got = lax.ppermute(z_send, ('row', 'col'), z_pairs)  10.7 us
    ppermute x1, starting transfers between devices, body(): met = lax.ppermute(give, 'row', swap)  8.8 us
    pallas_call x1, Pallas kernels, body(): pl.pallas_call(conv_kernel, out_shape=bf16(rows_n * send_cap, plane, chan...  7.65 us
    all_to_all x1, starting transfers between devices, body(): lax.all_to_all(outgoing.reshape(rows_n, send_cap * plane, chan), 'row', s...  4.7 us
    ppermute x1, waiting for transfers between devices, body(): crossed = lax.ppermute(cross, 'row', between)  4.3 us
    unnamed x12, local copies, waits for them, and re-layouts  3.45 us
  transfers between devices with their start and end apart: 7, of which 4 were waited for; matrix products, arithmetic and copies ran while one was open for 2% of the time, Pallas kernels for 1%

profile of v4, /device:TPU:1, one launch (start us, length us, event | category | flops | bytes accessed | tf_op | source)
XLA Modules:
  0.0 105.2 jit_solution(5634610699019665637)
XLA Ops:
  0.0 1.1 %copy-done.2 = bf16[1,1,1,3,8,8,8,256]{7,6,5,4,3,2,1,0:T(8,128)(2,1)S(1)} copy-done((bf16[1,1,1,3,8,8,8,256]{7,6,5,4,3,2,1,0:T(8,128)(2,1)S(1)}, bf16[1,1,1,3,8,8,8,256]{7,6,5,4,3,2,1,0:T(8,128)(2,1)}, u32[]{:S(2)}) %copy-start.2) | copy-done | bytes 786456
  1.1 0.8 shard_map.65
  1.9 0.0 copy-start.4
  1.9 8.8 %collective-permute-start = (bf16[3,3,64,256]{3,2,1,0:T(8,128)(2,1)S(1)}, bf16[3,3,64,256]{3,2,1,0:T(8,128)(2,1)S(1)}, u32[]{:S(2)}, u32[]{:S(2)}) collective-permute-start(bf16[3,3,64,256]{3,2,1,0:T(8,128)(2,1)S(1)} %get-tuple-element.16), channel_id=1, source_target_pairs={{0,8},{8,0},{16,24},{24,16},{32,40},{40,32},{48,56},{56,48},{64,72... | collective-permute-start | bytes 884744 | tf_op jit(solution)/shard_map/ppermute | solution.py:326
  10.7 0.7 copy.10.owners_ref
  11.4 0.9 copy-done.1
  12.4 0.6 shard_map.64
  13.0 0.0 collective-permute-done.met_ref
  13.0 17.2 %all_gather.3.own_ref = bf16[256,1920]{1,0:T(8,128)(2,1)S(1)} all-gather(bf16[16,1920]{1,0:T(8,128)(2,1)S(1)} %shard_map.64), channel_id=1, replica_groups=mesh['depth'=4,'row'=16,'col'=8] {'row'}, dimensions={0}, use_global_device_ids=true | all-gather | bytes 1044480 | tf_op jit(solution)/shard_map/all_gather | solution.py:329
  30.2 0.1 shard_map.66
  30.4 2.2 %collective-permute-start.1 = (bf16[256,1920]{1,0:T(8,128)(2,1)S(1)}, bf16[256,1920]{1,0:T(8,128)(2,1)S(1)}, u32[]{:S(2)}, u32[]{:S(2)}) collective-permute-start(bf16[256,1920]{1,0:T(8,128)(2,1)S(1)} %get-tuple-element.22), channel_id=1, source_target_pairs={{0,128},{8,392},{16,144},{24,408},{32,160},{40,424},{48,176},{56,4... | collective-permute-start | bytes 2949128 | tf_op jit(solution)/shard_map/ppermute | solution.py:349
  32.5 10.7 %collective-permute-start.3 = (bf16[256,1920]{1,0:T(8,128)(2,1)S(1)}, bf16[256,1920]{1,0:T(8,128)(2,1)S(1)}, u32[]{:S(2)}, u32[]{:S(2)}) collective-permute-start(bf16[256,1920]{1,0:T(8,128)(2,1)S(1)} %get-tuple-element.26), channel_id=1, source_target_pairs={{0,1},{1,2},{2,3},{3,4},{4,5},{5,6},{6,7},{7,0},{8,15},{9,8},{10,9... | collective-permute-start | bytes 2949128 | tf_op jit(solution)/shard_map/ppermute | solution.py:350
  43.2 1.9 %collective-permute-start.2 = (bf16[3,64,256]{2,1,0:T(8,128)(2,1)S(1)}, bf16[3,64,256]{2,1,0:T(8,128)(2,1)S(1)}, u32[]{:S(2)}, u32[]{:S(2)}) collective-permute-start(bf16[3,64,256]{2,1,0:T(8,128)(2,1)S(1)} %get-tuple-element.23), channel_id=1, source_target_pairs={{8,16},{16,8},{24,32},{32,24},{40,48},{48,40},{56,64},{64,56},{72,... | collective-permute-start | bytes 294920 | tf_op jit(solution)/shard_map/ppermute | solution.py:327
  45.1 4.3 %collective-permute-done.2.crossed_ref = bf16[3,64,256]{2,1,0:T(8,128)(2,1)S(1)} collective-permute-done((bf16[3,64,256]{2,1,0:T(8,128)(2,1)S(1)}, bf16[3,64,256]{2,1,0:T(8,128)(2,1)S(1)}, u32[]{:S(2)}, u32[]{:S(2)}) %collective-permute-start.2) | collective-permute-done | bytes 98336 | tf_op jit(solution)/shard_map/ppermute | solution.py:327
  49.4 0.0 collective-permute-done.1.x_ref
  49.4 1.9 %collective-permute-start.4 = (bf16[256,1920]{1,0:T(8,128)(2,1)S(1)}, bf16[256,1920]{1,0:T(8,128)(2,1)S(1)}, u32[]{:S(2)}, u32[]{:S(2)}) collective-permute-start(bf16[256,1920]{1,0:T(8,128)(2,1)S(1)} %collective-permute-done.1.x_ref), channel_id=1, source_target_pairs={{0,8},{8,0},{16,24},{24,16},{32,40},{40,32},{48,56},{56,48},{64,72... | collective-permute-start | bytes 2949128 | tf_op jit(solution)/shard_map/ppermute | solution.py:352
  51.3 2.9 %collective-permute-done.3.z_ref = bf16[256,1920]{1,0:T(8,128)(2,1)S(1)} collective-permute-done((bf16[256,1920]{1,0:T(8,128)(2,1)S(1)}, bf16[256,1920]{1,0:T(8,128)(2,1)S(1)}, u32[]{:S(2)}, u32[]{:S(2)}) %collective-permute-start.3) | collective-permute-done | bytes 983072 | tf_op jit(solution)/shard_map/ppermute | solution.py:350
  54.2 2.4 %collective-permute-start.5 = (bf16[256,1920]{1,0:T(8,128)(2,1)S(1)}, bf16[256,1920]{1,0:T(8,128)(2,1)S(1)}, u32[]{:S(2)}, u32[]{:S(2)}) collective-permute-start(bf16[256,1920]{1,0:T(8,128)(2,1)S(1)} %collective-permute-done.3.z_ref), channel_id=1, source_target_pairs={{0,8},{8,0},{16,24},{24,16},{32,40},{40,32},{48,56},{56,48},{64,72... | collective-permute-start | bytes 2949128 | tf_op jit(solution)/shard_map/ppermute | solution.py:353
  56.6 0.7 copy.11.near_ref
  57.3 0.0 collective-permute-done.4.xo_ref
  57.3 1.5 %collective-permute-done.5.zo_ref = bf16[256,1920]{1,0:T(8,128)(2,1)S(1)} collective-permute-done((bf16[256,1920]{1,0:T(8,128)(2,1)S(1)}, bf16[256,1920]{1,0:T(8,128)(2,1)S(1)}, u32[]{:S(2)}, u32[]{:S(2)}) %collective-permute-start.5) | collective-permute-done | bytes 983072 | tf_op jit(solution)/shard_map/ppermute | solution.py:353
  58.8 2.8 %shard_map.67.cols_ref = bf16[19,3,10,64,128]{4,3,2,1,0:T(8,128)(2,1)S(1)} custom-call(s32[1,1,1,3,6]{4,3,2,1,0:T(4,128)S(1)} %copy.11.near_ref, bf16[3,8,64,256]{3,2,1,0:T(8,128)(2,1)S(1)} %get-tuple-element.18.fi_ref, bf16[6,3,64,256]{3,2,1,0:T(8,128)(2,1)S(1)} %get-tuple-element.19.faces_ref, bf16[3,3,64,256]{3,2,1,0:T(8,128)(2,1)S(1)} %collective-permute-done.met_ref, ...), custom_call_target="tpu_custom_call" | custom-call | flops 16777216 | bytes 6291456 | tf_op jit(solution)/shard_map/pallas_call | solution.py:355
  61.6 0.0 copy-done.3
  61.6 0.0 copy-start
  61.6 7.7 %shard_map.68 = bf16[32,64,256]{2,1,0:T(8,128)(2,1)} custom-call(s32[1,1,1,3,8]{4,3,2,1,0:T(4,128)S(1)} %copy.10.owners_ref, bf16[19,3,10,64,128]{4,3,2,1,0:T(8,128)(2,1)S(1)} %shard_map.67.cols_ref, bf16[256,1920]{1,0:T(8,128)(2,1)S(1)} %all_gather.3.own_ref, bf16[256,1920]{1,0:T(8,128)(2,1)S(1)} %collective-permute-done.1.x_ref, ...), custom_call_target="tpu_custom_call" | custom-call | flops 5872025600 | bytes 8388608 | tf_op jit(solution)/shard_map/pallas_call | solution.py:370
  69.3 4.7 %all-to-all-start = ((bf16[16,128,256]{2,1,0:T(8,128)(2,1)}), bf16[16,128,256]{2,1,0:T(8,128)(2,1)S(1)}, u32[]{:S(2)}, u32[]{:S(2)}) async-start(bf16[16,128,256]{2,1,0:T(8,128)(2,1)} %bitcast.3), calls=%async_computation | async-start | bytes 2097152 | tf_op jit(solution)/shard_map/all_to_all | solution.py:383
  74.0 0.4 and_reduce_fusion
  74.4 0.1 convert_add_fusion
  74.5 0.4 select_reduce_fusion.source_ref
  74.9 27.0 %all-to-all-done = bf16[16,128,256]{2,1,0:T(8,128)(2,1)S(1)} async-done(((bf16[16,128,256]{2,1,0:T(8,128)(2,1)}), bf16[16,128,256]{2,1,0:T(8,128)(2,1)S(1)}, u32[]{:S(2)}, u32[]{:S(2)}) %all-to-all-start) | async-done | bytes 1048608 | tf_op jit(solution)/shard_map/all_to_all | solution.py:383
  101.9 0.0 copy-done
  101.9 3.3 %shard_map.69 = bf16[16,4,2,4,2,8,128]{6,5,4,3,2,1,0:T(8,128)(2,1)} custom-call(s32[16]{0:T(128)S(1)} %select_reduce_fusion.source_ref, bf16[32,64,256]{2,1,0:T(8,128)(2,1)S(1)} %bitcast.6, bf16[8,256,128]{2,1,0:T(8,128)(2,1)S(1)} %copy-done), custom_call_target="tpu_custom_call" | custom-call | flops 566231040 | bytes 4194304 | tf_op jit(solution)/shard_map/pallas_call | solution.py:400
  (9 shorter events, 0.1 us)
Async XLA Ops:
  0.0 1.1 %copy-start.2 = (bf16[1,1,1,3,8,8,8,256]{7,6,5,4,3,2,1,0:T(8,128)(2,1)S(1)}, bf16[1,1,1,3,8,8,8,256]{7,6,5,4,3,2,1,0:T(8,128)(2,1)}, u32[]{:S(2)}) copy-start(bf16[1,1,1,3,8,8,8,256]{7,6,5,4,3,2,1,0:T(8,128)(2,1)} %param.6) | copy-start | bytes 2359300
  1.1 60.4 %copy-start.3 = (bf16[1,1,1,3,8,8,8,256]{7,6,5,4,3,2,1,0:T(8,128)(2,1)S(1)}, bf16[1,1,1,3,8,8,8,256]{7,6,5,4,3,2,1,0:T(8,128)(2,1)}, u32[]{:S(2)}) copy-start(bf16[1,1,1,3,8,8,8,256]{7,6,5,4,3,2,1,0:T(8,128)(2,1)} %param.6) | copy-start | bytes 2359300
  1.9 59.6 %copy-start.4 = (f32[256]{0:T(256)S(1)}, f32[256]{0:T(256)}, u32[]{:S(2)}) copy-start(f32[256]{0:T(256)} %param.10) | copy-start | bytes 3076
  1.9 11.1 %collective-permute-start = (bf16[3,3,64,256]{3,2,1,0:T(8,128)(2,1)S(1)}, bf16[3,3,64,256]{3,2,1,0:T(8,128)(2,1)S(1)}, u32[]{:S(2)}, u32[]{:S(2)}) collective-permute-start(bf16[3,3,64,256]{3,2,1,0:T(8,128)(2,1)S(1)} %get-tuple-element.16), channel_id=1, source_target_pairs={{0,8},{8,0},{16,24},{24,16},{32,40},{40,32},{48,56},{56,48},{64,72... | collective-permute-start | bytes 884744 | tf_op jit(solution)/shard_map/ppermute | solution.py:326
  11.4 0.9 copy-start.1
  30.4 19.1 %collective-permute-start.1 = (bf16[256,1920]{1,0:T(8,128)(2,1)S(1)}, bf16[256,1920]{1,0:T(8,128)(2,1)S(1)}, u32[]{:S(2)}, u32[]{:S(2)}) collective-permute-start(bf16[256,1920]{1,0:T(8,128)(2,1)S(1)} %get-tuple-element.22), channel_id=1, source_target_pairs={{0,128},{8,392},{16,144},{24,408},{32,160},{40,424},{48,176},{56,4... | collective-permute-start | bytes 2949128 | tf_op jit(solution)/shard_map/ppermute | solution.py:349
  32.5 21.7 %collective-permute-start.3 = (bf16[256,1920]{1,0:T(8,128)(2,1)S(1)}, bf16[256,1920]{1,0:T(8,128)(2,1)S(1)}, u32[]{:S(2)}, u32[]{:S(2)}) collective-permute-start(bf16[256,1920]{1,0:T(8,128)(2,1)S(1)} %get-tuple-element.26), channel_id=1, source_target_pairs={{0,1},{1,2},{2,3},{3,4},{4,5},{5,6},{6,7},{7,0},{8,15},{9,8},{10,9... | collective-permute-start | bytes 2949128 | tf_op jit(solution)/shard_map/ppermute | solution.py:350
  43.2 6.2 %collective-permute-start.2 = (bf16[3,64,256]{2,1,0:T(8,128)(2,1)S(1)}, bf16[3,64,256]{2,1,0:T(8,128)(2,1)S(1)}, u32[]{:S(2)}, u32[]{:S(2)}) collective-permute-start(bf16[3,64,256]{2,1,0:T(8,128)(2,1)S(1)} %get-tuple-element.23), channel_id=1, source_target_pairs={{8,16},{16,8},{24,32},{32,24},{40,48},{48,40},{56,64},{64,56},{72,... | collective-permute-start | bytes 294920 | tf_op jit(solution)/shard_map/ppermute | solution.py:327
  49.4 7.9 %collective-permute-start.4 = (bf16[256,1920]{1,0:T(8,128)(2,1)S(1)}, bf16[256,1920]{1,0:T(8,128)(2,1)S(1)}, u32[]{:S(2)}, u32[]{:S(2)}) collective-permute-start(bf16[256,1920]{1,0:T(8,128)(2,1)S(1)} %collective-permute-done.1.x_ref), channel_id=1, source_target_pairs={{0,8},{8,0},{16,24},{24,16},{32,40},{40,32},{48,56},{56,48},{64,72... | collective-permute-start | bytes 2949128 | tf_op jit(solution)/shard_map/ppermute | solution.py:352
  54.2 4.6 %collective-permute-start.5 = (bf16[256,1920]{1,0:T(8,128)(2,1)S(1)}, bf16[256,1920]{1,0:T(8,128)(2,1)S(1)}, u32[]{:S(2)}, u32[]{:S(2)}) collective-permute-start(bf16[256,1920]{1,0:T(8,128)(2,1)S(1)} %collective-permute-done.3.z_ref), channel_id=1, source_target_pairs={{0,8},{8,0},{16,24},{24,16},{32,40},{40,32},{48,56},{56,48},{64,72... | collective-permute-start | bytes 2949128 | tf_op jit(solution)/shard_map/ppermute | solution.py:353
  61.6 40.3 %copy-start = (bf16[8,256,128]{2,1,0:T(8,128)(2,1)S(1)}, bf16[8,256,128]{2,1,0:T(8,128)(2,1)}, u32[]{:S(2)}) copy-start(bf16[8,256,128]{2,1,0:T(8,128)(2,1)} %up_ref.1) | copy-start | bytes 1572868
  69.3 32.6 %all-to-all-start = ((bf16[16,128,256]{2,1,0:T(8,128)(2,1)}), bf16[16,128,256]{2,1,0:T(8,128)(2,1)S(1)}, u32[]{:S(2)}, u32[]{:S(2)}) async-start(bf16[16,128,256]{2,1,0:T(8,128)(2,1)} %bitcast.3), calls=%async_computation | async-start | bytes 2097152 | tf_op jit(solution)/shard_map/all_to_all | solution.py:383

commit v5 on v4

--- a/solution.py
+++ b/solution.py
@@ -396,7 +396,7 @@
     source = jnp.sum(jnp.where(mine[None] & (notes[None] % OCAP == wanted), origin[None], 0), axis=(1, 2))
 
     half = edge // 2
-    each = 4
+    each = 8
     grown = pl.pallas_call(
         grow_kernel,
         grid_spec=pltpu.PrefetchScalarGridSpec(

time: 106 us -> 105 us (level)
  no operation moved by 1% of the time
where the time goes in v5:
time: 105 us
  waiting for transfers between devices  35.7 us (34%)
  starting transfers between devices  32.5 us (31%)
  blocking collectives  17.2 us (16%)
  Pallas kernels  14.7 us (14%)
  local copies, waits for them, and re-layouts  3.49 us (3%)
    all_to_all x1, waiting for transfers between devices, body(): lax.all_to_all(outgoing.reshape(rows_n, send_cap * plane, chan), 'row', s...  27 us
    all_gather x1, blocking collectives, body(): own_w = lax.all_gather(piece, 'row', axis=0, tiled=True)  17.2 us
    ppermute x1, starting transfers between devices, body(): z_got = lax.ppermute(z_send, ('row', 'col'), z_pairs)  10.7 us
    ppermute x1, starting transfers between devices, body(): met = lax.ppermute(give, 'row', swap)  8.8 us
    pallas_call x1, Pallas kernels, body(): pl.pallas_call(conv_kernel, out_shape=bf16(rows_n * send_cap, plane, chan...  7.65 us
    all_to_all x1, starting transfers between devices, body(): lax.all_to_all(outgoing.reshape(rows_n, send_cap * plane, chan), 'row', s...  4.7 us
    ppermute x1, waiting for transfers between devices, body(): crossed = lax.ppermute(cross, 'row', between)  4.3 us
    unnamed x12, local copies, waits for them, and re-layouts  3.45 us
  transfers between devices with their start and end apart: 7, of which 4 were waited for; matrix products, arithmetic and copies ran while one was open for 2% of the time, Pallas kernels for 1%

profile of v5, /device:TPU:1, one launch (start us, length us, event | category | flops | bytes accessed | tf_op | source)
XLA Modules:
  0.0 104.6 jit_solution(18123748393179174958)
XLA Ops:
  0.0 1.1 %copy-done.2 = bf16[1,1,1,3,8,8,8,256]{7,6,5,4,3,2,1,0:T(8,128)(2,1)S(1)} copy-done((bf16[1,1,1,3,8,8,8,256]{7,6,5,4,3,2,1,0:T(8,128)(2,1)S(1)}, bf16[1,1,1,3,8,8,8,256]{7,6,5,4,3,2,1,0:T(8,128)(2,1)}, u32[]{:S(2)}) %copy-start.2) | copy-done | bytes 786456
  1.1 0.8 shard_map.65
  1.9 0.0 copy-start.4
  1.9 8.8 %collective-permute-start = (bf16[3,3,64,256]{3,2,1,0:T(8,128)(2,1)S(1)}, bf16[3,3,64,256]{3,2,1,0:T(8,128)(2,1)S(1)}, u32[]{:S(2)}, u32[]{:S(2)}) collective-permute-start(bf16[3,3,64,256]{3,2,1,0:T(8,128)(2,1)S(1)} %get-tuple-element.16), channel_id=1, source_target_pairs={{0,8},{8,0},{16,24},{24,16},{32,40},{40,32},{48,56},{56,48},{64,72... | collective-permute-start | bytes 884744 | tf_op jit(solution)/shard_map/ppermute | solution.py:326
  10.7 0.7 copy.10.owners_ref
  11.4 0.9 copy-done.1
  12.4 0.6 shard_map.64
  13.0 0.0 collective-permute-done.met_ref
  13.0 17.2 %all_gather.3.own_ref = bf16[256,1920]{1,0:T(8,128)(2,1)S(1)} all-gather(bf16[16,1920]{1,0:T(8,128)(2,1)S(1)} %shard_map.64), channel_id=1, replica_groups=mesh['depth'=4,'row'=16,'col'=8] {'row'}, dimensions={0}, use_global_device_ids=true | all-gather | bytes 1044480 | tf_op jit(solution)/shard_map/all_gather | solution.py:329
  30.2 0.1 shard_map.66
  30.4 2.2 %collective-permute-start.1 = (bf16[256,1920]{1,0:T(8,128)(2,1)S(1)}, bf16[256,1920]{1,0:T(8,128)(2,1)S(1)}, u32[]{:S(2)}, u32[]{:S(2)}) collective-permute-start(bf16[256,1920]{1,0:T(8,128)(2,1)S(1)} %get-tuple-element.22), channel_id=1, source_target_pairs={{0,128},{8,392},{16,144},{24,408},{32,160},{40,424},{48,176},{56,4... | collective-permute-start | bytes 2949128 | tf_op jit(solution)/shard_map/ppermute | solution.py:349
  32.5 10.7 %collective-permute-start.3 = (bf16[256,1920]{1,0:T(8,128)(2,1)S(1)}, bf16[256,1920]{1,0:T(8,128)(2,1)S(1)}, u32[]{:S(2)}, u32[]{:S(2)}) collective-permute-start(bf16[256,1920]{1,0:T(8,128)(2,1)S(1)} %get-tuple-element.26), channel_id=1, source_target_pairs={{0,1},{1,2},{2,3},{3,4},{4,5},{5,6},{6,7},{7,0},{8,15},{9,8},{10,9... | collective-permute-start | bytes 2949128 | tf_op jit(solution)/shard_map/ppermute | solution.py:350
  43.2 1.9 %collective-permute-start.2 = (bf16[3,64,256]{2,1,0:T(8,128)(2,1)S(1)}, bf16[3,64,256]{2,1,0:T(8,128)(2,1)S(1)}, u32[]{:S(2)}, u32[]{:S(2)}) collective-permute-start(bf16[3,64,256]{2,1,0:T(8,128)(2,1)S(1)} %get-tuple-element.23), channel_id=1, source_target_pairs={{8,16},{16,8},{24,32},{32,24},{40,48},{48,40},{56,64},{64,56},{72,... | collective-permute-start | bytes 294920 | tf_op jit(solution)/shard_map/ppermute | solution.py:327
  45.1 4.3 %collective-permute-done.2.crossed_ref = bf16[3,64,256]{2,1,0:T(8,128)(2,1)S(1)} collective-permute-done((bf16[3,64,256]{2,1,0:T(8,128)(2,1)S(1)}, bf16[3,64,256]{2,1,0:T(8,128)(2,1)S(1)}, u32[]{:S(2)}, u32[]{:S(2)}) %collective-permute-start.2) | collective-permute-done | bytes 98336 | tf_op jit(solution)/shard_map/ppermute | solution.py:327
  49.4 0.0 collective-permute-done.1.x_ref
  49.4 1.9 %collective-permute-start.4 = (bf16[256,1920]{1,0:T(8,128)(2,1)S(1)}, bf16[256,1920]{1,0:T(8,128)(2,1)S(1)}, u32[]{:S(2)}, u32[]{:S(2)}) collective-permute-start(bf16[256,1920]{1,0:T(8,128)(2,1)S(1)} %collective-permute-done.1.x_ref), channel_id=1, source_target_pairs={{0,8},{8,0},{16,24},{24,16},{32,40},{40,32},{48,56},{56,48},{64,72... | collective-permute-start | bytes 2949128 | tf_op jit(solution)/shard_map/ppermute | solution.py:352
  51.3 2.9 %collective-permute-done.3.z_ref = bf16[256,1920]{1,0:T(8,128)(2,1)S(1)} collective-permute-done((bf16[256,1920]{1,0:T(8,128)(2,1)S(1)}, bf16[256,1920]{1,0:T(8,128)(2,1)S(1)}, u32[]{:S(2)}, u32[]{:S(2)}) %collective-permute-start.3) | collective-permute-done | bytes 983072 | tf_op jit(solution)/shard_map/ppermute | solution.py:350
  54.2 2.4 %collective-permute-start.5 = (bf16[256,1920]{1,0:T(8,128)(2,1)S(1)}, bf16[256,1920]{1,0:T(8,128)(2,1)S(1)}, u32[]{:S(2)}, u32[]{:S(2)}) collective-permute-start(bf16[256,1920]{1,0:T(8,128)(2,1)S(1)} %collective-permute-done.3.z_ref), channel_id=1, source_target_pairs={{0,8},{8,0},{16,24},{24,16},{32,40},{40,32},{48,56},{56,48},{64,72... | collective-permute-start | bytes 2949128 | tf_op jit(solution)/shard_map/ppermute | solution.py:353
  56.6 0.7 copy.11.near_ref
  57.3 0.0 collective-permute-done.4.xo_ref
  57.3 1.5 %collective-permute-done.5.zo_ref = bf16[256,1920]{1,0:T(8,128)(2,1)S(1)} collective-permute-done((bf16[256,1920]{1,0:T(8,128)(2,1)S(1)}, bf16[256,1920]{1,0:T(8,128)(2,1)S(1)}, u32[]{:S(2)}, u32[]{:S(2)}) %collective-permute-start.5) | collective-permute-done | bytes 983072 | tf_op jit(solution)/shard_map/ppermute | solution.py:353
  58.8 2.8 %shard_map.67.cols_ref = bf16[19,3,10,64,128]{4,3,2,1,0:T(8,128)(2,1)S(1)} custom-call(s32[1,1,1,3,6]{4,3,2,1,0:T(4,128)S(1)} %copy.11.near_ref, bf16[3,8,64,256]{3,2,1,0:T(8,128)(2,1)S(1)} %get-tuple-element.18.fi_ref, bf16[6,3,64,256]{3,2,1,0:T(8,128)(2,1)S(1)} %get-tuple-element.19.faces_ref, bf16[3,3,64,256]{3,2,1,0:T(8,128)(2,1)S(1)} %collective-permute-done.met_ref, ...), custom_call_target="tpu_custom_call" | custom-call | flops 16777216 | bytes 6291456 | tf_op jit(solution)/shard_map/pallas_call | solution.py:355
  61.6 0.0 copy-done.3
  61.6 0.0 copy-done.4
  61.6 0.0 copy-start
  61.6 7.7 %shard_map.68 = bf16[32,64,256]{2,1,0:T(8,128)(2,1)} custom-call(s32[1,1,1,3,8]{4,3,2,1,0:T(4,128)S(1)} %copy.10.owners_ref, bf16[19,3,10,64,128]{4,3,2,1,0:T(8,128)(2,1)S(1)} %shard_map.67.cols_ref, bf16[256,1920]{1,0:T(8,128)(2,1)S(1)} %all_gather.3.own_ref, bf16[256,1920]{1,0:T(8,128)(2,1)S(1)} %collective-permute-done.1.x_ref, ...), custom_call_target="tpu_custom_call" | custom-call | flops 5872025600 | bytes 8388608 | tf_op jit(solution)/shard_map/pallas_call | solution.py:370
  69.3 4.7 %all-to-all-start = ((bf16[16,128,256]{2,1,0:T(8,128)(2,1)}), bf16[16,128,256]{2,1,0:T(8,128)(2,1)S(1)}, u32[]{:S(2)}, u32[]{:S(2)}) async-start(bf16[16,128,256]{2,1,0:T(8,128)(2,1)} %bitcast.3), calls=%async_computation | async-start | bytes 2097152 | tf_op jit(solution)/shard_map/all_to_all | solution.py:383
  74.0 0.4 and_reduce_fusion
  74.4 0.1 convert_add_fusion
  74.5 0.4 select_reduce_fusion.source_ref
  74.9 27.0 %all-to-all-done = bf16[16,128,256]{2,1,0:T(8,128)(2,1)S(1)} async-done(((bf16[16,128,256]{2,1,0:T(8,128)(2,1)}), bf16[16,128,256]{2,1,0:T(8,128)(2,1)S(1)}, u32[]{:S(2)}, u32[]{:S(2)}) %all-to-all-start) | async-done | bytes 1048608 | tf_op jit(solution)/shard_map/all_to_all | solution.py:383
  101.9 2.7 %shard_map.69 = bf16[16,4,2,4,2,8,128]{6,5,4,3,2,1,0:T(8,128)(2,1)} custom-call(s32[16]{0:T(128)S(1)} %select_reduce_fusion.source_ref, bf16[32,64,256]{2,1,0:T(8,128)(2,1)S(1)} %bitcast.6, bf16[8,256,128]{2,1,0:T(8,128)(2,1)S(1)} %copy-done), custom_call_target="tpu_custom_call" | custom-call | flops 566231040 | bytes 4194304 | tf_op jit(solution)/shard_map/pallas_call | solution.py:400
  (9 shorter events, 0.1 us)
Async XLA Ops:
  0.0 1.1 %copy-start.2 = (bf16[1,1,1,3,8,8,8,256]{7,6,5,4,3,2,1,0:T(8,128)(2,1)S(1)}, bf16[1,1,1,3,8,8,8,256]{7,6,5,4,3,2,1,0:T(8,128)(2,1)}, u32[]{:S(2)}) copy-start(bf16[1,1,1,3,8,8,8,256]{7,6,5,4,3,2,1,0:T(8,128)(2,1)} %param.6) | copy-start | bytes 2359300
  1.1 60.4 %copy-start.3 = (bf16[1,1,1,3,8,8,8,256]{7,6,5,4,3,2,1,0:T(8,128)(2,1)S(1)}, bf16[1,1,1,3,8,8,8,256]{7,6,5,4,3,2,1,0:T(8,128)(2,1)}, u32[]{:S(2)}) copy-start(bf16[1,1,1,3,8,8,8,256]{7,6,5,4,3,2,1,0:T(8,128)(2,1)} %param.6) | copy-start | bytes 2359300
  1.9 59.6 %copy-start.4 = (f32[256]{0:T(256)S(1)}, f32[256]{0:T(256)}, u32[]{:S(2)}) copy-start(f32[256]{0:T(256)} %param.10) | copy-start | bytes 3076
  1.9 11.1 %collective-permute-start = (bf16[3,3,64,256]{3,2,1,0:T(8,128)(2,1)S(1)}, bf16[3,3,64,256]{3,2,1,0:T(8,128)(2,1)S(1)}, u32[]{:S(2)}, u32[]{:S(2)}) collective-permute-start(bf16[3,3,64,256]{3,2,1,0:T(8,128)(2,1)S(1)} %get-tuple-element.16), channel_id=1, source_target_pairs={{0,8},{8,0},{16,24},{24,16},{32,40},{40,32},{48,56},{56,48},{64,72... | collective-permute-start | bytes 884744 | tf_op jit(solution)/shard_map/ppermute | solution.py:326
  11.4 0.9 copy-start.1
  30.4 19.1 %collective-permute-start.1 = (bf16[256,1920]{1,0:T(8,128)(2,1)S(1)}, bf16[256,1920]{1,0:T(8,128)(2,1)S(1)}, u32[]{:S(2)}, u32[]{:S(2)}) collective-permute-start(bf16[256,1920]{1,0:T(8,128)(2,1)S(1)} %get-tuple-element.22), channel_id=1, source_target_pairs={{0,128},{8,392},{16,144},{24,408},{32,160},{40,424},{48,176},{56,4... | collective-permute-start | bytes 2949128 | tf_op jit(solution)/shard_map/ppermute | solution.py:349
  32.5 21.7 %collective-permute-start.3 = (bf16[256,1920]{1,0:T(8,128)(2,1)S(1)}, bf16[256,1920]{1,0:T(8,128)(2,1)S(1)}, u32[]{:S(2)}, u32[]{:S(2)}) collective-permute-start(bf16[256,1920]{1,0:T(8,128)(2,1)S(1)} %get-tuple-element.26), channel_id=1, source_target_pairs={{0,1},{1,2},{2,3},{3,4},{4,5},{5,6},{6,7},{7,0},{8,15},{9,8},{10,9... | collective-permute-start | bytes 2949128 | tf_op jit(solution)/shard_map/ppermute | solution.py:350
  43.2 6.2 %collective-permute-start.2 = (bf16[3,64,256]{2,1,0:T(8,128)(2,1)S(1)}, bf16[3,64,256]{2,1,0:T(8,128)(2,1)S(1)}, u32[]{:S(2)}, u32[]{:S(2)}) collective-permute-start(bf16[3,64,256]{2,1,0:T(8,128)(2,1)S(1)} %get-tuple-element.23), channel_id=1, source_target_pairs={{8,16},{16,8},{24,32},{32,24},{40,48},{48,40},{56,64},{64,56},{72,... | collective-permute-start | bytes 294920 | tf_op jit(solution)/shard_map/ppermute | solution.py:327
  49.4 7.9 %collective-permute-start.4 = (bf16[256,1920]{1,0:T(8,128)(2,1)S(1)}, bf16[256,1920]{1,0:T(8,128)(2,1)S(1)}, u32[]{:S(2)}, u32[]{:S(2)}) collective-permute-start(bf16[256,1920]{1,0:T(8,128)(2,1)S(1)} %collective-permute-done.1.x_ref), channel_id=1, source_target_pairs={{0,8},{8,0},{16,24},{24,16},{32,40},{40,32},{48,56},{56,48},{64,72... | collective-permute-start | bytes 2949128 | tf_op jit(solution)/shard_map/ppermute | solution.py:352
  54.2 4.6 %collective-permute-start.5 = (bf16[256,1920]{1,0:T(8,128)(2,1)S(1)}, bf16[256,1920]{1,0:T(8,128)(2,1)S(1)}, u32[]{:S(2)}, u32[]{:S(2)}) collective-permute-start(bf16[256,1920]{1,0:T(8,128)(2,1)S(1)} %collective-permute-done.3.z_ref), channel_id=1, source_target_pairs={{0,8},{8,0},{16,24},{24,16},{32,40},{40,32},{48,56},{56,48},{64,72... | collective-permute-start | bytes 2949128 | tf_op jit(solution)/shard_map/ppermute | solution.py:353
  61.6 40.3 %copy-start = (bf16[8,256,128]{2,1,0:T(8,128)(2,1)S(1)}, bf16[8,256,128]{2,1,0:T(8,128)(2,1)}, u32[]{:S(2)}) copy-start(bf16[8,256,128]{2,1,0:T(8,128)(2,1)} %up_ref.1) | copy-start | bytes 1572868
  69.3 32.6 %all-to-all-start = ((bf16[16,128,256]{2,1,0:T(8,128)(2,1)}), bf16[16,128,256]{2,1,0:T(8,128)(2,1)S(1)}, u32[]{:S(2)}, u32[]{:S(2)}) async-start(bf16[16,128,256]{2,1,0:T(8,128)(2,1)} %bitcast.3), calls=%async_computation | async-start | bytes 2097152 | tf_op jit(solution)/shard_map/all_to_all | solution.py:383

commit v6 on v5

--- a/solution.py
+++ b/solution.py
@@ -325,7 +325,7 @@
     between = [(r, r + 1 - 2 * (1 - r % 2)) for r in range(1, rows_n - 1)]
     met = lax.ppermute(give, "row", swap)
     crossed = lax.ppermute(cross, "row", between)
-    piece, met = lax.optimization_barrier((piece, met))
+    piece, give = lax.optimization_barrier((piece, give))
     own_w = lax.all_gather(piece, "row", axis=0, tiled=True)
     x_send, z_send = pl.pallas_call(
         pack_kernel,

time: 105 us -> 105 us (level)
  no operation moved by 1% of the time
where the time goes in v6:
time: 105 us
  waiting for transfers between devices  35.7 us (34%)
  starting transfers between devices  32.5 us (31%)
  blocking collectives  17.2 us (16%)
  Pallas kernels  14.7 us (14%)
  local copies, waits for them, and re-layouts  3.49 us (3%)
    all_to_all x1, waiting for transfers between devices, body(): lax.all_to_all(outgoing.reshape(rows_n, send_cap * plane, chan), 'row', s...  27 us
    all_gather x1, blocking collectives, body(): own_w = lax.all_gather(piece, 'row', axis=0, tiled=True)  17.2 us
    ppermute x1, starting transfers between devices, body(): z_got = lax.ppermute(z_send, ('row', 'col'), z_pairs)  10.7 us
    ppermute x1, starting transfers between devices, body(): met = lax.ppermute(give, 'row', swap)  8.8 us
    pallas_call x1, Pallas kernels, body(): pl.pallas_call(conv_kernel, out_shape=bf16(rows_n * send_cap, plane, chan...  7.65 us
    all_to_all x1, starting transfers between devices, body(): lax.all_to_all(outgoing.reshape(rows_n, send_cap * plane, chan), 'row', s...  4.71 us
    ppermute x1, waiting for transfers between devices, body(): crossed = lax.ppermute(cross, 'row', between)  4.3 us
    unnamed x12, local copies, waits for them, and re-layouts  3.45 us
  transfers between devices with their start and end apart: 7, of which 4 were waited for; matrix products, arithmetic and copies ran while one was open for 2% of the time, Pallas kernels for 1%

profile of v6, /device:TPU:1, one launch (start us, length us, event | category | flops | bytes accessed | tf_op | source)
XLA Modules:
  0.0 104.6 jit_solution(12826369686594238842)
XLA Ops:
  0.0 1.1 %copy-done.2 = bf16[1,1,1,3,8,8,8,256]{7,6,5,4,3,2,1,0:T(8,128)(2,1)S(1)} copy-done((bf16[1,1,1,3,8,8,8,256]{7,6,5,4,3,2,1,0:T(8,128)(2,1)S(1)}, bf16[1,1,1,3,8,8,8,256]{7,6,5,4,3,2,1,0:T(8,128)(2,1)}, u32[]{:S(2)}) %copy-start.2) | copy-done | bytes 786456
  1.1 0.8 shard_map.65
  1.9 0.0 copy-start.4
  1.9 8.8 %collective-permute-start = (bf16[3,3,64,256]{3,2,1,0:T(8,128)(2,1)S(1)}, bf16[3,3,64,256]{3,2,1,0:T(8,128)(2,1)S(1)}, u32[]{:S(2)}, u32[]{:S(2)}) collective-permute-start(bf16[3,3,64,256]{3,2,1,0:T(8,128)(2,1)S(1)} %get-tuple-element.15), channel_id=1, source_target_pairs={{0,8},{8,0},{16,24},{24,16},{32,40},{40,32},{48,56},{56,48},{64,72... | collective-permute-start | bytes 884744 | tf_op jit(solution)/shard_map/ppermute | solution.py:326
  10.7 0.7 copy.10.owners_ref
  11.4 0.9 copy-done.1
  12.4 0.6 shard_map.64
  13.0 17.2 %all_gather.3.own_ref = bf16[256,1920]{1,0:T(8,128)(2,1)S(1)} all-gather(bf16[16,1920]{1,0:T(8,128)(2,1)S(1)} %shard_map.64), channel_id=1, replica_groups=mesh['depth'=4,'row'=16,'col'=8] {'row'}, dimensions={0}, use_global_device_ids=true | all-gather | bytes 1044480 | tf_op jit(solution)/shard_map/all_gather | solution.py:329
  30.2 0.0 collective-permute-done.met_ref
  30.2 0.1 shard_map.66
  30.3 2.2 %collective-permute-start.1 = (bf16[256,1920]{1,0:T(8,128)(2,1)S(1)}, bf16[256,1920]{1,0:T(8,128)(2,1)S(1)}, u32[]{:S(2)}, u32[]{:S(2)}) collective-permute-start(bf16[256,1920]{1,0:T(8,128)(2,1)S(1)} %get-tuple-element.20), channel_id=1, source_target_pairs={{0,128},{8,392},{16,144},{24,408},{32,160},{40,424},{48,176},{56,4... | collective-permute-start | bytes 2949128 | tf_op jit(solution)/shard_map/ppermute | solution.py:349
  32.5 10.7 %collective-permute-start.3 = (bf16[256,1920]{1,0:T(8,128)(2,1)S(1)}, bf16[256,1920]{1,0:T(8,128)(2,1)S(1)}, u32[]{:S(2)}, u32[]{:S(2)}) collective-permute-start(bf16[256,1920]{1,0:T(8,128)(2,1)S(1)} %get-tuple-element.24), channel_id=1, source_target_pairs={{0,1},{1,2},{2,3},{3,4},{4,5},{5,6},{6,7},{7,0},{8,15},{9,8},{10,9... | collective-permute-start | bytes 2949128 | tf_op jit(solution)/shard_map/ppermute | solution.py:350
  43.2 1.9 %collective-permute-start.2 = (bf16[3,64,256]{2,1,0:T(8,128)(2,1)S(1)}, bf16[3,64,256]{2,1,0:T(8,128)(2,1)S(1)}, u32[]{:S(2)}, u32[]{:S(2)}) collective-permute-start(bf16[3,64,256]{2,1,0:T(8,128)(2,1)S(1)} %get-tuple-element.21), channel_id=1, source_target_pairs={{8,16},{16,8},{24,32},{32,24},{40,48},{48,40},{56,64},{64,56},{72,... | collective-permute-start | bytes 294920 | tf_op jit(solution)/shard_map/ppermute | solution.py:327
  45.1 4.3 %collective-permute-done.2.crossed_ref = bf16[3,64,256]{2,1,0:T(8,128)(2,1)S(1)} collective-permute-done((bf16[3,64,256]{2,1,0:T(8,128)(2,1)S(1)}, bf16[3,64,256]{2,1,0:T(8,128)(2,1)S(1)}, u32[]{:S(2)}, u32[]{:S(2)}) %collective-permute-start.2) | collective-permute-done | bytes 98336 | tf_op jit(solution)/shard_map/ppermute | solution.py:327
  49.4 0.0 collective-permute-done.1.x_ref
  49.4 1.9 %collective-permute-start.4 = (bf16[256,1920]{1,0:T(8,128)(2,1)S(1)}, bf16[256,1920]{1,0:T(8,128)(2,1)S(1)}, u32[]{:S(2)}, u32[]{:S(2)}) collective-permute-start(bf16[256,1920]{1,0:T(8,128)(2,1)S(1)} %collective-permute-done.1.x_ref), channel_id=1, source_target_pairs={{0,8},{8,0},{16,24},{24,16},{32,40},{40,32},{48,56},{56,48},{64,72... | collective-permute-start | bytes 2949128 | tf_op jit(solution)/shard_map/ppermute | solution.py:352
  51.3 2.9 %collective-permute-done.3.z_ref = bf16[256,1920]{1,0:T(8,128)(2,1)S(1)} collective-permute-done((bf16[256,1920]{1,0:T(8,128)(2,1)S(1)}, bf16[256,1920]{1,0:T(8,128)(2,1)S(1)}, u32[]{:S(2)}, u32[]{:S(2)}) %collective-permute-start.3) | collective-permute-done | bytes 983072 | tf_op jit(solution)/shard_map/ppermute | solution.py:350
  54.2 2.4 %collective-permute-start.5 = (bf16[256,1920]{1,0:T(8,128)(2,1)S(1)}, bf16[256,1920]{1,0:T(8,128)(2,1)S(1)}, u32[]{:S(2)}, u32[]{:S(2)}) collective-permute-start(bf16[256,1920]{1,0:T(8,128)(2,1)S(1)} %collective-permute-done.3.z_ref), channel_id=1, source_target_pairs={{0,8},{8,0},{16,24},{24,16},{32,40},{40,32},{48,56},{56,48},{64,72... | collective-permute-start | bytes 2949128 | tf_op jit(solution)/shard_map/ppermute | solution.py:353
  56.6 0.7 copy.11.near_ref
  57.3 0.0 collective-permute-done.4.xo_ref
  57.3 1.5 %collective-permute-done.5.zo_ref = bf16[256,1920]{1,0:T(8,128)(2,1)S(1)} collective-permute-done((bf16[256,1920]{1,0:T(8,128)(2,1)S(1)}, bf16[256,1920]{1,0:T(8,128)(2,1)S(1)}, u32[]{:S(2)}, u32[]{:S(2)}) %collective-permute-start.5) | collective-permute-done | bytes 983072 | tf_op jit(solution)/shard_map/ppermute | solution.py:353
  58.8 2.8 %shard_map.67.cols_ref = bf16[19,3,10,64,128]{4,3,2,1,0:T(8,128)(2,1)S(1)} custom-call(s32[1,1,1,3,6]{4,3,2,1,0:T(4,128)S(1)} %copy.11.near_ref, bf16[3,8,64,256]{3,2,1,0:T(8,128)(2,1)S(1)} %get-tuple-element.17.fi_ref, bf16[6,3,64,256]{3,2,1,0:T(8,128)(2,1)S(1)} %get-tuple-element.18.faces_ref, bf16[3,3,64,256]{3,2,1,0:T(8,128)(2,1)S(1)} %collective-permute-done.met_ref, ...), custom_call_target="tpu_custom_call" | custom-call | flops 16777216 | bytes 6291456 | tf_op jit(solution)/shard_map/pallas_call | solution.py:355
  61.6 0.0 copy-done.3
  61.6 0.0 copy-done.4
  61.6 0.0 copy-start
  61.6 7.7 %shard_map.68 = bf16[32,64,256]{2,1,0:T(8,128)(2,1)} custom-call(s32[1,1,1,3,8]{4,3,2,1,0:T(4,128)S(1)} %copy.10.owners_ref, bf16[19,3,10,64,128]{4,3,2,1,0:T(8,128)(2,1)S(1)} %shard_map.67.cols_ref, bf16[256,1920]{1,0:T(8,128)(2,1)S(1)} %all_gather.3.own_ref, bf16[256,1920]{1,0:T(8,128)(2,1)S(1)} %collective-permute-done.1.x_ref, ...), custom_call_target="tpu_custom_call" | custom-call | flops 5872025600 | bytes 8388608 | tf_op jit(solution)/shard_map/pallas_call | solution.py:370
  69.2 4.7 %all-to-all-start = ((bf16[16,128,256]{2,1,0:T(8,128)(2,1)}), bf16[16,128,256]{2,1,0:T(8,128)(2,1)S(1)}, u32[]{:S(2)}, u32[]{:S(2)}) async-start(bf16[16,128,256]{2,1,0:T(8,128)(2,1)} %bitcast.3), calls=%async_computation | async-start | bytes 2097152 | tf_op jit(solution)/shard_map/all_to_all | solution.py:383
  74.0 0.4 and_reduce_fusion
  74.4 0.1 convert_add_fusion
  74.5 0.4 select_reduce_fusion.source_ref
  74.9 27.0 %all-to-all-done = bf16[16,128,256]{2,1,0:T(8,128)(2,1)S(1)} async-done(((bf16[16,128,256]{2,1,0:T(8,128)(2,1)}), bf16[16,128,256]{2,1,0:T(8,128)(2,1)S(1)}, u32[]{:S(2)}, u32[]{:S(2)}) %all-to-all-start) | async-done | bytes 1048608 | tf_op jit(solution)/shard_map/all_to_all | solution.py:383
  101.9 2.7 %shard_map.69 = bf16[16,4,2,4,2,8,128]{6,5,4,3,2,1,0:T(8,128)(2,1)} custom-call(s32[16]{0:T(128)S(1)} %select_reduce_fusion.source_ref, bf16[32,64,256]{2,1,0:T(8,128)(2,1)S(1)} %bitcast.6, bf16[8,256,128]{2,1,0:T(8,128)(2,1)S(1)} %copy-done), custom_call_target="tpu_custom_call" | custom-call | flops 566231040 | bytes 4194304 | tf_op jit(solution)/shard_map/pallas_call | solution.py:400
  (9 shorter events, 0.1 us)
Async XLA Ops:
  0.0 1.1 %copy-start.2 = (bf16[1,1,1,3,8,8,8,256]{7,6,5,4,3,2,1,0:T(8,128)(2,1)S(1)}, bf16[1,1,1,3,8,8,8,256]{7,6,5,4,3,2,1,0:T(8,128)(2,1)}, u32[]{:S(2)}) copy-start(bf16[1,1,1,3,8,8,8,256]{7,6,5,4,3,2,1,0:T(8,128)(2,1)} %param.6) | copy-start | bytes 2359300
  1.1 60.4 %copy-start.3 = (bf16[1,1,1,3,8,8,8,256]{7,6,5,4,3,2,1,0:T(8,128)(2,1)S(1)}, bf16[1,1,1,3,8,8,8,256]{7,6,5,4,3,2,1,0:T(8,128)(2,1)}, u32[]{:S(2)}) copy-start(bf16[1,1,1,3,8,8,8,256]{7,6,5,4,3,2,1,0:T(8,128)(2,1)} %param.6) | copy-start | bytes 2359300
  1.9 59.6 %copy-start.4 = (f32[256]{0:T(256)S(1)}, f32[256]{0:T(256)}, u32[]{:S(2)}) copy-start(f32[256]{0:T(256)} %param.10) | copy-start | bytes 3076
  1.9 28.3 %collective-permute-start = (bf16[3,3,64,256]{3,2,1,0:T(8,128)(2,1)S(1)}, bf16[3,3,64,256]{3,2,1,0:T(8,128)(2,1)S(1)}, u32[]{:S(2)}, u32[]{:S(2)}) collective-permute-start(bf16[3,3,64,256]{3,2,1,0:T(8,128)(2,1)S(1)} %get-tuple-element.15), channel_id=1, source_target_pairs={{0,8},{8,0},{16,24},{24,16},{32,40},{40,32},{48,56},{56,48},{64,72... | collective-permute-start | bytes 884744 | tf_op jit(solution)/shard_map/ppermute | solution.py:326
  11.4 0.9 copy-start.1
  30.3 19.1 %collective-permute-start.1 = (bf16[256,1920]{1,0:T(8,128)(2,1)S(1)}, bf16[256,1920]{1,0:T(8,128)(2,1)S(1)}, u32[]{:S(2)}, u32[]{:S(2)}) collective-permute-start(bf16[256,1920]{1,0:T(8,128)(2,1)S(1)} %get-tuple-element.20), channel_id=1, source_target_pairs={{0,128},{8,392},{16,144},{24,408},{32,160},{40,424},{48,176},{56,4... | collective-permute-start | bytes 2949128 | tf_op jit(solution)/shard_map/ppermute | solution.py:349
  32.5 21.7 %collective-permute-start.3 = (bf16[256,1920]{1,0:T(8,128)(2,1)S(1)}, bf16[256,1920]{1,0:T(8,128)(2,1)S(1)}, u32[]{:S(2)}, u32[]{:S(2)}) collective-permute-start(bf16[256,1920]{1,0:T(8,128)(2,1)S(1)} %get-tuple-element.24), channel_id=1, source_target_pairs={{0,1},{1,2},{2,3},{3,4},{4,5},{5,6},{6,7},{7,0},{8,15},{9,8},{10,9... | collective-permute-start | bytes 2949128 | tf_op jit(solution)/shard_map/ppermute | solution.py:350
  43.2 6.2 %collective-permute-start.2 = (bf16[3,64,256]{2,1,0:T(8,128)(2,1)S(1)}, bf16[3,64,256]{2,1,0:T(8,128)(2,1)S(1)}, u32[]{:S(2)}, u32[]{:S(2)}) collective-permute-start(bf16[3,64,256]{2,1,0:T(8,128)(2,1)S(1)} %get-tuple-element.21), channel_id=1, source_target_pairs={{8,16},{16,8},{24,32},{32,24},{40,48},{48,40},{56,64},{64,56},{72,... | collective-permute-start | bytes 294920 | tf_op jit(solution)/shard_map/ppermute | solution.py:327
  49.4 7.9 %collective-permute-start.4 = (bf16[256,1920]{1,0:T(8,128)(2,1)S(1)}, bf16[256,1920]{1,0:T(8,128)(2,1)S(1)}, u32[]{:S(2)}, u32[]{:S(2)}) collective-permute-start(bf16[256,1920]{1,0:T(8,128)(2,1)S(1)} %collective-permute-done.1.x_ref), channel_id=1, source_target_pairs={{0,8},{8,0},{16,24},{24,16},{32,40},{40,32},{48,56},{56,48},{64,72... | collective-permute-start | bytes 2949128 | tf_op jit(solution)/shard_map/ppermute | solution.py:352
  54.2 4.6 %collective-permute-start.5 = (bf16[256,1920]{1,0:T(8,128)(2,1)S(1)}, bf16[256,1920]{1,0:T(8,128)(2,1)S(1)}, u32[]{:S(2)}, u32[]{:S(2)}) collective-permute-start(bf16[256,1920]{1,0:T(8,128)(2,1)S(1)} %collective-permute-done.3.z_ref), channel_id=1, source_target_pairs={{0,8},{8,0},{16,24},{24,16},{32,40},{40,32},{48,56},{56,48},{64,72... | collective-permute-start | bytes 2949128 | tf_op jit(solution)/shard_map/ppermute | solution.py:353
  61.6 40.3 %copy-start = (bf16[8,256,128]{2,1,0:T(8,128)(2,1)S(1)}, bf16[8,256,128]{2,1,0:T(8,128)(2,1)}, u32[]{:S(2)}) copy-start(bf16[8,256,128]{2,1,0:T(8,128)(2,1)} %up_ref.1) | copy-start | bytes 1572868
  69.2 32.6 %all-to-all-start = ((bf16[16,128,256]{2,1,0:T(8,128)(2,1)}), bf16[16,128,256]{2,1,0:T(8,128)(2,1)S(1)}, u32[]{:S(2)}, u32[]{:S(2)}) async-start(bf16[16,128,256]{2,1,0:T(8,128)(2,1)} %bitcast.3), calls=%async_computation | async-start | bytes 2097152 | tf_op jit(solution)/shard_map/all_to_all | solution.py:383
